TPU v7x, 32 devices: a whole 2x2x4 slice. The times are simulated.
32 devices in a mesh: seq: 8 (over z, core), tp: 4 (over y, x).
Axes of the slice: x: 2, y: 2, z: 4, core: 2. Of those that a mesh axis runs over, the one named last changes fastest.
Arguments:
- block_input: bfloat16 [8192, 2048], P('seq'), may hold values from -6 to 6
- norm_one: float32 [2048], replicated, may hold values from 0.1 to 1.9
- w_query: bfloat16 [2048, 2048], P(None, 'tp'), may hold values from -0.1875 to 0.1875
- w_key: bfloat16 [2048, 2048], P(None, 'tp'), may hold values from -0.1875 to 0.1875
- w_value: bfloat16 [2048, 2048], P(None, 'tp'), may hold values from -0.125 to 0.125
- w_out: bfloat16 [2048, 2048], P('tp'), may hold values from -0.75 to 0.75
- norm_two: float32 [2048], replicated, may hold values from 0.1 to 1.9
- w_gate: bfloat16 [2048, 5504], P(None, 'tp'), may hold values from -0.125 to 0.125
- w_up: bfloat16 [2048, 5504], P(None, 'tp'), may hold values from -0.125 to 0.125
- w_down: bfloat16 [5504, 2048], P('tp'), may hold values from -0.078125 to 0.078125
- starts: int32 [8192], P('seq'), may hold values from 0 to 8191, as said below
- cotangent: bfloat16 [8192, 2048], P('seq'), may hold values from -6 to 6
Outputs:
- output: bfloat16 [8192, 2048], P('seq')
- grad_input: float32 [8192, 2048], P('seq')
- grad_norm_one: float32 [2048], P('seq')
- grad_query: float32 [2048, 2048], P('seq', 'tp')
- grad_key: float32 [2048, 2048], P('seq', 'tp')
- grad_value: float32 [2048, 2048], P('seq', 'tp')
- grad_out: float32 [2048, 2048], P('tp', 'seq')
- grad_norm_two: float32 [2048], P('seq')
- grad_gate: float32 [2048, 5504], P('seq', 'tp')
- grad_up: float32 [2048, 5504], P('seq', 'tp')
- grad_down: float32 [5504, 2048], P('tp', 'seq')
Inputs may be any that keep to these rules, and one draw needn't show every extreme that they name: starts never falls along the tokens, starts[i] <= i, and all tokens from starts[i] to i have the same start: at most five sequences laid end to end. One of them begins within the first 1024 tokens and ends within the last 1024.
All inputs are finite; a program needn't handle non-finite values.
Results may differ from a plain program's by a relative error of at most 0.015.
The roundings to bfloat16 on the way count: a program that leaves them out, or rounds other values in their place, can miss the bound.
Values may be sent and summed in bfloat16 or wider, within the bound.
No kernel may reach another device: no remote copies, remote signals or barrier semaphores. Data moves between devices by JAX's collectives and lax.ppermute only.
A program may use at most 320 MiB of HBM per device.

v0:
```python
import jax
import jax.numpy as jnp
from jax import lax
from jax.sharding import PartitionSpec as P

HEAD = 128
WINDOW = 2048


def shifted(array, axis, by):
    peers = lax.axis_size(axis)
    pairs = [(i, i + by) for i in range(peers) if 0 <= i + by < peers]
    return lax.ppermute(array, axis, pairs)


def normalize(values, gain):
    factor = lax.rsqrt(jnp.mean(values * values, axis=-1, keepdims=True) + 1e-06)
    return values * factor * gain


def rotary_tables(positions):
    half_head = HEAD // 2
    freqs = 10000.0 ** (-2.0 * jnp.arange(half_head, dtype=jnp.float32) / HEAD)
    angles = positions.astype(jnp.float32)[:, None] * freqs[None, :]
    return (jnp.cos(angles), jnp.sin(angles))


def rotate(values, cosine, sine_table):
    half_head = values.shape[-1] // 2
    lower_half = values[..., :half_head]
    upper_half = values[..., half_head:]
    cos_wide = cosine[:, None, :]
    sin_wide = sine_table[:, None, :]
    return jnp.concatenate(
        [
            lower_half * cos_wide - upper_half * sin_wide,
            upper_half * cos_wide + lower_half * sin_wide,
        ],
        axis=-1,
    )


def gated(gate, up_proj):
    return jax.nn.silu(gate) * up_proj


def outer(left, right):
    return lax.dot_general(
        left, right, (((0,), (0,)), ((), ())), preferred_element_type=jnp.float32
    )


def against(left, right):
    return lax.dot_general(
        left, right, (((1,), (1,)), ((), ())), preferred_element_type=jnp.float32
    )


def on_device(
    block_input,
    norm_one,
    w_query,
    w_key,
    w_value,
    w_out,
    norm_two,
    w_gate,
    w_up,
    w_down,
    starts,
    cotangent,
):
    tok_rows = block_input.shape[0]
    local_heads = w_query.shape[1] // HEAD
    reach = WINDOW // tok_rows
    scale = HEAD ** (-0.5)
    offset = lax.axis_index("seq") * tok_rows
    row_index = offset + jnp.arange(tok_rows, dtype=jnp.int32)
    col_index = offset - reach * tok_rows + jnp.arange((reach + 1) * tok_rows, dtype=jnp.int32)
    allowed = (
        (col_index[None, :] <= row_index[:, None])
        & (col_index[None, :] > row_index[:, None] - WINDOW)
        & (col_index[None, :] >= starts[:, None])
    )
    allowed = allowed[None]
    cosine, sine_table = rotary_tables(row_index - starts)
    input_float = block_input.astype(jnp.float32)
    normed_one, pull_one = jax.vjp(normalize, input_float, norm_one)
    hidden_one = normed_one.astype(jnp.bfloat16)
    query_pre = jnp.dot(hidden_one, w_query, preferred_element_type=jnp.float32).reshape(
        tok_rows, local_heads, HEAD
    )
    key_pre = jnp.dot(hidden_one, w_key, preferred_element_type=jnp.float32).reshape(
        tok_rows, local_heads, HEAD
    )
    value_pre = jnp.dot(hidden_one, w_value, preferred_element_type=jnp.float32)
    query = rotate(query_pre, cosine, sine_table).astype(jnp.bfloat16)
    key_rot = rotate(key_pre, cosine, sine_table).astype(jnp.bfloat16)
    packed = jnp.stack([key_rot.reshape(tok_rows, -1), value_pre.astype(jnp.bfloat16)])

    def raw_scores(all_keys):
        scores = (
            jnp.einsum("qhd,khd->hqk", query, all_keys, preferred_element_type=jnp.float32) * scale
        )
        return jnp.where(allowed, scores, -1e30)

    pieces = [shifted(packed, "seq", shift_step) for shift_step in range(reach, 0, -1)]
    both = jnp.concatenate(pieces + [packed], axis=1)
    keys_all = both[0].reshape(-1, local_heads, HEAD)
    values_all = both[1].reshape(-1, local_heads, HEAD)
    scores = raw_scores(keys_all)
    peak = jnp.max(scores, axis=-1, keepdims=True)
    expo = jnp.exp(scores - peak)
    total = jnp.sum(expo, axis=-1, keepdims=True)
    probs = expo / total
    heads_out = jnp.einsum(
        "hqk,khd->qhd", probs.astype(jnp.bfloat16), values_all, preferred_element_type=jnp.float32
    )
    attended = heads_out.reshape(tok_rows, -1).astype(jnp.bfloat16)
    attn_part = jnp.dot(attended, w_out, preferred_element_type=jnp.float32)
    mid_rows = input_float + lax.psum(attn_part, "tp")
    normed_two, pull_two = jax.vjp(normalize, mid_rows, norm_two)
    hidden_two = normed_two.astype(jnp.bfloat16)
    gate = jnp.dot(hidden_two, w_gate, preferred_element_type=jnp.float32)
    up_proj = jnp.dot(hidden_two, w_up, preferred_element_type=jnp.float32)
    product, pull_gated = jax.vjp(gated, gate, up_proj)
    activation = product.astype(jnp.bfloat16)
    mlp_part = jnp.dot(activation, w_down, preferred_element_type=jnp.float32)
    grad_down = outer(activation, cotangent)
    d_act = against(cotangent, w_down)
    d_gate, d_up = pull_gated(d_act)
    d_gate_low = d_gate.astype(jnp.bfloat16)
    d_up_low = d_up.astype(jnp.bfloat16)
    grad_gate = outer(hidden_two, d_gate_low)
    grad_up = outer(hidden_two, d_up_low)
    d_two_part = against(d_gate_low, w_gate) + against(d_up_low, w_up)
    output = (mid_rows + lax.psum(mlp_part.astype(jnp.bfloat16), "tp").astype(jnp.float32)).astype(
        jnp.bfloat16
    )
    d_hidden_two = lax.psum(d_two_part, "tp")
    d_mid_part, grad_norm_two = pull_two(d_hidden_two)
    d_mid = cotangent.astype(jnp.float32) + d_mid_part
    d_mid_low = d_mid.astype(jnp.bfloat16)
    grad_out = outer(attended, d_mid_low)
    d_attended = against(d_mid_low, w_out).astype(jnp.bfloat16).reshape(tok_rows, local_heads, HEAD)
    probs_back = jnp.exp(raw_scores(keys_all) - peak) / total
    d_probs = jnp.einsum("qhd,khd->hqk", d_attended, values_all, preferred_element_type=jnp.float32)
    grad_values = jnp.einsum(
        "hqk,qhd->khd",
        probs_back.astype(jnp.bfloat16),
        d_attended,
        preferred_element_type=jnp.float32,
    )
    delta = jnp.sum(d_probs * probs_back, axis=-1, keepdims=True)
    d_scores = (probs_back * (d_probs - delta)).astype(jnp.bfloat16)
    d_query_rot = (
        jnp.einsum("hqk,khd->qhd", d_scores, keys_all, preferred_element_type=jnp.float32) * scale
    )
    grad_keys = (
        jnp.einsum("hqk,qhd->khd", d_scores, query, preferred_element_type=jnp.float32) * scale
    )
    grad_window = jnp.stack(
        [grad_keys.reshape(-1, local_heads * HEAD), grad_values.reshape(-1, local_heads * HEAD)]
    )
    owned = grad_window[:, reach * tok_rows :]
    for shift_step in range(1, reach + 1):
        slot = reach - shift_step
        owned = owned + shifted(
            grad_window[:, slot * tok_rows : (slot + 1) * tok_rows], "seq", -shift_step
        )
    d_key_rot = owned[0].reshape(tok_rows, local_heads, HEAD)
    d_value_low = owned[1].astype(jnp.bfloat16)
    d_query_low = (
        rotate(d_query_rot, cosine, -sine_table).reshape(tok_rows, -1).astype(jnp.bfloat16)
    )
    d_key_low = rotate(d_key_rot, cosine, -sine_table).reshape(tok_rows, -1).astype(jnp.bfloat16)
    grad_query = outer(hidden_one, d_query_low)
    grad_key = outer(hidden_one, d_key_low)
    grad_value = outer(hidden_one, d_value_low)
    d_one_part = (
        against(d_query_low, w_query) + against(d_key_low, w_key) + against(d_value_low, w_value)
    )
    d_hidden_one = lax.psum(d_one_part, "tp")
    d_input_part, grad_norm_one = pull_one(d_hidden_one)
    grad_input = d_mid + d_input_part
    (
        grad_query,
        grad_key,
        grad_value,
        grad_out,
        grad_norm_one,
        grad_norm_two,
        grad_gate,
        grad_up,
        grad_down,
    ) = (
        lax.psum_scatter(grad_query, "seq", scatter_dimension=0, tiled=True),
        lax.psum_scatter(grad_key, "seq", scatter_dimension=0, tiled=True),
        lax.psum_scatter(grad_value, "seq", scatter_dimension=0, tiled=True),
        lax.psum_scatter(grad_out, "seq", scatter_dimension=1, tiled=True),
        lax.psum_scatter(grad_norm_one, "seq", scatter_dimension=0, tiled=True),
        lax.psum_scatter(grad_norm_two, "seq", scatter_dimension=0, tiled=True),
        lax.psum_scatter(grad_gate, "seq", scatter_dimension=0, tiled=True),
        lax.psum_scatter(grad_up, "seq", scatter_dimension=0, tiled=True),
        lax.psum_scatter(grad_down, "seq", scatter_dimension=1, tiled=True),
    )
    return (
        output,
        grad_input,
        grad_norm_one,
        grad_query,
        grad_key,
        grad_value,
        grad_out,
        grad_norm_two,
        grad_gate,
        grad_up,
        grad_down,
    )


def solution(mesh):
    in_specs = (
        P("seq", None),
        P(),
        P(None, "tp"),
        P(None, "tp"),
        P(None, "tp"),
        P("tp", None),
        P(),
        P(None, "tp"),
        P(None, "tp"),
        P("tp", None),
        P("seq"),
        P("seq", None),
    )
    out_specs = (
        P("seq", None),
        P("seq", None),
        P("seq"),
        P("seq", "tp"),
        P("seq", "tp"),
        P("seq", "tp"),
        P("tp", "seq"),
        P("seq"),
        P("seq", "tp"),
        P("seq", "tp"),
        P("tp", "seq"),
    )
    return jax.shard_map(
        on_device, mesh=mesh, in_specs=in_specs, out_specs=out_specs, check_vma=False
    )
```

profile of v0, /device:TPU:0, one launch (start us, length us, event | category | flops | bytes accessed | tf_op | source)
XLA Modules:
  0.0 1761.2 jit_solution(4484422797995187314)
XLA Ops:
  11.1 5.1 fusion.42
  25.1 5.4 fusion.61
  40.0 6.1 subtract_convert_fusion.2
  60.8 5.3 compare_and_fusion
  66.1 39.8 %collective-permute-done = bf16[2,1024,512]{2,1,0:T(8,128)(2,1)} collective-permute-done((bf16[2,1024,512]{2,1,0:T(8,128)(2,1)}, bf16[2,1024,512]{2,1,0:T(8,128)(2,1)}, u32[]{:S(2)}, u32[]{:S(2)}) %collective-permute-start) | collective-permute-done | bytes 2097184 | tf_op jit(solution)/shard_map/ppermute | solution.py:13
  117.4 5.6 reshape_squeeze.9
  123.0 24.8 %fusion.67 = (f32[4,1024]{1,0:T(4,128)S(1)}, f32[4,1024,3072]{2,1,0:T(8,128)}) fusion(pred[1024,3072]{1,0:T(8,128)(4,1)} %compare_and_fusion, bf16[3072,4,128]{0,2,1:T(8,128)(2,1)} %bitcast.71, bf16[1024,4,64]{2,0,1:T(8,128)(2,1)} %get-tuple-element.31, bf16[1024,4,64]{2,0,1:T(8,128)(2,1)S(1)} %copy-done.11), kind=kOutput, calls=%fused_computation.110 | convolution fusion | flops 3273657344 | bytes 57688064 | tf_op jit(solution)/shard_map/sub | solution.py:113
  147.8 18.7 %fusion.34 = bf16[4,128,1024]{2,1,0:T(8,128)(2,1)S(1)} fusion(bf16[3072,4,128]{2,1,0:T(4,128)(2,1)} %reshape_squeeze.9, f32[4,1024,3072]{2,1,0:T(8,128)} %get-tuple-element.50, f32[4,1024]{1,0:T(4,128)S(1)} %get-tuple-element.49), kind=kOutput, calls=%fused_computation.76 | convolution fusion | flops 3246915584 | bytes 54542336 | tf_op jit(solution)/shard_map/hqk,khd->qhd/dot_general | solution.py:116
  167.5 5.8 fusion.68
  173.8 193.2 %all-reduce.8.cloned.1.call-done = f32[1024,2048]{1,0:T(8,128)} async-done(((f32[1024,2048]{1,0:T(8,128)}), f32[1024,2048]{1,0:T(8,128)}) %all-reduce.8.cloned.1.call-update) | async-done | bytes 8388624 | tf_op jit(solution)/shard_map/psum | solution.py:121
  367.1 5.7 multiply_reduce_fusion.3
  378.2 9.8 fusion.70
  388.0 11.0 fusion.69
  399.0 14.9 multiply_convert_fusion.2
  413.9 9.7 fusion.71
  423.6 9.5 convolution_add_fusion
  433.2 11.0 convolution_convert_fusion
  444.2 161.8 %all-reduce.12.cloned.1.call-done = f32[1024,2048]{1,0:T(8,128)} async-done(((f32[1024,2048]{1,0:T(8,128)}), f32[1024,2048]{1,0:T(8,128)}) %all-reduce.12.cloned.1.call-update) | async-done | bytes 8388624 | tf_op jit(solution)/shard_map/psum | solution.py:140
  606.0 7.8 multiply_reduce_fusion.1
  613.8 100.7 %all-reduce.10.cloned.1.call-done = bf16[1024,2048]{1,0:T(8,128)(2,1)} async-done(((bf16[1024,2048]{1,0:T(8,128)(2,1)}), bf16[1024,2048]{1,0:T(8,128)(2,1)}) %all-reduce.10.cloned.1.call-update) | async-done | bytes 4194320 | tf_op jit(solution)/shard_map/psum | solution.py:137
  714.5 12.3 fusion.13
  731.1 19.7 %fusion.5 = f32[4,128,3072]{2,1,0:T(8,128)} fusion(bf16[1024,4,128]{0,2,1:T(8,128)(2,1)S(1)} %bitcast.83, f32[4,1024,3072]{2,1,0:T(8,128)} %get-tuple-element.50, f32[4,1024]{1,0:T(4,128)S(1)} %get-tuple-element.49), kind=kOutput, calls=%fused_computation.21 | convolution fusion | flops 3246391296 | bytes 57688064 | tf_op jit(solution)/shard_map/hqk,qhd->khd/dot_general | solution.py:148
  750.9 32.8 %multiply_reduce_fusion = (f32[4,1024]{1,0:T(4,128)S(1)}, f32[4,1024,3072]{2,1,0:T(8,128)}) fusion(f32[4,1024,3072]{2,1,0:T(8,128)} %get-tuple-element.50, f32[4,1024]{1,0:T(4,128)S(1)} %get-tuple-element.49, bf16[1024,4,128]{0,2,1:T(8,128)(2,1)} %bitcast.84, bf16[3072,4,128]{2,1,0:T(4,128)(2,1)} %reshape_squeeze.9), kind=kOutput, calls=%fused_computation.2 | convolution fusion | flops 3258970112 | bytes 104890368 | tf_op jit(solution)/shard_map/qhd,khd->hqk/dot_general | solution.py:147
  783.7 40.5 %multiply_convert_fusion = bf16[4,1024,3072]{2,1,0:T(8,128)(2,1)} fusion(f32[4,1024,3072]{2,1,0:T(8,128)} %get-tuple-element.52, f32[4,1024]{1,0:T(4,128)S(1)} %get-tuple-element.51, f32[4,1024,3072]{2,1,0:T(8,128)} %get-tuple-element.50, f32[4,1024]{1,0:T(4,128)S(1)} %get-tuple-element.49), kind=kLoop, calls=%fused_computation.1 | loop fusion | flops 50331648 | bytes 125861888 | tf_op jit(solution)/shard_map/convert_element_type | solution.py:155
  824.2 10.6 convolution_multiply_fusion
  834.8 5.4 fusion.23
  842.8 12.6 multiply_bitcast_fusion
  855.4 124.9 %collective-permute-done.3 = f32[2,1024,512]{1,2,0:T(8,128)} collective-permute-done((f32[2,1024,512]{1,2,0:T(8,128)}, f32[2,1024,512]{1,2,0:T(8,128)}, u32[]{:S(2)}, u32[]{:S(2)}) %collective-permute-start.3) | collective-permute-done | bytes 4194336 | tf_op jit(solution)/shard_map/ppermute | solution.py:13
  980.3 5.6 fusion.26
  1006.9 5.7 fusion.72
  1012.6 9.4 add_add_fusion.2
  1023.2 7.7 fusion.30
  1031.6 7.0 fusion.56
  1039.8 7.0 fusion.54
  1046.9 7.8 fusion.44
  1054.7 11.2 fusion.76
  1066.0 11.2 fusion.75
  1077.5 11.2 fusion.74
  1090.6 102.8 %all-reduce.14.cloned.1.call-done = f32[1024,2048]{1,0:T(8,128)} async-done(((f32[1024,2048]{1,0:T(8,128)}), f32[1024,2048]{1,0:T(8,128)}) %all-reduce.14.cloned.1.call-update) | async-done | bytes 8388624 | tf_op jit(solution)/shard_map/psum | solution.py:183
  1193.3 6.1 fusion.12
  1199.5 30.2 %all-reduce.2 = (f32[2048]{0:T(1024)S(1)}, f32[2048]{0:T(1024)S(1)}) all-reduce(f32[2048]{0:T(1024)S(1)} %get-tuple-element.13, f32[2048]{0:T(1024)S(1)} %copy-done.25), channel_id=2, replica_groups=mesh['seq'=8,'tp'=4] {'seq'}, use_global_device_ids=true, to_apply=%region_12.13.clone | all-reduce | flops 4096 | bytes 32768
  1231.0 12.0 fusion.14
  1247.3 50.9 %reduce-scatter.8.cloned.1.call-done = f32[256,512]{1,0:T(8,128)} async-done(((f32[2048,512]{1,0:T(8,128)}), f32[256,512]{1,0:T(8,128)}) %reduce-scatter.8.cloned.1.call-update) | async-done | bytes 524304 | tf_op jit(solution)/shard_map/reduce_scatter | solution.py:197
  1298.2 51.0 %reduce-scatter.10.cloned.1.call-done = f32[256,512]{1,0:T(8,128)} async-done(((f32[2048,512]{1,0:T(8,128)}), f32[256,512]{1,0:T(8,128)}) %reduce-scatter.10.cloned.1.call-update) | async-done | bytes 524304 | tf_op jit(solution)/shard_map/reduce_scatter | solution.py:198
  1349.2 51.0 %reduce-scatter.12.cloned.1.call-done = f32[256,512]{1,0:T(8,128)} async-done(((f32[2048,512]{1,0:T(8,128)}), f32[256,512]{1,0:T(8,128)}) %reduce-scatter.12.cloned.1.call-update) | async-done | bytes 524304 | tf_op jit(solution)/shard_map/reduce_scatter | solution.py:199
  1400.3 117.9 %reduce-scatter.18.cloned.1.call-done = f32[256,1376]{0,1:T(8,128)} async-done(((f32[2048,1376]{0,1:T(8,128)}), f32[256,1376]{0,1:T(8,128)}) %reduce-scatter.18.cloned.1.call-update) | async-done | bytes 1409040 | tf_op jit(solution)/shard_map/reduce_scatter | solution.py:204
  1518.2 118.0 %reduce-scatter.16.cloned.1.call-done = f32[256,1376]{0,1:T(8,128)} async-done(((f32[2048,1376]{0,1:T(8,128)}), f32[256,1376]{0,1:T(8,128)}) %reduce-scatter.16.cloned.1.call-update) | async-done | bytes 1409040 | tf_op jit(solution)/shard_map/reduce_scatter | solution.py:203
  1636.1 118.1 %reduce-scatter.20.cloned.1.call-done = f32[1376,256]{1,0:T(8,128)} async-done(((f32[1376,2048]{1,0:T(8,128)}), f32[1376,256]{1,0:T(8,128)}) %reduce-scatter.20.cloned.1.call-update) | async-done | bytes 1409040 | tf_op jit(solution)/shard_map/reduce_scatter | solution.py:205
  (148 shorter events, 93.9 us)
Async XLA Ops:
  7.2 160.3 %copy-start = (bf16[512,2048]{1,0:T(8,128)(2,1)S(1)}, bf16[512,2048]{1,0:T(8,128)(2,1)}, u32[]{:S(2)}) copy-start(bf16[512,2048]{1,0:T(8,128)(2,1)} %param.17) | copy-start | bytes 6291460
  7.2 3.9 copy-start.26
  7.2 359.9 %all-reduce.8.cloned.1.call-start = ((), (), s32[]{:S(2)}) async-start(), calls=%async_computation.7 | async-start | bytes 16777216 | tf_op jit(solution)/shard_map/psum | solution.py:121
  7.3 3.8 copy-start.3
  11.1 14.0 copy-start.21
  11.1 5.1 copy-start.29
  31.6 5.1 copy-start.28
  40.0 6.1 copy-start.7
  52.6 13.5 collective-permute-start.1
  56.3 49.5 %collective-permute-start = (bf16[2,1024,512]{2,1,0:T(8,128)(2,1)}, bf16[2,1024,512]{2,1,0:T(8,128)(2,1)}, u32[]{:S(2)}, u32[]{:S(2)}) collective-permute-start(bf16[2,1024,512]{2,1,0:T(8,128)(2,1)} %pad_maximum_fusion.1), channel_id=1, source_target_pairs={{0,8},{4,12},{8,16},{12,20},{16,24},{20,28},{1,9},{5,13},{9,17},{1... | collective-permute-start | bytes 6291464 | tf_op jit(solution)/shard_map/ppermute | solution.py:13
  117.4 5.6 copy-start.11
  173.3 199.5 %copy-start.20 = (f32[2048]{0:T(1024)S(1)}, f32[2048]{0:T(1024)}, u32[]{:S(2)}) copy-start(f32[2048]{0:T(1024)} %param.18) | copy-start | bytes 24580
  173.3 432.7 %all-reduce.12.cloned.1.call-start = ((), (), s32[]{:S(2)}) async-start(), calls=%async_computation.9 | async-start | bytes 16777216 | tf_op jit(solution)/shard_map/psum | solution.py:140
  372.8 3.4 copy-start.2
  376.2 2.0 copy-start.10
  388.0 11.0 copy-start.9
  388.0 25.9 %slice-start.2 = ((s8[5636096]{0:T(1024)(128)(4,1)}), s8[4194304]{0:T(1024)(128)(4,1)S(1)}, s32[]{:S(2)}) async-start(s8[5636096]{0:T(1024)(128)(4,1)} %bitcast.79), calls=%async_computation.20 | async-start | bytes 8388608
  388.0 35.6 %slice-start = ((s8[5636096]{0:T(1024)(128)(4,1)}), s8[4194304]{0:T(1024)(128)(4,1)S(1)}, s32[]{:S(2)}) async-start(s8[5636096]{0:T(1024)(128)(4,1)} %bitcast.69), calls=%async_computation.18 | async-start | bytes 8388608
  399.0 14.9 slice-start.3
  399.0 24.6 %slice-start.1 = ((s8[5636096]{0:T(1024)(128)(4,1)}), s8[1441792]{0:T(1024)(128)(4,1)S(1)}, s32[]{:S(2)}) async-start(s8[5636096]{0:T(1024)(128)(4,1)} %bitcast.69), calls=%async_computation.19 | async-start | bytes 2883584
  413.9 9.7 copy-start.16
  433.1 281.4 %all-reduce.10.cloned.1.call-start = ((), (), s32[]{:S(2)}) async-start(), calls=%async_computation.8 | async-start | bytes 8388608 | tf_op jit(solution)/shard_map/psum | solution.py:137
  444.2 749.2 %all-reduce.14.cloned.1.call-start = ((), (), s32[]{:S(2)}) async-start(), calls=%async_computation.10 | async-start | bytes 16777216 | tf_op jit(solution)/shard_map/psum | solution.py:183
  726.8 3.4 copy-start.4
  783.7 40.5 %copy-start.12 = (bf16[1024,4,64]{2,0,1:T(8,128)(2,1)S(1)}, bf16[1024,4,64]{2,0,1:T(8,128)(2,1)}, u32[]{:S(2)}) copy-start(bf16[1024,4,64]{2,0,1:T(8,128)(2,1)} %get-tuple-element.30) | copy-start | bytes 1572868
  783.7 40.5 %copy-start.13 = (bf16[1024,4,64]{2,0,1:T(8,128)(2,1)S(1)}, bf16[1024,4,64]{2,0,1:T(8,128)(2,1)}, u32[]{:S(2)}) copy-start(bf16[1024,4,64]{2,0,1:T(8,128)(2,1)} %get-tuple-element.31) | copy-start | bytes 1572868
  840.3 15.2 collective-permute-start.2
  841.5 138.8 %collective-permute-start.3 = (f32[2,1024,512]{1,2,0:T(8,128)}, f32[2,1024,512]{1,2,0:T(8,128)}, u32[]{:S(2)}, u32[]{:S(2)}) collective-permute-start(f32[2,1024,512]{1,2,0:T(8,128)} %get-tuple-element.20), channel_id=1, source_target_pairs={{8,0},{12,4},{16,8},{20,12},{24,16},{28,20},{9,1},{13,5},{17,9},{2... | collective-permute-start | bytes 12582920 | tf_op jit(solution)/shard_map/ppermute | solution.py:13
  985.9 2.6 copy-start.5
  988.5 6.5 copy-start.8
  988.5 6.5 copy-start.18
  999.2 1.9 copy-start.14
  999.2 1.9 copy-start.15
  1002.4 4.5 copy-start.30
  1006.9 5.7 copy-start.6
  1006.9 5.7 copy-start.17
  1022.0 1.2 copy-start.32
  1022.0 225.3 %reduce-scatter.14.cloned.1.call-start = ((), (), s32[]{:S(2)}) async-start(), calls=%async_computation.14 | async-start | bytes 4718592 | tf_op jit(solution)/shard_map/reduce_scatter | solution.py:200
  1030.9 267.3 %reduce-scatter.8.cloned.1.call-start = ((), (), s32[]{:S(2)}) async-start(), calls=%async_computation.11 | async-start | bytes 4718592 | tf_op jit(solution)/shard_map/reduce_scatter | solution.py:197
  1038.6 1.2 copy-start.19
  1038.6 310.6 %reduce-scatter.10.cloned.1.call-start = ((), (), s32[]{:S(2)}) async-start(), calls=%async_computation.12 | async-start | bytes 4718592 | tf_op jit(solution)/shard_map/reduce_scatter | solution.py:198
  1046.8 353.5 %reduce-scatter.12.cloned.1.call-start = ((), (), s32[]{:S(2)}) async-start(), calls=%async_computation.13 | async-start | bytes 4718592 | tf_op jit(solution)/shard_map/reduce_scatter | solution.py:199
  1054.6 463.5 %reduce-scatter.18.cloned.1.call-start = ((), (), s32[]{:S(2)}) async-start(), calls=%async_computation.16 | async-start | bytes 12681216 | tf_op jit(solution)/shard_map/reduce_scatter | solution.py:204
  1065.9 570.2 %reduce-scatter.16.cloned.1.call-start = ((), (), s32[]{:S(2)}) async-start(), calls=%async_computation.15 | async-start | bytes 12681216 | tf_op jit(solution)/shard_map/reduce_scatter | solution.py:203
  1077.2 677.1 %reduce-scatter.20.cloned.1.call-start = ((), (), s32[]{:S(2)}) async-start(), calls=%async_computation.17 | async-start | bytes 12681216 | tf_op jit(solution)/shard_map/reduce_scatter | solution.py:205
  1090.5 108.9 %copy-start.25 = (f32[2048]{0:T(1024)S(1)}, f32[2048]{0:T(1024)}, u32[]{:S(2)}) copy-start(f32[2048]{0:T(1024)} %get-tuple-element.11) | copy-start | bytes 24580
  1090.5 140.4 %copy-start.24 = (f32[1024]{0:T(1024)S(1)}, f32[1024]{0:T(1024)}, u32[]{:S(2)}) copy-start(f32[1024]{0:T(1024)} %copy-done.23) | copy-start | bytes 12292
  1231.0 523.3 %copy-start.1 = (bf16[512,2048]{1,0:T(8,128)(2,1)S(1)}, bf16[512,2048]{1,0:T(8,128)(2,1)}, u32[]{:S(2)}) copy-start(bf16[512,2048]{1,0:T(8,128)(2,1)} %param.17) | copy-start | bytes 6291460
  (6 other events, 4.6 us)
Sparse Core Ops, SparseCore 0:
  173.4 193.6 all-reduce.7
  433.2 172.7 all-reduce.11
  609.9 104.5 all-reduce.9
  1022.1 171.1 all-reduce.13
  1196.0 51.2 reduce-scatter.13
  1250.0 48.1 reduce-scatter.7
  1301.1 48.1 reduce-scatter.9
  1352.1 48.1 reduce-scatter.11
  1403.2 114.9 reduce-scatter.17
  1520.9 115.1 reduce-scatter.15
  1639.0 115.1 reduce-scatter.19
where the time goes:
time: 1770 us; the launch traced here: 1760 us
  waiting for transfers between devices  1230 us (69%)
  matrix products  289 us (16%)
  other arithmetic  127 us (7%)
  local copies, waits for them, and re-layouts  53.6 us (3%)
  blocking collectives  30.2 us (2%)
    psum x1, waiting for transfers between devices, on_device(): mid_rows = input_float + lax.psum(attn_part, 'tp')  193 us
    ppermute x4, waiting for transfers between devices, shifted(): return lax.ppermute(array, axis, pairs)  165 us
    psum x1, waiting for transfers between devices, on_device(): d_hidden_two = lax.psum(d_two_part, 'tp')  162 us
    reduce_scatter x1, waiting for transfers between devices, on_device(): lax.psum_scatter(grad_down, 'seq', scatter_dimension=1, tiled=True)  118 us
    reduce_scatter x1, waiting for transfers between devices, on_device(): lax.psum_scatter(grad_gate, 'seq', scatter_dimension=0, tiled=True)  118 us
    reduce_scatter x1, waiting for transfers between devices, on_device(): lax.psum_scatter(grad_up, 'seq', scatter_dimension=0, tiled=True)  118 us
    psum x1, waiting for transfers between devices, on_device(): d_hidden_one = lax.psum(d_one_part, 'tp')  103 us
    psum x1, waiting for transfers between devices, on_device(): lax.psum(mlp_part.astype(jnp.bfloat16), 'tp').astype(jnp.float32)  101 us
  transfers between devices with their start and end apart: 15, of which 13 were waited for; matrix products, arithmetic and copies ran while one was open for 7% of the time, Pallas kernels for 0%

commit v1 on v0

v1 whole, which is shorter than its diff:
```python
import jax
import jax.numpy as jnp
from jax import lax
from jax.experimental import pallas as pl
from jax.experimental.pallas import tpu as pltpu
from jax.sharding import PartitionSpec as P

HEAD = 128
WINDOW = 2048
LOG2E = 1.4426950408889634
SCALE = HEAD ** (-0.5)
NEG = -1e30
F32 = jnp.float32
BF16 = jnp.bfloat16
MIB = 1024 * 1024

NN = (((1,), (0,)), ((), ()))
NT = (((1,), (1,)), ((), ()))
TN = (((0,), (0,)), ((), ()))


def mm(a, b, dims=NN):
    return lax.dot_general(a, b, dims, preferred_element_type=F32)


def to_relative(array, me, n):
    rows = array.shape[0] // n
    return jnp.concatenate(
        [lax.dynamic_slice_in_dim(array, (r ^ me) * rows, rows, 0) for r in range(n)], axis=0
    )


def to_natural(blocks, me):
    rows = blocks[0].shape[0]
    whole = jnp.zeros((rows * len(blocks),) + blocks[0].shape[1:], blocks[0].dtype)
    for r, block in enumerate(blocks):
        whole = lax.dynamic_update_slice_in_dim(whole, block, (r ^ me) * rows, 0)
    return whole


def swap(array, bit, axis="tp"):
    size = lax.axis_size(axis)
    return lax.ppermute(array, axis, [(i, i ^ bit) for i in range(size)])


def bits_of(n):
    return [1 << b for b in range(n.bit_length() - 1)]


def sum_blocks(part, n):
    rows, width = part.shape[0] // n, part.shape[1]
    halves = []
    for half, order in enumerate((bits_of(n), bits_of(n)[::-1])):
        columns = slice(half * width // 2, (half + 1) * width // 2)
        held = {r: part[r * rows : (r + 1) * rows, columns] for r in range(n)}
        for bit in order:
            sent = [r for r in held if r & bit]
            got = swap(jnp.concatenate([held[r] for r in sent]).astype(BF16), bit)
            held = {
                r ^ bit: held[r ^ bit].astype(F32)
                + got[k * rows : (k + 1) * rows].astype(F32)
                for k, r in enumerate(sent)
            }
        halves.append(held[0])
    return jnp.concatenate(halves, axis=1)


def all_blocks(own, n):
    rows, width = own.shape
    halves = []
    for half, order in enumerate((bits_of(n)[::-1], bits_of(n))):
        held = {0: own[:, half * width // 2 : (half + 1) * width // 2]}
        for bit in order:
            have = sorted(held)
            got = swap(jnp.concatenate([held[r] for r in have]), bit)
            for k, r in enumerate(have):
                held[r ^ bit] = got[k * rows : (k + 1) * rows]
        halves.append(held)
    return [jnp.concatenate([half[r] for half in halves], axis=1) for r in range(n)]


def rotated(a, cosine, sine):
    return a * cosine + pltpu.roll(a, HEAD // 2, 1) * sine


def qkv_kernel(me_ref, x_ref, gain_ref, wq_ref, wk_ref, wv_ref, cos_ref, sin_ref, h_ref, q_ref, k_ref, v_ref):
    x = x_ref[...].astype(F32)
    factor = lax.rsqrt(jnp.mean(x * x, axis=-1, keepdims=True) + 1e-06)
    hidden = (x * factor * gain_ref[...]).astype(BF16)
    h_ref[...] = hidden
    cosine, sine = cos_ref[...], sin_ref[...]
    for w_ref, out_ref in ((wk_ref, k_ref), (wq_ref, q_ref)):
        pre = mm(hidden, w_ref[...])
        for head in range(pre.shape[1] // HEAD):
            cols = slice(head * HEAD, (head + 1) * HEAD)
            out_ref[:, cols] = rotated(pre[:, cols], cosine, sine).astype(BF16)
    v_ref[...] = mm(hidden, wv_ref[...]).astype(BF16)


def qkv(me, x, gain, wq, wk, wv, cosine, sine, n):
    tokens, width = x.shape
    local = wq.shape[1]
    rows = tokens // n
    whole = lambda r, m: (0, 0)
    mine = lambda r, m: (r, 0)
    return pl.pallas_call(
        qkv_kernel,
        grid_spec=pltpu.PrefetchScalarGridSpec(
            num_scalar_prefetch=1,
            grid=(n,),
            in_specs=[
                pl.BlockSpec((rows, width), lambda r, m: (r ^ m[0], 0)),
                pl.BlockSpec((1, width), whole),
                pl.BlockSpec((width, local), whole),
                pl.BlockSpec((width, local), whole),
                pl.BlockSpec((width, local), whole),
                pl.BlockSpec((rows, HEAD), mine),
                pl.BlockSpec((rows, HEAD), mine),
            ],
            out_specs=[
                pl.BlockSpec((rows, width), mine),
                pl.BlockSpec((rows, local), mine),
                pl.BlockSpec((rows, local), mine),
                pl.BlockSpec((rows, local), mine),
            ],
        ),
        out_shape=[
            jax.ShapeDtypeStruct((tokens, width), BF16),
            jax.ShapeDtypeStruct((tokens, local), BF16),
            jax.ShapeDtypeStruct((tokens, local), BF16),
            jax.ShapeDtypeStruct((tokens, local), BF16),
        ],
        compiler_params=pltpu.CompilerParams(vmem_limit_bytes=40 * MIB),
        cost_estimate=pl.CostEstimate(
            flops=6 * tokens * width * local,
            bytes_accessed=4 * tokens * width + 6 * (tokens + width) * local,
            transcendentals=0,
        ),
        name="project",
    )(me, x, gain, wq, wk, wv, cosine, sine)


def key_rows(me, rb, c, n, rows):
    w = rb + c
    stored = ((w & ~(n - 1)) | ((w & (n - 1)) ^ me)) * rows
    return pl.multiple_of(stored, rows), w * rows


def masked(s, first, low, query_at, diagonal):
    key_at = first + lax.broadcasted_iota(jnp.int32, s.shape, 0)
    keep = key_at >= low
    if diagonal:
        keep = keep & (key_at <= query_at)
    return jnp.where(keep, s, NEG)


def attend_kernel(n, me_ref, q_ref, k_ref, v_ref, low_ref, o_ref, lse_ref, s_ref, vt_ref):
    rows = q_ref.shape[0]
    me = me_ref[0]
    r = pl.program_id(1)
    rb = r ^ me
    chunks = 2 * n + 1

    @pl.when(r == 0)
    def _():
        for c in range(3 * n):
            cut = slice(c * rows, (c + 1) * rows)
            vt_ref[:, cut] = v_ref[cut, :].T

    q = q_ref[...]
    low = low_ref[...]
    query_at = (rb + 2 * n) * rows + lax.broadcasted_iota(jnp.int32, (1, rows), 1)
    top = jnp.full((1, rows), NEG, F32)
    for c in range(chunks):
        stored, first = key_rows(me, rb, c, n, rows)
        s = mm(k_ref[pl.ds(stored, rows), :], q, NT)
        s = masked(s, first, low, query_at, c == chunks - 1)
        s_ref[c * rows : (c + 1) * rows, :] = s
        top = jnp.maximum(top, jnp.max(s, axis=0, keepdims=True))
    top = top * (SCALE * LOG2E)
    total = jnp.zeros((1, rows), F32)
    acc = jnp.zeros((HEAD, rows), F32)
    for c in range(chunks):
        stored, first = key_rows(me, rb, c, n, rows)
        p = jnp.exp2(s_ref[c * rows : (c + 1) * rows, :] * (SCALE * LOG2E) - top)
        total = total + jnp.sum(p, axis=0, keepdims=True)
        acc = acc + mm(vt_ref[:, pl.ds(stored, rows)], p.astype(BF16))
    o_ref[...] = (acc / total).T.astype(BF16)
    lse_ref[...] = (top + jnp.log2(total)).reshape(lse_ref.shape)


def attend(me, q, keys, values, low, n):
    tokens, local = q.shape
    heads = local // HEAD
    rows = tokens // n
    window = keys.shape[0]
    pairs = heads * tokens * (2 * tokens + rows)
    return pl.pallas_call(
        lambda *refs: attend_kernel(n, *refs),
        grid_spec=pltpu.PrefetchScalarGridSpec(
            num_scalar_prefetch=1,
            grid=(heads, n),
            in_specs=[
                pl.BlockSpec((rows, HEAD), lambda h, r, m: (r, h)),
                pl.BlockSpec((window, HEAD), lambda h, r, m: (0, h)),
                pl.BlockSpec((window, HEAD), lambda h, r, m: (0, h)),
                pl.BlockSpec((1, rows), lambda h, r, m: (0, r)),
            ],
            out_specs=[
                pl.BlockSpec((rows, HEAD), lambda h, r, m: (r, h)),
                pl.BlockSpec((1, 1, rows), lambda h, r, m: (h, 0, r)),
            ],
            scratch_shapes=[
                pltpu.VMEM(((2 * n + 1) * rows, rows), F32),
                pltpu.VMEM((HEAD, window), BF16),
            ],
        ),
        out_shape=[
            jax.ShapeDtypeStruct((tokens, local), BF16),
            jax.ShapeDtypeStruct((heads, 1, tokens), F32),
        ],
        compiler_params=pltpu.CompilerParams(vmem_limit_bytes=40 * MIB),
        cost_estimate=pl.CostEstimate(
            flops=8 * pairs * HEAD, bytes_accessed=16 * tokens * local, transcendentals=pairs
        ),
        name="attend",
    )(me, q, keys, values, low)


def attend_back_kernel(
    n, me_ref, q_ref, k_ref, v_ref, low_ref, o_ref, do_ref, lse_ref, cos_ref, sin_ref,
    dq_ref, dk_ref, dv_ref, dk_acc, dv_acc, kt_ref,
):
    rows = q_ref.shape[0]
    me = me_ref[0]
    r = pl.program_id(1)
    rb = r ^ me
    chunks = 2 * n + 1

    @pl.when(r == 0)
    def _():
        for c in range(3 * n):
            cut = slice(c * rows, (c + 1) * rows)
            kt_ref[:, cut] = k_ref[cut, :].T
            dk_acc[cut, :] = jnp.zeros((rows, HEAD), F32)
            dv_acc[cut, :] = jnp.zeros((rows, HEAD), F32)

    q, do = q_ref[...], do_ref[...]
    low = low_ref[...]
    lse = lse_ref[...].reshape(1, rows)
    delta = jnp.sum((do.astype(F32) * o_ref[...].astype(F32)).T, axis=0, keepdims=True)
    query_at = (rb + 2 * n) * rows + lax.broadcasted_iota(jnp.int32, (1, rows), 1)
    dqt = jnp.zeros((HEAD, rows), F32)
    for c in range(chunks):
        stored, first = key_rows(me, rb, c, n, rows)
        here = pl.ds(stored, rows)
        s = mm(k_ref[here, :], q, NT) * (SCALE * LOG2E)
        s = masked(s, first, low, query_at, c == chunks - 1)
        p = jnp.exp2(s - lse)
        dv_acc[here, :] += mm(p.astype(BF16), do)
        dp = mm(v_ref[here, :], do, NT)
        ds = (p * (dp - delta)).astype(BF16)
        dk_acc[here, :] += mm(ds, q)
        dqt = dqt + mm(kt_ref[:, here], ds)
    dq_ref[...] = rotated(dqt.T * SCALE, cos_ref[...], -sin_ref[...]).astype(BF16)

    @pl.when(r == n - 1)
    def _():
        for c in range(3 * n):
            cut = slice(c * rows, (c + 1) * rows)
            dk_ref[cut, :] = (dk_acc[cut, :] * SCALE).astype(BF16)
            dv_ref[cut, :] = dv_acc[cut, :].astype(BF16)


def attend_back(me, q, keys, values, low, attended, d_attended, lse, cosine, sine, n):
    tokens, local = q.shape
    heads = local // HEAD
    rows = tokens // n
    window = keys.shape[0]
    pairs = heads * tokens * (2 * tokens + rows)
    block = pl.BlockSpec((rows, HEAD), lambda h, r, m: (r, h))
    whole = pl.BlockSpec((window, HEAD), lambda h, r, m: (0, h))
    table = pl.BlockSpec((rows, HEAD), lambda h, r, m: (r, 0))
    return pl.pallas_call(
        lambda *refs: attend_back_kernel(n, *refs),
        grid_spec=pltpu.PrefetchScalarGridSpec(
            num_scalar_prefetch=1,
            grid=(heads, n),
            in_specs=[
                block,
                whole,
                whole,
                pl.BlockSpec((1, rows), lambda h, r, m: (0, r)),
                block,
                block,
                pl.BlockSpec((1, 1, rows), lambda h, r, m: (h, 0, r)),
                table,
                table,
            ],
            out_specs=[block, whole, whole],
            scratch_shapes=[
                pltpu.VMEM((window, HEAD), F32),
                pltpu.VMEM((window, HEAD), F32),
                pltpu.VMEM((HEAD, window), BF16),
            ],
        ),
        out_shape=[
            jax.ShapeDtypeStruct((tokens, local), BF16),
            jax.ShapeDtypeStruct((window, local), BF16),
            jax.ShapeDtypeStruct((window, local), BF16),
        ],
        compiler_params=pltpu.CompilerParams(vmem_limit_bytes=40 * MIB),
        cost_estimate=pl.CostEstimate(
            flops=20 * pairs * HEAD, bytes_accessed=30 * tokens * local, transcendentals=pairs
        ),
        name="attend_back",
    )(me, q, keys, values, low, attended, d_attended, lse, cosine, sine)


def rotate_wide(values, cosine, sine):
    tokens, local = values.shape
    split = values.reshape(tokens, local // HEAD, 2, HEAD // 2)
    swapped = jnp.concatenate([split[:, :, 1:], split[:, :, :1]], axis=2).reshape(tokens, local)
    heads = local // HEAD
    return values * jnp.tile(cosine, (1, heads)) + swapped * jnp.tile(sine, (1, heads))


def gain_sums(sums, n):
    for bit in bits_of(n):
        sums = sums + swap(sums, bit)
    peers = lax.axis_size("seq")
    at = lax.axis_index("seq")
    for bit in bits_of(peers)[::-1]:
        half = sums.shape[1] // 2
        upper = (at & bit) != 0
        low_part, high_part = sums[:, :half], sums[:, half:]
        kept = jnp.where(upper, high_part, low_part)
        sums = kept + swap(jnp.where(upper, low_part, high_part), bit, "seq")
    return sums


def scattered(grad, dim):
    return lax.psum_scatter(grad.astype(BF16), "seq", scatter_dimension=dim, tiled=True).astype(F32)


def on_device(
    block_input, norm_one, w_query, w_key, w_value, w_out, norm_two, w_gate, w_up, w_down,
    starts, cotangent,
):
    tokens, width = block_input.shape
    n = lax.axis_size("tp")
    me = lax.axis_index("tp")
    peers = lax.axis_size("seq")
    at = lax.axis_index("seq")
    odd = (at & 1) != 0
    rows = tokens // n
    me_array = jnp.full((1,), me, jnp.int32)

    order = to_relative(jnp.arange(tokens, dtype=jnp.int32), me, n)
    starts_here = to_relative(starts, me, n)
    positions = (at * tokens + order - starts_here).astype(F32)
    freqs = 10000.0 ** (-2.0 * jnp.arange(HEAD // 2, dtype=F32) / HEAD)
    angles = positions[:, None] * freqs[None, :]
    cosine, sine = jnp.cos(angles), jnp.sin(angles)
    cosine, sine = jnp.concatenate([cosine, cosine], 1), jnp.concatenate([-sine, sine], 1)
    low = jnp.maximum(starts_here - (at - 2) * tokens, order + 2 * tokens - WINDOW + 1)[None, :]

    hidden_one, query, key, value = qkv(
        me_array, block_input, norm_one[None, :], w_query, w_key, w_value, cosine, sine, n
    )

    right_two = [(i, i + 2) for i in range(peers - 2)]
    left_two = [(i + 2, i) for i in range(peers - 2)]
    to_odd = [(i, i + 1) for i in range(0, peers, 2)]
    to_even = [(i + 1, i) for i in range(0, peers, 2)]
    packed = jnp.stack([key, value])
    before_two = lax.ppermute(packed, "seq", right_two)
    across = lax.ppermute(packed, "seq", to_odd)
    before_one = jnp.where(odd, across, lax.ppermute(before_two, "seq", to_even))
    window = jnp.concatenate([before_two, before_one, packed], axis=1)
    keys, values = window[0], window[1]

    attended, lse = attend(me_array, query, keys, values, low, n)
    attn_part = mm(attended, w_out).astype(BF16)
    input_own = lax.dynamic_slice_in_dim(block_input, me * rows, rows, 0).astype(F32)
    cot_own = lax.dynamic_slice_in_dim(cotangent, me * rows, rows, 0).astype(F32)
    cot = to_relative(cotangent, me, n)
    d_act = mm(cot, w_down, NT)

    mid = input_own + sum_blocks(attn_part, n)
    r_two = lax.rsqrt(jnp.mean(mid * mid, axis=-1, keepdims=True) + 1e-06)
    n_two = mid * r_two
    hidden_two = jnp.concatenate(all_blocks((n_two * norm_two).astype(BF16), n), axis=0)

    gate = mm(hidden_two, w_gate)
    up = mm(hidden_two, w_up)
    s = 1.0 / (1.0 + jnp.exp(-gate))
    silu = gate * s
    activation = (silu * up).astype(BF16)
    d_gate = (d_act * up * s * (1.0 + gate * (1.0 - s))).astype(BF16)
    d_up = (d_act * silu).astype(BF16)
    d_two_part = (mm(d_gate, w_gate, NT) + mm(d_up, w_up, NT)).astype(BF16)
    d_hidden_two = sum_blocks(d_two_part, n)
    e_two = d_hidden_two * norm_two
    d_mid = cot_own + r_two * (e_two - n_two * jnp.mean(e_two * n_two, axis=-1, keepdims=True))
    d_mid_low = jnp.concatenate(all_blocks(d_mid.astype(BF16), n), axis=0)

    mlp_part = mm(activation, w_down).astype(BF16)
    grad_down = scattered(mm(activation, cot, TN), 1)
    grad_gate = scattered(mm(hidden_two, d_gate, TN), 0)
    grad_up = scattered(mm(hidden_two, d_up, TN), 0)
    out_own = (mid + sum_blocks(mlp_part, n)).astype(BF16)
    output = to_natural(all_blocks(out_own, n), me)

    d_attended = mm(d_mid_low, w_out, NT).astype(BF16)
    grad_out = scattered(mm(attended, d_mid_low, TN), 1)
    d_query, d_keys, d_values = attend_back(
        me_array, query, keys, values, low, attended, d_attended, lse, cosine, sine, n
    )
    d_window = jnp.stack([d_keys, d_values])
    d_two_back, d_one_back, d_own = (
        d_window[:, :tokens], d_window[:, tokens : 2 * tokens], d_window[:, 2 * tokens :],
    )
    d_across = swap(d_one_back, 1, "seq").astype(F32)
    sent = (d_two_back.astype(F32) + jnp.where(odd, d_across, 0.0)).astype(BF16)
    d_own = d_own.astype(F32) + jnp.where(odd, 0.0, d_across)
    d_own = d_own + lax.ppermute(sent, "seq", left_two).astype(F32)
    d_key = rotate_wide(d_own[0], cosine, -sine).astype(BF16)
    d_value = d_own[1].astype(BF16)

    d_one_part = (
        mm(d_query, w_query, NT) + mm(d_key, w_key, NT) + mm(d_value, w_value, NT)
    ).astype(BF16)
    d_hidden_one = sum_blocks(d_one_part, n)
    grad_query = scattered(mm(hidden_one, d_query, TN), 0)
    grad_key = scattered(mm(hidden_one, d_key, TN), 0)
    grad_value = scattered(mm(hidden_one, d_value, TN), 0)

    r_one = lax.rsqrt(jnp.mean(input_own * input_own, axis=-1, keepdims=True) + 1e-06)
    n_one = input_own * r_one
    e_one = d_hidden_one * norm_one
    input_grad = d_mid + r_one * (e_one - n_one * jnp.mean(e_one * n_one, axis=-1, keepdims=True))
    others = all_blocks(input_grad.astype(BF16), n)[1:]
    grad_input = to_natural([input_grad] + [b.astype(F32) for b in others], me)
    gains = gain_sums(
        jnp.stack([jnp.sum(d_hidden_one * n_one, 0), jnp.sum(d_hidden_two * n_two, 0)]), n
    )
    return (
        output, grad_input, gains[0], grad_query, grad_key, grad_value, grad_out, gains[1],
        grad_gate, grad_up, grad_down,
    )


def solution(mesh):
    in_specs = (
        P("seq", None), P(), P(None, "tp"), P(None, "tp"), P(None, "tp"), P("tp", None), P(),
        P(None, "tp"), P(None, "tp"), P("tp", None), P("seq"), P("seq", None),
    )
    out_specs = (
        P("seq", None), P("seq", None), P("seq"), P("seq", "tp"), P("seq", "tp"), P("seq", "tp"),
        P("tp", "seq"), P("seq"), P("seq", "tp"), P("seq", "tp"), P("tp", "seq"),
    )
    return jax.shard_map(
        on_device, mesh=mesh, in_specs=in_specs, out_specs=out_specs, check_vma=False
    )
```

time: 1770 us -> 791 us (0.45)
  waiting for transfers between devices: 1230 us -> 350 us
  matrix products: 289 us -> 177 us
  Pallas kernels: 0 us -> 85.6 us
  other arithmetic: 127 us -> 66.5 us
  starting transfers between devices: 12.1 us -> 47.7 us
  blocking collectives: 30.2 us -> 0 us
    psum x4 -> x0, waiting for transfers between devices: 559 us -> none  [the longest x1 193 us: on_device(): mid_rows = input_float + lax.psum(attn_part, 'tp')]
    reduce_scatter x7, waiting for transfers between devices: 511 us -> 0.01 us  [scattered(): lax.psum_scatter(grad.astype(BF16), 'seq', scatter_dimension=dim, tiled=T...]
    ppermute x4 -> x42, waiting for transfers between devices: 165 us -> 350 us  [the longest x38 258 us: swap(): return lax.ppermute(array, axis, [(i, i ^ bit) for i in range(size)])]
    dot_general x26 -> x18, matrix products: 264 us -> 177 us  [mm(): return lax.dot_general(a, b, dims, preferred_element_type=F32)]
    pallas_call x0 -> x3, Pallas kernels: none -> 85.6 us  [the longest x1 48.6 us: attend_back(): pl.pallas_call(lambda *refs: attend_back_kernel(n, *refs), grid_spec=pltp...]
    ppermute x4 -> x42, starting transfers between devices: 10.8 us -> 47.2 us  [the longest x38 35 us: swap(): return lax.ppermute(array, axis, [(i, i ^ bit) for i in range(size)])]
    unnamed x1 -> x0, blocking collectives: 30.2 us -> none
    sub x1 -> x0, matrix products: 24.8 us -> none  [on_device(): expo = jnp.exp(scores - peak)]
  transfers between devices with their start and end apart: 15 -> 49, of which waited for: 13 -> 30; matrix products, arithmetic and copies ran while one was open for 7% -> 22% of each run, Pallas kernels for 0% -> 6%
where the time goes in v1:
time: 791 us; the launch traced here: 786 us
  waiting for transfers between devices  350 us (44%)
  matrix products  177 us (22%)
  Pallas kernels  85.6 us (11%)
  other arithmetic  66.5 us (8%)
  starting transfers between devices  47.7 us (6%)
  local copies, waits for them, and re-layouts  43 us (5%)
  between operations  15.8 us (2%)
    ppermute x38, waiting for transfers between devices, swap(): return lax.ppermute(array, axis, [(i, i ^ bit) for i in range(size)])  258 us
    dot_general x18, matrix products, mm(): return lax.dot_general(a, b, dims, preferred_element_type=F32)  177 us
    pallas_call x1, Pallas kernels, attend_back(): pl.pallas_call(lambda *refs: attend_back_kernel(n, *refs), grid_spec=pltp...  48.6 us
    ppermute x1, waiting for transfers between devices, on_device(): d_own = d_own + lax.ppermute(sent, 'seq', left_two).astype(F32)  46.3 us
    ppermute x1, waiting for transfers between devices, on_device(): before_two = lax.ppermute(packed, 'seq', right_two)  41.1 us
    ppermute x38, starting transfers between devices, swap(): return lax.ppermute(array, axis, [(i, i ^ bit) for i in range(size)])  35 us
    pallas_call x1, Pallas kernels, attend(): pl.pallas_call(lambda *refs: attend_kernel(n, *refs), grid_spec=pltpu.Pre...  26.4 us
  transfers between devices with their start and end apart: 49, of which 30 were waited for; matrix products, arithmetic and copies ran while one was open for 22% of the time, Pallas kernels for 6%

profile of v1, /device:TPU:0, one launch (start us, length us, event | category | flops | bytes accessed | tf_op | source)
XLA Modules:
  0.0 785.5 jit_solution(10876532787972770353)
XLA Ops:
  13.6 10.6 %project.1 = (bf16[1024,2048]{1,0:T(8,128)(2,1)}, bf16[1024,512]{1,0:T(8,128)(2,1)S(1)}, bf16[1024,512]{1,0:T(8,128)(2,1)S(1)}, bf16[1024,512]{1,0:T(8,128)(2,1)S(1)}) custom-call(s32[1]{0:T(128)} %bitcast.me_ref.refs_0_, bf16[1024,2048]{1,0:T(8,128)(2,1)} %x_ref.1, f32[1,2048]{1,0:T(1,128)S(1)} %bitcast.78, bf16[2048,512]{1,0:T(8,128)(2,1)S(1)} %copy-done.16, ...), custom_call_target="tpu_custom_call" | custom-call | flops 6442450944 | bytes 17825792 | tf_op jit(solution)/shard_map/project/pallas_call | solution.py:106
  26.7 6.3 collective-permute-start
  35.7 41.1 %collective-permute-done = bf16[2,1024,512]{2,1,0:T(8,128)(2,1)} collective-permute-done((bf16[2,1024,512]{2,1,0:T(8,128)(2,1)}, bf16[2,1024,512]{2,1,0:T(8,128)(2,1)}, u32[]{:S(2)}, u32[]{:S(2)}) %collective-permute-start) | collective-permute-done | bytes 2097184 | tf_op jit(solution)/shard_map/ppermute | solution.py:377
  78.3 4.8 collective-permute-done.2
  85.0 3.1 maximum_maximum_fusion
  89.3 26.4 %attend.1 = (bf16[1024,512]{1,0:T(8,128)(2,1)S(1)}, f32[4,1,1024]{2,1,0:T(1,128)S(1)}) custom-call(s32[1]{0:T(128)} %bitcast.me_ref.refs_0_, bf16[1024,512]{1,0:T(8,128)(2,1)S(1)} %copy-done.25, bf16[3072,512]{1,0:T(8,128)(2,1)S(1)} %get-tuple-element.47.refs_2_, bf16[3072,512]{1,0:T(8,128)(2,1)S(1)} %get-tuple-element.46.refs_3_, s32[1,1024]{1,0:T(1,128)S(1)} %fusion.26.refs_4_), custom_call_target="tpu_custom_call" | custom-call | flops 9663676416 | bytes 8388608 | tf_op jit(solution)/shard_map/attend/pallas_call | solution.py:198
  121.5 22.0 %collective-permute-done.3 = bf16[512,1024]{1,0:T(8,128)(2,1)S(1)} collective-permute-done((bf16[512,1024]{1,0:T(8,128)(2,1)S(1)}, bf16[512,1024]{1,0:T(8,128)(2,1)S(1)}, u32[]{:S(2)}, u32[]{:S(2)}) %collective-permute-start.3) | collective-permute-done | bytes 1048608 | tf_op jit(solution)/shard_map/ppermute | solution.py:43
  145.3 11.6 %collective-permute-done.4 = bf16[256,1024]{1,0:T(8,128)(2,1)S(1)} collective-permute-done((bf16[256,1024]{1,0:T(8,128)(2,1)S(1)}, bf16[256,1024]{1,0:T(8,128)(2,1)S(1)}, u32[]{:S(2)}, u32[]{:S(2)}) %collective-permute-start.4) | collective-permute-done | bytes 524320 | tf_op jit(solution)/shard_map/ppermute | solution.py:43
  159.0 10.7 %collective-permute-done.6 = bf16[256,1024]{1,0:T(8,128)(2,1)S(1)} collective-permute-done((bf16[256,1024]{1,0:T(8,128)(2,1)S(1)}, bf16[256,1024]{1,0:T(8,128)(2,1)S(1)}, u32[]{:S(2)}, u32[]{:S(2)}) %collective-permute-start.6) | collective-permute-done | bytes 524320 | tf_op jit(solution)/shard_map/ppermute | solution.py:43
  177.8 7.6 collective-permute-done.7
  189.0 9.4 %fusion.20 = f32[1024,1376]{0,1:T(8,128)} fusion(bf16[1376,2048]{1,0:T(8,128)(2,1)S(1)} %bitcast.102, bf16[256,2048]{1,0:T(8,128)(2,1)S(1)} %get-tuple-element.59, bf16[256,2048]{1,0:T(8,128)(2,1)S(1)} %get-tuple-element.60, bf16[256,2048]{1,0:T(8,128)(2,1)S(1)} %get-tuple-element.58, bf16[256,2048]{1,0:T(8,128)(2,1)S(1)} %get-tuple-element.57), kind=kOutput, calls=%fused_computation.102 | convolution fusion | flops 5788139520 | bytes 15466496 | tf_op jit(solution)/shard_map/dot_general | solution.py:23
  198.5 10.6 %collective-permute-done.8 = bf16[512,1024]{1,0:T(8,128)(2,1)S(1)} collective-permute-done((bf16[512,1024]{1,0:T(8,128)(2,1)S(1)}, bf16[512,1024]{1,0:T(8,128)(2,1)S(1)}, u32[]{:S(2)}, u32[]{:S(2)}) %collective-permute-start.8) | collective-permute-done | bytes 1048608 | tf_op jit(solution)/shard_map/ppermute | solution.py:43
  210.4 26.3 %fusion.30 = f32[1024,1376]{0,1:T(8,128)} fusion(bf16[2048,1376]{0,1:T(8,128)(2,1)S(1)} %bitcast.100, bf16[256,1024]{1,0:T(8,128)(2,1)S(1)} %get-tuple-element.92, bf16[256,1024]{1,0:T(8,128)(2,1)S(1)} %get-tuple-element.90, bf16[256,1024]{1,0:T(8,128)(2,1)S(1)} %get-tuple-element.91, bf16[256,1024]{1,0:T(8,128)(2,1)S(1)} %collective-permute-done.7, ...), kind=kOutput, calls=%fused_computation.133 | convolution fusion | flops 5800722432 | bytes 15466496 | tf_op jit(solution)/shard_map/dot_general | solution.py:23
  236.7 19.2 %multiply_convert_fusion = (bf16[1024,1376]{0,1:T(8,128)(2,1)}, bf16[1024,1376]{0,1:T(8,128)(2,1)}, bf16[1024,1376]{0,1:T(8,128)(2,1)}) fusion(f32[1024,1376]{0,1:T(8,128)} %fusion.20, f32[1024,1376]{0,1:T(8,128)} %fusion.30, bf16[2048,1376]{0,1:T(8,128)(2,1)} %param.19, bf16[256,1024]{1,0:T(8,128)(2,1)} %copy-done.55, bf16[256,1024]{1,0:T(8,128)(2,1)} %copy-done.53, ...), kind=kOutput, calls=%fused_computation.10 | convolution fusion | flops 5821857792 | bytes 29556736 | tf_op jit(solution)/shard_map/dot_general | solution.py:23
  255.9 10.0 %fusion.56 = f32[1024,2048]{1,0:T(8,128)S(1)} fusion(bf16[1024,1376]{0,1:T(8,128)(2,1)} %get-tuple-element.44, bf16[2048,1376]{0,1:T(8,128)(2,1)} %param.19), kind=kOutput, calls=%fused_computation.157 | convolution fusion | flops 5771362304 | bytes 16842752 | tf_op jit(solution)/shard_map/dot_general | solution.py:23
  265.9 9.5 %add_convert_fusion.1 = bf16[1024,2048]{1,0:T(8,128)(2,1)S(1)} fusion(f32[1024,2048]{1,0:T(8,128)S(1)} %fusion.56, bf16[1024,1376]{0,1:T(8,128)(2,1)S(1)} %copy-done.65, bf16[2048,1376]{0,1:T(8,128)(2,1)} %param.20), kind=kOutput, calls=%fused_computation.1 | convolution fusion | flops 5775556608 | bytes 21037056 | tf_op jit(solution)/shard_map/dot_general | solution.py:23
  277.7 20.5 %collective-permute-done.19 = bf16[512,1024]{1,0:T(8,128)(2,1)S(1)} collective-permute-done((bf16[512,1024]{1,0:T(8,128)(2,1)S(1)}, bf16[512,1024]{1,0:T(8,128)(2,1)S(1)}, u32[]{:S(2)}, u32[]{:S(2)}) %collective-permute-start.19) | collective-permute-done | bytes 1048608 | tf_op jit(solution)/shard_map/ppermute | solution.py:43
  301.4 9.4 %collective-permute-done.20 = bf16[256,1024]{1,0:T(8,128)(2,1)S(1)} collective-permute-done((bf16[256,1024]{1,0:T(8,128)(2,1)S(1)}, bf16[256,1024]{1,0:T(8,128)(2,1)S(1)}, u32[]{:S(2)}, u32[]{:S(2)}) %collective-permute-start.20) | collective-permute-done | bytes 524320 | tf_op jit(solution)/shard_map/ppermute | solution.py:43
  311.9 10.9 %collective-permute-done.22 = bf16[256,1024]{1,0:T(8,128)(2,1)S(1)} collective-permute-done((bf16[256,1024]{1,0:T(8,128)(2,1)S(1)}, bf16[256,1024]{1,0:T(8,128)(2,1)S(1)}, u32[]{:S(2)}, u32[]{:S(2)}) %collective-permute-start.22) | collective-permute-done | bytes 524320 | tf_op jit(solution)/shard_map/ppermute | solution.py:43
  327.3 10.5 %collective-permute-done.23 = bf16[256,1024]{1,0:T(8,128)(2,1)S(1)} collective-permute-done((bf16[256,1024]{1,0:T(8,128)(2,1)S(1)}, bf16[256,1024]{1,0:T(8,128)(2,1)S(1)}, u32[]{:S(2)}, u32[]{:S(2)}) %collective-permute-start.23) | collective-permute-done | bytes 524320 | tf_op jit(solution)/shard_map/ppermute | solution.py:43
  340.9 19.1 %collective-permute-done.24 = bf16[512,1024]{1,0:T(8,128)(2,1)S(1)} collective-permute-done((bf16[512,1024]{1,0:T(8,128)(2,1)S(1)}, bf16[512,1024]{1,0:T(8,128)(2,1)S(1)}, u32[]{:S(2)}, u32[]{:S(2)}) %collective-permute-start.24) | collective-permute-done | bytes 1048608 | tf_op jit(solution)/shard_map/ppermute | solution.py:43
  361.4 15.0 %convolution_convert_fusion.5 = bf16[512,2048]{1,0:T(8,128)(2,1)} fusion(bf16[1024,512]{1,0:T(8,128)(2,1)S(1)} %get-tuple-element.23.refs_5_, bf16[256,1024]{1,0:T(8,128)(2,1)S(1)} %get-tuple-element.80, bf16[256,1024]{1,0:T(8,128)(2,1)S(1)} %get-tuple-element.78, bf16[256,1024]{1,0:T(8,128)(2,1)S(1)} %get-tuple-element.79, ...), kind=kOutput, calls=%fused_computation.31 | convolution fusion | flops 2177892352 | bytes 7340032 | tf_op jit(solution)/shard_map/dot_general | solution.py:23
  376.6 7.6 convolution_convert_fusion.9.refs_6_
  384.3 48.6 %attend_back.1 = (bf16[1024,512]{1,0:T(8,128)(2,1)S(1)}, bf16[3072,512]{1,0:T(8,128)(2,1)S(1)}, bf16[3072,512]{1,0:T(8,128)(2,1)S(1)}) custom-call(s32[1]{0:T(128)} %bitcast.me_ref.refs_0_, bf16[1024,512]{1,0:T(8,128)(2,1)S(1)} %copy-done.26, bf16[3072,512]{1,0:T(8,128)(2,1)} %copy-done.7, bf16[3072,512]{1,0:T(8,128)(2,1)} %copy-done.6, ...), custom_call_target="tpu_custom_call" | custom-call | flops 24159191040 | bytes 15728640 | tf_op jit(solution)/shard_map/attend_back/pallas_call | solution.py:284
  435.5 3.8 convolution_convert_fusion.8
  439.3 11.0 %convolution_convert_fusion = bf16[2048,1376]{0,1:T(8,128)(2,1)} fusion(bf16[1024,1376]{0,1:T(8,128)(2,1)} %get-tuple-element.43, bf16[256,1024]{1,0:T(8,128)(2,1)} %copy-done.55, bf16[256,1024]{1,0:T(8,128)(2,1)} %copy-done.53, bf16[256,1024]{1,0:T(8,128)(2,1)} %copy-done.54, bf16[256,1024]{1,0:T(8,128)(2,1)} %copy-done.50, ...), kind=kOutput, calls=%fused_computation.2 | convolution fusion | flops 5803540480 | bytes 12648448 | tf_op jit(solution)/shard_map/dot_general | solution.py:23
  450.4 11.2 %convolution_convert_fusion.1 = bf16[2048,1376]{0,1:T(8,128)(2,1)} fusion(bf16[1024,1376]{0,1:T(8,128)(2,1)} %get-tuple-element.44, bf16[256,1024]{1,0:T(8,128)(2,1)} %copy-done.55, bf16[256,1024]{1,0:T(8,128)(2,1)} %copy-done.53, bf16[256,1024]{1,0:T(8,128)(2,1)} %copy-done.54, bf16[256,1024]{1,0:T(8,128)(2,1)} %copy-done.50, ...), kind=kOutput, calls=%fused_computation.3 | convolution fusion | flops 5803540480 | bytes 12648448 | tf_op jit(solution)/shard_map/dot_general | solution.py:23
  461.7 10.3 %convolution_convert_fusion.2 = bf16[1376,2048]{1,0:T(8,128)(2,1)} fusion(bf16[1024,1376]{0,1:T(8,128)(2,1)} %get-tuple-element.45, bf16[256,2048]{1,0:T(8,128)(2,1)} %copy-done.46, bf16[256,2048]{1,0:T(8,128)(2,1)} %copy-done.47, bf16[256,2048]{1,0:T(8,128)(2,1)} %copy-done.45, bf16[256,2048]{1,0:T(8,128)(2,1)} %copy-done.33), kind=kOutput, calls=%fused_computation.4 | convolution fusion | flops 5790957568 | bytes 12648448 | tf_op jit(solution)/shard_map/dot_general | solution.py:23
  472.1 9.7 %convolution_convert_fusion.3 = bf16[1024,2048]{1,0:T(8,128)(2,1)S(1)} fusion(bf16[1024,1376]{0,1:T(8,128)(2,1)} %get-tuple-element.45, bf16[1376,2048]{1,0:T(8,128)(2,1)} %param.21), kind=kOutput, calls=%fused_computation.24 | convolution fusion | flops 5773459456 | bytes 12648448 | tf_op jit(solution)/shard_map/dot_general | solution.py:23
  485.3 17.8 %collective-permute-done.11 = bf16[512,1024]{1,0:T(8,128)(2,1)S(1)} collective-permute-done((bf16[512,1024]{1,0:T(8,128)(2,1)S(1)}, bf16[512,1024]{1,0:T(8,128)(2,1)S(1)}, u32[]{:S(2)}, u32[]{:S(2)}) %collective-permute-start.11) | collective-permute-done | bytes 1048608 | tf_op jit(solution)/shard_map/ppermute | solution.py:43
  504.9 5.6 collective-permute-done.13
  510.6 10.8 %collective-permute-done.12 = bf16[256,1024]{1,0:T(8,128)(2,1)S(1)} collective-permute-done((bf16[256,1024]{1,0:T(8,128)(2,1)S(1)}, bf16[256,1024]{1,0:T(8,128)(2,1)S(1)}, u32[]{:S(2)}, u32[]{:S(2)}) %collective-permute-start.12) | collective-permute-done | bytes 524320 | tf_op jit(solution)/shard_map/ppermute | solution.py:43
  524.4 11.2 %collective-permute-done.14 = bf16[256,1024]{1,0:T(8,128)(2,1)S(1)} collective-permute-done((bf16[256,1024]{1,0:T(8,128)(2,1)S(1)}, bf16[256,1024]{1,0:T(8,128)(2,1)S(1)}, u32[]{:S(2)}, u32[]{:S(2)}) %collective-permute-start.14) | collective-permute-done | bytes 524320 | tf_op jit(solution)/shard_map/ppermute | solution.py:43
  541.6 11.8 %collective-permute-done.15 = bf16[256,1024]{1,0:T(8,128)(2,1)S(1)} collective-permute-done((bf16[256,1024]{1,0:T(8,128)(2,1)S(1)}, bf16[256,1024]{1,0:T(8,128)(2,1)S(1)}, u32[]{:S(2)}, u32[]{:S(2)}) %collective-permute-start.15) | collective-permute-done | bytes 524320 | tf_op jit(solution)/shard_map/ppermute | solution.py:43
  555.1 5.8 fusion.57
  560.9 46.3 %collective-permute-done.28 = bf16[2,1024,512]{2,1,0:T(8,128)(2,1)S(1)} collective-permute-done((bf16[2,1024,512]{2,1,0:T(8,128)(2,1)S(1)}, bf16[2,1024,512]{2,1,0:T(8,128)(2,1)S(1)}, u32[]{:S(2)}, u32[]{:S(2)}) %collective-permute-start.28) | collective-permute-done | bytes 2097184 | tf_op jit(solution)/shard_map/ppermute | solution.py:427
  610.0 3.2 slice.394
  621.9 5.7 fusion.58
  627.6 3.8 convolution_convert_fusion.7
  631.8 10.9 %add_convert_fusion = bf16[1024,2048]{1,0:T(8,128)(2,1)} fusion(f32[1024,2048]{1,0:T(8,128)} %fusion.57, f32[1024,2048]{1,0:T(8,128)} %fusion.58, bf16[2048,512]{1,0:T(8,128)(2,1)S(1)} %copy-done.9, f32[2,1024,512]{2,1,0:T(8,128)} %fusion.2), kind=kOutput, calls=%fused_computation | convolution fusion | flops 2153775104 | bytes 24117248 | tf_op jit(solution)/shard_map/dot_general | solution.py:23
  652.4 16.5 %collective-permute-done.29 = bf16[512,1024]{1,0:T(8,128)(2,1)} collective-permute-done((bf16[512,1024]{1,0:T(8,128)(2,1)S(1)}, bf16[512,1024]{1,0:T(8,128)(2,1)}, u32[]{:S(2)}, u32[]{:S(2)}) %collective-permute-start.29) | collective-permute-done | bytes 1048608 | tf_op jit(solution)/shard_map/ppermute | solution.py:43
  675.9 19.6 %collective-permute-done.31 = bf16[512,1024]{1,0:T(8,128)(2,1)S(1)} collective-permute-done((bf16[512,1024]{1,0:T(8,128)(2,1)S(1)}, bf16[512,1024]{1,0:T(8,128)(2,1)S(1)}, u32[]{:S(2)}, u32[]{:S(2)}) %collective-permute-start.31) | collective-permute-done | bytes 1048608 | tf_op jit(solution)/shard_map/ppermute | solution.py:43
  695.5 9.6 %collective-permute-done.30 = bf16[256,1024]{1,0:T(8,128)(2,1)S(1)} collective-permute-done((bf16[256,1024]{1,0:T(8,128)(2,1)S(1)}, bf16[256,1024]{1,0:T(8,128)(2,1)S(1)}, u32[]{:S(2)}, u32[]{:S(2)}) %collective-permute-start.30) | collective-permute-done | bytes 524320 | tf_op jit(solution)/shard_map/ppermute | solution.py:43
  708.2 5.6 convolution_convert_fusion.6
  713.8 6.4 collective-permute-done.32
  723.8 3.5 collective-permute-done.37
  749.8 4.5 broadcast_in_dim.17
  763.3 3.5 collective-permute-done.36
  (337 shorter events, 150.8 us)
Async XLA Ops:
  7.2 731.7 %reduce-scatter.14.cloned.1.call-start = ((), (), s32[]{:S(2)}) async-start(), calls=%async_computation.10 | async-start | bytes 2359296 | tf_op jit(solution)/shard_map/reduce_scatter | solution.py:343
  26.7 50.1 %collective-permute-start = (bf16[2,1024,512]{2,1,0:T(8,128)(2,1)}, bf16[2,1024,512]{2,1,0:T(8,128)(2,1)}, u32[]{:S(2)}, u32[]{:S(2)}) collective-permute-start(bf16[2,1024,512]{2,1,0:T(8,128)(2,1)} %pad_maximum_fusion.2), channel_id=1, source_target_pairs={{0,8},{4,12},{8,16},{12,20},{16,24},{20,28},{1,9},{5,13},{9,17},{1... | collective-permute-start | bytes 6291464 | tf_op jit(solution)/shard_map/ppermute | solution.py:377
  32.9 45.4 %collective-permute-start.1 = (bf16[2,1024,512]{2,1,0:T(8,128)(2,1)}, bf16[2,1024,512]{2,1,0:T(8,128)(2,1)}, u32[]{:S(2)}, u32[]{:S(2)}) collective-permute-start(bf16[2,1024,512]{2,1,0:T(8,128)(2,1)} %pad_maximum_fusion.2), channel_id=1, source_target_pairs={{0,4},{8,12},{16,20},{24,28},{1,5},{9,13},{17,21},{25,29},{2,6},{1... | collective-permute-start | bytes 6291464 | tf_op jit(solution)/shard_map/ppermute | solution.py:378
  76.8 6.4 collective-permute-start.2
  118.3 25.3 %collective-permute-start.3 = (bf16[512,1024]{1,0:T(8,128)(2,1)S(1)}, bf16[512,1024]{1,0:T(8,128)(2,1)S(1)}, u32[]{:S(2)}, u32[]{:S(2)}) collective-permute-start(bf16[512,1024]{1,0:T(8,128)(2,1)S(1)} %pad_maximum_fusion.6), channel_id=1, source_target_pairs={{0,1},{1,0},{2,3},{3,2},{4,5},{5,4},{6,7},{7,6},{8,9},{9,8},{10,11... | collective-permute-start | bytes 3145736 | tf_op jit(solution)/shard_map/ppermute | solution.py:43
  119.9 25.4 %collective-permute-start.5 = (bf16[512,1024]{1,0:T(8,128)(2,1)S(1)}, bf16[512,1024]{1,0:T(8,128)(2,1)S(1)}, u32[]{:S(2)}, u32[]{:S(2)}) collective-permute-start(bf16[512,1024]{1,0:T(8,128)(2,1)S(1)} %concatenate.223), channel_id=1, source_target_pairs={{0,2},{1,3},{2,0},{3,1},{4,6},{5,7},{6,4},{7,5},{8,10},{9,11},{10,... | collective-permute-start | bytes 3145736 | tf_op jit(solution)/shard_map/ppermute | solution.py:43
  143.7 13.2 %collective-permute-start.4 = (bf16[256,1024]{1,0:T(8,128)(2,1)S(1)}, bf16[256,1024]{1,0:T(8,128)(2,1)S(1)}, u32[]{:S(2)}, u32[]{:S(2)}) collective-permute-start(bf16[256,1024]{1,0:T(8,128)(2,1)S(1)} %add_convert_fusion.9), channel_id=1, source_target_pairs={{0,2},{1,3},{2,0},{3,1},{4,6},{5,7},{6,4},{7,5},{8,10},{9,11},{10,... | collective-permute-start | bytes 1572872 | tf_op jit(solution)/shard_map/ppermute | solution.py:43
  157.4 12.3 %collective-permute-start.6 = (bf16[256,1024]{1,0:T(8,128)(2,1)S(1)}, bf16[256,1024]{1,0:T(8,128)(2,1)S(1)}, u32[]{:S(2)}, u32[]{:S(2)}) collective-permute-start(bf16[256,1024]{1,0:T(8,128)(2,1)S(1)} %get-tuple-element.66), channel_id=1, source_target_pairs={{0,1},{1,0},{2,3},{3,2},{4,5},{5,4},{6,7},{7,6},{8,9},{9,8},{10,11... | collective-permute-start | bytes 1572872 | tf_op jit(solution)/shard_map/ppermute | solution.py:43
  174.1 11.4 %collective-permute-start.7 = (bf16[256,1024]{1,0:T(8,128)(2,1)S(1)}, bf16[256,1024]{1,0:T(8,128)(2,1)S(1)}, u32[]{:S(2)}, u32[]{:S(2)}) collective-permute-start(bf16[256,1024]{1,0:T(8,128)(2,1)S(1)} %get-tuple-element.93), channel_id=1, source_target_pairs={{0,2},{1,3},{2,0},{3,1},{4,6},{5,7},{6,4},{7,5},{8,10},{9,11},{10,... | collective-permute-start | bytes 1572872 | tf_op jit(solution)/shard_map/ppermute | solution.py:43
  175.7 12.9 %collective-permute-start.9 = (bf16[256,1024]{1,0:T(8,128)(2,1)S(1)}, bf16[256,1024]{1,0:T(8,128)(2,1)S(1)}, u32[]{:S(2)}, u32[]{:S(2)}) collective-permute-start(bf16[256,1024]{1,0:T(8,128)(2,1)S(1)} %get-tuple-element.94), channel_id=1, source_target_pairs={{0,1},{1,0},{2,3},{3,2},{4,5},{5,4},{6,7},{7,6},{8,9},{9,8},{10,11... | collective-permute-start | bytes 1572872 | tf_op jit(solution)/shard_map/ppermute | solution.py:43
  185.5 23.6 %collective-permute-start.8 = (bf16[512,1024]{1,0:T(8,128)(2,1)S(1)}, bf16[512,1024]{1,0:T(8,128)(2,1)S(1)}, u32[]{:S(2)}, u32[]{:S(2)}) collective-permute-start(bf16[512,1024]{1,0:T(8,128)(2,1)S(1)} %pad_maximum_fusion.7), channel_id=1, source_target_pairs={{0,1},{1,0},{2,3},{3,2},{4,5},{5,4},{6,7},{7,6},{8,9},{9,8},{10,11... | collective-permute-start | bytes 3145736 | tf_op jit(solution)/shard_map/ppermute | solution.py:43
  188.6 20.6 %collective-permute-start.10 = (bf16[512,1024]{1,0:T(8,128)(2,1)S(1)}, bf16[512,1024]{1,0:T(8,128)(2,1)S(1)}, u32[]{:S(2)}, u32[]{:S(2)}) collective-permute-start(bf16[512,1024]{1,0:T(8,128)(2,1)S(1)} %pad_maximum_fusion.8), channel_id=1, source_target_pairs={{0,2},{1,3},{2,0},{3,1},{4,6},{5,7},{6,4},{7,5},{8,10},{9,11},{10,... | collective-permute-start | bytes 3145736 | tf_op jit(solution)/shard_map/ppermute | solution.py:43
  275.5 22.7 %collective-permute-start.19 = (bf16[512,1024]{1,0:T(8,128)(2,1)S(1)}, bf16[512,1024]{1,0:T(8,128)(2,1)S(1)}, u32[]{:S(2)}, u32[]{:S(2)}) collective-permute-start(bf16[512,1024]{1,0:T(8,128)(2,1)S(1)} %pad_maximum_fusion.12), channel_id=1, source_target_pairs={{0,1},{1,0},{2,3},{3,2},{4,5},{5,4},{6,7},{7,6},{8,9},{9,8},{10,11... | collective-permute-start | bytes 3145736 | tf_op jit(solution)/shard_map/ppermute | solution.py:43
  277.2 24.2 %collective-permute-start.21 = (bf16[512,1024]{1,0:T(8,128)(2,1)S(1)}, bf16[512,1024]{1,0:T(8,128)(2,1)S(1)}, u32[]{:S(2)}, u32[]{:S(2)}) collective-permute-start(bf16[512,1024]{1,0:T(8,128)(2,1)S(1)} %concatenate.225), channel_id=1, source_target_pairs={{0,2},{1,3},{2,0},{3,1},{4,6},{5,7},{6,4},{7,5},{8,10},{9,11},{10,... | collective-permute-start | bytes 3145736 | tf_op jit(solution)/shard_map/ppermute | solution.py:43
  298.4 12.4 %collective-permute-start.20 = (bf16[256,1024]{1,0:T(8,128)(2,1)S(1)}, bf16[256,1024]{1,0:T(8,128)(2,1)S(1)}, u32[]{:S(2)}, u32[]{:S(2)}) collective-permute-start(bf16[256,1024]{1,0:T(8,128)(2,1)S(1)} %add_convert_fusion.5), channel_id=1, source_target_pairs={{0,2},{1,3},{2,0},{3,1},{4,6},{5,7},{6,4},{7,5},{8,10},{9,11},{10,... | collective-permute-start | bytes 1572872 | tf_op jit(solution)/shard_map/ppermute | solution.py:43
  311.3 11.5 %collective-permute-start.22 = (bf16[256,1024]{1,0:T(8,128)(2,1)S(1)}, bf16[256,1024]{1,0:T(8,128)(2,1)S(1)}, u32[]{:S(2)}, u32[]{:S(2)}) collective-permute-start(bf16[256,1024]{1,0:T(8,128)(2,1)S(1)} %get-tuple-element.54), channel_id=1, source_target_pairs={{0,1},{1,0},{2,3},{3,2},{4,5},{5,4},{6,7},{7,6},{8,9},{9,8},{10,11... | collective-permute-start | bytes 1572872 | tf_op jit(solution)/shard_map/ppermute | solution.py:43
  326.4 11.4 %collective-permute-start.23 = (bf16[256,1024]{1,0:T(8,128)(2,1)S(1)}, bf16[256,1024]{1,0:T(8,128)(2,1)S(1)}, u32[]{:S(2)}, u32[]{:S(2)}) collective-permute-start(bf16[256,1024]{1,0:T(8,128)(2,1)S(1)} %get-tuple-element.81), channel_id=1, source_target_pairs={{0,2},{1,3},{2,0},{3,1},{4,6},{5,7},{6,4},{7,5},{8,10},{9,11},{10,... | collective-permute-start | bytes 1572872 | tf_op jit(solution)/shard_map/ppermute | solution.py:43
  327.0 12.5 %collective-permute-start.25 = (bf16[256,1024]{1,0:T(8,128)(2,1)S(1)}, bf16[256,1024]{1,0:T(8,128)(2,1)S(1)}, u32[]{:S(2)}, u32[]{:S(2)}) collective-permute-start(bf16[256,1024]{1,0:T(8,128)(2,1)S(1)} %get-tuple-element.82), channel_id=1, source_target_pairs={{0,1},{1,0},{2,3},{3,2},{4,5},{5,4},{6,7},{7,6},{8,9},{9,8},{10,11... | collective-permute-start | bytes 1572872 | tf_op jit(solution)/shard_map/ppermute | solution.py:43
  337.9 22.1 %collective-permute-start.24 = (bf16[512,1024]{1,0:T(8,128)(2,1)S(1)}, bf16[512,1024]{1,0:T(8,128)(2,1)S(1)}, u32[]{:S(2)}, u32[]{:S(2)}) collective-permute-start(bf16[512,1024]{1,0:T(8,128)(2,1)S(1)} %pad_maximum_fusion.13), channel_id=1, source_target_pairs={{0,1},{1,0},{2,3},{3,2},{4,5},{5,4},{6,7},{7,6},{8,9},{9,8},{10,11... | collective-permute-start | bytes 3145736 | tf_op jit(solution)/shard_map/ppermute | solution.py:43
  339.6 20.5 %collective-permute-start.26 = (bf16[512,1024]{1,0:T(8,128)(2,1)S(1)}, bf16[512,1024]{1,0:T(8,128)(2,1)S(1)}, u32[]{:S(2)}, u32[]{:S(2)}) collective-permute-start(bf16[512,1024]{1,0:T(8,128)(2,1)S(1)} %pad_maximum_fusion.14), channel_id=1, source_target_pairs={{0,2},{1,3},{2,0},{3,1},{4,6},{5,7},{6,4},{7,5},{8,10},{9,11},{10,... | collective-permute-start | bytes 3145736 | tf_op jit(solution)/shard_map/ppermute | solution.py:43
  376.5 364.2 %reduce-scatter.8.cloned.1.call-start = ((), (), s32[]{:S(2)}) async-start(), calls=%async_computation.7 | async-start | bytes 2359296 | tf_op jit(solution)/shard_map/reduce_scatter | solution.py:343
  439.3 317.0 %reduce-scatter.18.cloned.1.call-start = ((), (), s32[]{:S(2)}) async-start(), calls=%async_computation.12 | async-start | bytes 6340608 | tf_op jit(solution)/shard_map/reduce_scatter | solution.py:343
  450.3 308.3 %reduce-scatter.16.cloned.1.call-start = ((), (), s32[]{:S(2)}) async-start(), calls=%async_computation.11 | async-start | bytes 6340608 | tf_op jit(solution)/shard_map/reduce_scatter | solution.py:343
  461.6 299.4 %reduce-scatter.20.cloned.1.call-start = ((), (), s32[]{:S(2)}) async-start(), calls=%async_computation.13 | async-start | bytes 6340608 | tf_op jit(solution)/shard_map/reduce_scatter | solution.py:343
  472.0 302.6 %reduce-scatter.10.cloned.1.call-start = ((), (), s32[]{:S(2)}) async-start(), calls=%async_computation.8 | async-start | bytes 2359296 | tf_op jit(solution)/shard_map/reduce_scatter | solution.py:343
  482.0 21.1 %collective-permute-start.11 = (bf16[512,1024]{1,0:T(8,128)(2,1)S(1)}, bf16[512,1024]{1,0:T(8,128)(2,1)S(1)}, u32[]{:S(2)}, u32[]{:S(2)}) collective-permute-start(bf16[512,1024]{1,0:T(8,128)(2,1)S(1)} %pad_maximum_fusion.9), channel_id=1, source_target_pairs={{0,1},{1,0},{2,3},{3,2},{4,5},{5,4},{6,7},{7,6},{8,9},{9,8},{10,11... | collective-permute-start | bytes 3145736 | tf_op jit(solution)/shard_map/ppermute | solution.py:43
  484.4 37.6 %collective-permute-start.27 = (bf16[2,1024,512]{2,1,0:T(8,128)(2,1)S(1)}, bf16[2,1024,512]{2,1,0:T(8,128)(2,1)S(1)}, u32[]{:S(2)}, u32[]{:S(2)}) collective-permute-start(bf16[2,1024,512]{2,1,0:T(8,128)(2,1)S(1)} %fusion.14), channel_id=1, source_target_pairs={{0,4},{4,0},{8,12},{12,8},{16,20},{20,16},{24,28},{28,24},{1,5},{5... | collective-permute-start | bytes 6291464 | tf_op jit(solution)/shard_map/ppermute | solution.py:43
  484.5 26.0 %collective-permute-start.13 = (bf16[512,1024]{1,0:T(8,128)(2,1)S(1)}, bf16[512,1024]{1,0:T(8,128)(2,1)S(1)}, u32[]{:S(2)}, u32[]{:S(2)}) collective-permute-start(bf16[512,1024]{1,0:T(8,128)(2,1)S(1)} %concatenate.224), channel_id=1, source_target_pairs={{0,2},{1,3},{2,0},{3,1},{4,6},{5,7},{6,4},{7,5},{8,10},{9,11},{10,... | collective-permute-start | bytes 3145736 | tf_op jit(solution)/shard_map/ppermute | solution.py:43
  503.3 18.1 %collective-permute-start.12 = (bf16[256,1024]{1,0:T(8,128)(2,1)S(1)}, bf16[256,1024]{1,0:T(8,128)(2,1)S(1)}, u32[]{:S(2)}, u32[]{:S(2)}) collective-permute-start(bf16[256,1024]{1,0:T(8,128)(2,1)S(1)} %add_convert_fusion.7), channel_id=1, source_target_pairs={{0,2},{1,3},{2,0},{3,1},{4,6},{5,7},{6,4},{7,5},{8,10},{9,11},{10,... | collective-permute-start | bytes 1572872 | tf_op jit(solution)/shard_map/ppermute | solution.py:43
  521.9 13.7 %collective-permute-start.14 = (bf16[256,1024]{1,0:T(8,128)(2,1)S(1)}, bf16[256,1024]{1,0:T(8,128)(2,1)S(1)}, u32[]{:S(2)}, u32[]{:S(2)}) collective-permute-start(bf16[256,1024]{1,0:T(8,128)(2,1)S(1)} %get-tuple-element.62), channel_id=1, source_target_pairs={{0,1},{1,0},{2,3},{3,2},{4,5},{5,4},{6,7},{7,6},{8,9},{9,8},{10,11... | collective-permute-start | bytes 1572872 | tf_op jit(solution)/shard_map/ppermute | solution.py:43
  522.7 84.5 %collective-permute-start.28 = (bf16[2,1024,512]{2,1,0:T(8,128)(2,1)S(1)}, bf16[2,1024,512]{2,1,0:T(8,128)(2,1)S(1)}, u32[]{:S(2)}, u32[]{:S(2)}) collective-permute-start(bf16[2,1024,512]{2,1,0:T(8,128)(2,1)S(1)} %fusion.4), channel_id=1, source_target_pairs={{8,0},{12,4},{16,8},{20,12},{24,16},{28,20},{9,1},{13,5},{17,9},{2... | collective-permute-start | bytes 6291464 | tf_op jit(solution)/shard_map/ppermute | solution.py:427
  540.5 12.9 %collective-permute-start.15 = (bf16[256,1024]{1,0:T(8,128)(2,1)S(1)}, bf16[256,1024]{1,0:T(8,128)(2,1)S(1)}, u32[]{:S(2)}, u32[]{:S(2)}) collective-permute-start(bf16[256,1024]{1,0:T(8,128)(2,1)S(1)} %get-tuple-element.87), channel_id=1, source_target_pairs={{0,2},{1,3},{2,0},{3,1},{4,6},{5,7},{6,4},{7,5},{8,10},{9,11},{10,... | collective-permute-start | bytes 1572872 | tf_op jit(solution)/shard_map/ppermute | solution.py:43
  541.2 104.3 %collective-permute-start.17 = (bf16[256,1024]{1,0:T(8,128)(2,1)}, bf16[256,1024]{1,0:T(8,128)(2,1)}, u32[]{:S(2)}, u32[]{:S(2)}) collective-permute-start(bf16[256,1024]{1,0:T(8,128)(2,1)} %get-tuple-element.88), channel_id=1, source_target_pairs={{0,1},{1,0},{2,3},{3,2},{4,5},{5,4},{6,7},{7,6},{8,9},{9,8},{10,11... | collective-permute-start | bytes 1572872 | tf_op jit(solution)/shard_map/ppermute | solution.py:43
  554.5 95.9 %collective-permute-start.16 = (bf16[512,1024]{1,0:T(8,128)(2,1)}, bf16[512,1024]{1,0:T(8,128)(2,1)}, u32[]{:S(2)}, u32[]{:S(2)}) collective-permute-start(bf16[512,1024]{1,0:T(8,128)(2,1)} %pad_maximum_fusion.10), channel_id=1, source_target_pairs={{0,1},{1,0},{2,3},{3,2},{4,5},{5,4},{6,7},{7,6},{8,9},{9,8},{10,11... | collective-permute-start | bytes 3145736 | tf_op jit(solution)/shard_map/ppermute | solution.py:43
  631.4 145.0 %reduce-scatter.12.cloned.1.call-start = ((), (), s32[]{:S(2)}) async-start(), calls=%async_computation.9 | async-start | bytes 2359296 | tf_op jit(solution)/shard_map/reduce_scatter | solution.py:343
  644.0 24.9 %collective-permute-start.29 = (bf16[512,1024]{1,0:T(8,128)(2,1)S(1)}, bf16[512,1024]{1,0:T(8,128)(2,1)}, u32[]{:S(2)}, u32[]{:S(2)}) collective-permute-start(bf16[512,1024]{1,0:T(8,128)(2,1)S(1)} %pad_maximum_fusion.15), channel_id=1, source_target_pairs={{0,1},{1,0},{2,3},{3,2},{4,5},{5,4},{6,7},{7,6},{8,9},{9,8},{10,11... | collective-permute-start | bytes 3145736 | tf_op jit(solution)/shard_map/ppermute | solution.py:43
  646.9 27.1 %collective-permute-start.18 = (bf16[512,1024]{1,0:T(8,128)(2,1)S(1)}, bf16[512,1024]{1,0:T(8,128)(2,1)S(1)}, u32[]{:S(2)}, u32[]{:S(2)}) collective-permute-start(bf16[512,1024]{1,0:T(8,128)(2,1)S(1)} %pad_maximum_fusion.11), channel_id=1, source_target_pairs={{0,2},{1,3},{2,0},{3,1},{4,6},{5,7},{6,4},{7,5},{8,10},{9,11},{10,... | collective-permute-start | bytes 3145736 | tf_op jit(solution)/shard_map/ppermute | solution.py:43
  649.8 45.8 %collective-permute-start.31 = (bf16[512,1024]{1,0:T(8,128)(2,1)S(1)}, bf16[512,1024]{1,0:T(8,128)(2,1)S(1)}, u32[]{:S(2)}, u32[]{:S(2)}) collective-permute-start(bf16[512,1024]{1,0:T(8,128)(2,1)S(1)} %concatenate.226), channel_id=1, source_target_pairs={{0,2},{1,3},{2,0},{3,1},{4,6},{5,7},{6,4},{7,5},{8,10},{9,11},{10,... | collective-permute-start | bytes 3145736 | tf_op jit(solution)/shard_map/ppermute | solution.py:43
  670.3 34.8 %collective-permute-start.30 = (bf16[256,1024]{1,0:T(8,128)(2,1)S(1)}, bf16[256,1024]{1,0:T(8,128)(2,1)S(1)}, u32[]{:S(2)}, u32[]{:S(2)}) collective-permute-start(bf16[256,1024]{1,0:T(8,128)(2,1)S(1)} %add_convert_fusion.3), channel_id=1, source_target_pairs={{0,2},{1,3},{2,0},{3,1},{4,6},{5,7},{6,4},{7,5},{8,10},{9,11},{10,... | collective-permute-start | bytes 1572872 | tf_op jit(solution)/shard_map/ppermute | solution.py:43
  707.7 12.5 %collective-permute-start.32 = (bf16[256,1024]{1,0:T(8,128)(2,1)}, bf16[256,1024]{1,0:T(8,128)(2,1)S(1)}, u32[]{:S(2)}, u32[]{:S(2)}) collective-permute-start(bf16[256,1024]{1,0:T(8,128)(2,1)} %get-tuple-element.50), channel_id=1, source_target_pairs={{0,1},{1,0},{2,3},{3,2},{4,5},{5,4},{6,7},{7,6},{8,9},{9,8},{10,11... | collective-permute-start | bytes 1572872 | tf_op jit(solution)/shard_map/ppermute | solution.py:43
  727.3 4.4 collective-permute-start.38
  731.8 4.7 collective-permute-start.39
  733.7 10.0 %collective-permute-start.35 = (bf16[256,1024]{1,0:T(8,128)(2,1)}, bf16[256,1024]{1,0:T(8,128)(2,1)S(1)}, u32[]{:S(2)}, u32[]{:S(2)}) collective-permute-start(bf16[256,1024]{1,0:T(8,128)(2,1)} %get-tuple-element.76), channel_id=1, source_target_pairs={{0,1},{1,0},{2,3},{3,2},{4,5},{5,4},{6,7},{7,6},{8,9},{9,8},{10,11... | collective-permute-start | bytes 1572872 | tf_op jit(solution)/shard_map/ppermute | solution.py:43
  734.8 11.8 %collective-permute-start.33 = (bf16[256,1024]{1,0:T(8,128)(2,1)}, bf16[256,1024]{1,0:T(8,128)(2,1)S(1)}, u32[]{:S(2)}, u32[]{:S(2)}) collective-permute-start(bf16[256,1024]{1,0:T(8,128)(2,1)} %get-tuple-element.75), channel_id=1, source_target_pairs={{0,2},{1,3},{2,0},{3,1},{4,6},{5,7},{6,4},{7,5},{8,10},{9,11},{10,... | collective-permute-start | bytes 1572872 | tf_op jit(solution)/shard_map/ppermute | solution.py:43
  736.4 6.1 collective-permute-start.40
  746.0 20.9 %collective-permute-start.36 = (bf16[512,1024]{1,0:T(8,128)(2,1)}, bf16[512,1024]{1,0:T(8,128)(2,1)}, u32[]{:S(2)}, u32[]{:S(2)}) collective-permute-start(bf16[512,1024]{1,0:T(8,128)(2,1)} %pad_maximum_fusion.17), channel_id=1, source_target_pairs={{0,2},{1,3},{2,0},{3,1},{4,6},{5,7},{6,4},{7,5},{8,10},{9,11},{10,... | collective-permute-start | bytes 3145736 | tf_op jit(solution)/shard_map/ppermute | solution.py:43
  748.8 19.8 %collective-permute-start.34 = (bf16[512,1024]{1,0:T(8,128)(2,1)}, bf16[512,1024]{1,0:T(8,128)(2,1)}, u32[]{:S(2)}, u32[]{:S(2)}) collective-permute-start(bf16[512,1024]{1,0:T(8,128)(2,1)} %pad_maximum_fusion.16), channel_id=1, source_target_pairs={{0,1},{1,0},{2,3},{3,2},{4,5},{5,4},{6,7},{7,6},{8,9},{9,8},{10,11... | collective-permute-start | bytes 3145736 | tf_op jit(solution)/shard_map/ppermute | solution.py:43
  749.8 5.9 collective-permute-start.41
  (74 other events, 1250.3 us)
Sparse Core Ops, SparseCore 0:
  376.6 36.5 reduce-scatter.13
  439.4 36.6 reduce-scatter.7
  478.4 71.4 reduce-scatter.17
  552.3 86.4 reduce-scatter.15
  641.0 61.7 reduce-scatter.19
  705.1 33.9 reduce-scatter.9
  741.5 34.3 reduce-scatter.11

commit v2 on v1

v2 whole, which is shorter than its diff:
```python
import jax
import jax.numpy as jnp
from jax import lax
from jax.experimental import pallas as pl
from jax.experimental.pallas import tpu as pltpu
from jax.sharding import PartitionSpec as P

HEAD = 128
WINDOW = 2048
LOG2E = 1.4426950408889634
SCALE = HEAD ** (-0.5)
NEG = -1e30
F32 = jnp.float32
BF16 = jnp.bfloat16
MIB = 1024 * 1024
GROUPS = 2

NN = (((1,), (0,)), ((), ()))
NT = (((1,), (1,)), ((), ()))
TN = (((0,), (0,)), ((), ()))


def mm(a, b, dims=NN):
    return lax.dot_general(a, b, dims, preferred_element_type=F32)


def tied(values, after):
    return lax.optimization_barrier((values, after))[0]


def call(body, grid, in_specs, out_specs, outs, args, name, scratch=(), flops=0, moved=0, exps=0, vmem=48):
    return pl.pallas_call(
        body,
        grid_spec=pltpu.PrefetchScalarGridSpec(
            num_scalar_prefetch=1,
            grid=grid,
            in_specs=in_specs,
            out_specs=out_specs,
            scratch_shapes=list(scratch),
        ),
        out_shape=[jax.ShapeDtypeStruct(shape, kind) for shape, kind in outs],
        compiler_params=pltpu.CompilerParams(vmem_limit_bytes=vmem * MIB),
        cost_estimate=pl.CostEstimate(flops=0, bytes_accessed=0, transcendentals=0),
        name=name,
    )(*args)


def fixed(shape):
    return pl.BlockSpec(shape, lambda *_: (0,) * len(shape), pipeline_mode=pl.Buffered(1))


def to_relative(array, me, n):
    rows = array.shape[0] // n
    return jnp.concatenate(
        [lax.dynamic_slice_in_dim(array, (r ^ me) * rows, rows, 0) for r in range(n)], axis=0
    )


def swap(array, bit, axis="tp"):
    size = lax.axis_size(axis)
    return lax.ppermute(array, axis, [(i, i ^ bit) for i in range(size)])


def bits_of(n):
    return [1 << b for b in range(n.bit_length() - 1)]


def sum_first(parts, n):
    cut = lambda r, side: parts[2 * r + side]
    if n == 4:
        three_left, three_right = swap(cut(3, 0), 1), swap(cut(3, 1), 2)
        one_left, two_right = swap(cut(1, 0), 1), swap(cut(2, 1), 2)
        one_right = (cut(1, 1).astype(F32) + three_right.astype(F32)).astype(BF16)
        two_left = (cut(2, 0).astype(F32) + three_left.astype(F32)).astype(BF16)
        return (one_right, two_left), ([cut(0, 0), one_left], [cut(0, 1), two_right])
    sides = []
    rows = parts[0].shape[0]
    for side, order in enumerate((bits_of(n), bits_of(n)[::-1])):
        held = {r: cut(r, side) for r in range(n)}
        for bit in order:
            sent = [r for r in held if r & bit]
            got = swap(jnp.concatenate([held[r] for r in sent]).astype(BF16), bit)
            held = {
                r ^ bit: held[r ^ bit].astype(F32) + got[k * rows : (k + 1) * rows].astype(F32)
                for k, r in enumerate(sent)
            }
        sides.append(held[0])
    return tuple(sides), ([], [])


def sum_second(sent, kept, n):
    if n == 4:
        one_right, two_left = swap(sent[0], 1), swap(sent[1], 2)
        return kept[0] + [two_left], kept[1] + [one_right]
    return [sent[0]], [sent[1]]


def all_blocks(own, n):
    left, right = own
    if n == 4:
        one_right, two_left = swap(right, 1), swap(left, 2)
        one_left, two_right = swap(left, 1), swap(right, 2)
        three_left, three_right = swap(two_left, 1), swap(one_right, 2)
        return [left, one_left, two_left, three_left], [right, one_right, two_right, three_right]
    sides = []
    rows = left.shape[0]
    for side, order in enumerate((bits_of(n)[::-1], bits_of(n))):
        held = {0: own[side]}
        for bit in order:
            have = sorted(held)
            got = swap(jnp.concatenate([held[r] for r in have]), bit)
            for k, r in enumerate(have):
                held[r ^ bit] = got[k * rows : (k + 1) * rows]
        sides.append([held[r] for r in range(n)])
    return sides[0], sides[1]


def rotated(a, cosine, sine):
    return a * cosine + pltpu.roll(a, HEAD // 2, 1) * sine


def total(refs):
    out = refs[0][...].astype(F32)
    for ref in refs[1:]:
        out = out + ref[...].astype(F32)
    return out


def heads_of(width):
    return [slice(h * HEAD, (h + 1) * HEAD) for h in range(width // HEAD)]


def keys_kernel(me_ref, x_ref, gain_ref, wk_ref, wv_ref, cos_ref, sin_ref, h_ref, *kv_refs):
    x = x_ref[...].astype(F32)
    factor = lax.rsqrt(jnp.mean(x * x, axis=-1, keepdims=True) + 1e-06)
    hidden = (x * factor * gain_ref[...]).astype(BF16)
    h_ref[...] = hidden
    cosine, sine = cos_ref[...], sin_ref[...]
    for g, kv_ref in enumerate(kv_refs):
        width = kv_ref.shape[2]
        cols = slice(g * width, (g + 1) * width)
        key = mm(hidden, wk_ref[:, cols])
        for cut in heads_of(width):
            kv_ref[0, :, cut] = rotated(key[:, cut], cosine, sine).astype(BF16)
        kv_ref[1] = mm(hidden, wv_ref[:, cols]).astype(BF16)


def project_keys(scal, x, gain, wk, wv, cosine, sine, n):
    tokens, width = x.shape
    local = wk.shape[1]
    rows, part = tokens // n, local // GROUPS
    mine = lambda r, m: (r, 0)
    return call(
        keys_kernel,
        (n,),
        [
            pl.BlockSpec((rows, width), lambda r, m: (r ^ m[0], 0)),
            fixed((1, width)),
            fixed((width, local)),
            fixed((width, local)),
            pl.BlockSpec((rows, HEAD), mine),
            pl.BlockSpec((rows, HEAD), mine),
        ],
        [pl.BlockSpec((rows, width), mine)]
        + [pl.BlockSpec((2, rows, part), lambda r, m: (0, r, 0))] * GROUPS,
        [((tokens, width), BF16)] + [((2, tokens, part), BF16)] * GROUPS,
        (scal, x, gain, wk, wv, cosine, sine),
        "project_keys",
        flops=4 * tokens * width * local,
        moved=4 * tokens * width + 4 * (tokens + width) * local,
    )


def query_kernel(me_ref, h_ref, w_ref, cos_ref, sin_ref, q_ref):
    pre = mm(h_ref[...], w_ref[...])
    for cut in heads_of(pre.shape[1]):
        q_ref[:, cut] = rotated(pre[:, cut], cos_ref[...], sin_ref[...]).astype(BF16)


def project_query(scal, hidden, wq, cosine, sine, n):
    tokens, width = hidden.shape
    local = wq.shape[1]
    rows = tokens // n
    mine = lambda r, m: (r, 0)
    return call(
        query_kernel,
        (n,),
        [
            pl.BlockSpec((rows, width), mine),
            fixed((width, local)),
            pl.BlockSpec((rows, HEAD), mine),
            pl.BlockSpec((rows, HEAD), mine),
        ],
        [pl.BlockSpec((rows, local), mine)],
        [((tokens, local), BF16)],
        (scal, hidden, wq, cosine, sine),
        "project_query",
        flops=2 * tokens * width * local,
        moved=2 * tokens * width + 2 * (tokens + width) * local,
    )[0]


def act_kernel(me_ref, cot_ref, w_ref, rel_ref, d_ref):
    cot = cot_ref[...]
    rel_ref[...] = cot
    d_ref[...] = mm(cot, w_ref[...], NT)


def project_cotangent(scal, cot, w_down, n):
    tokens, width = cot.shape
    hid = w_down.shape[0]
    rows = tokens // n
    mine = lambda r, m: (r, 0)
    return call(
        act_kernel,
        (n,),
        [pl.BlockSpec((rows, width), lambda r, m: (r ^ m[0], 0)), fixed((hid, width))],
        [pl.BlockSpec((rows, width), mine), pl.BlockSpec((rows, hid), mine)],
        [((tokens, width), BF16), ((tokens, hid), F32)],
        (scal, cot, w_down),
        "project_cotangent",
        flops=2 * tokens * width * hid,
        moved=4 * tokens * width + 4 * tokens * hid + 2 * width * hid,
    )


def masked(s, first, low, query_at, diagonal):
    key_at = first + lax.broadcasted_iota(jnp.int32, s.shape, 0)
    keep = key_at >= low
    if diagonal:
        keep = keep & (key_at <= query_at)
    return jnp.where(keep, s, NEG)


def lay_window(n, rows, me, odd, which, two_ref, odd_ref, even_ref, own_ref, put):
    for seg, refs in enumerate(((two_ref,), (odd_ref, even_ref), (own_ref,))):
        for sub in range(n):
            here = pl.ds(pl.multiple_of((sub ^ me) * rows, rows), rows)
            at = slice((seg * n + sub) * rows, (seg * n + sub + 1) * rows)
            if len(refs) == 1:
                put(at, refs[0][which, here, :])
            else:
                put(at, jnp.where(odd != 0, refs[0][which, here, :], refs[1][which, here, :]))


def attend_kernel(n, s_ref_, q_ref, two_ref, odd_ref, even_ref, own_ref, low_ref, o_ref, lse_ref, s_ref, k_ref, vt_ref):
    rows = q_ref.shape[0]
    me, odd = s_ref_[0], s_ref_[1]
    r = pl.program_id(1)
    rb = r ^ me
    chunks = 2 * n + 1

    @pl.when(r == 0)
    def _():
        def put_key(at, block):
            k_ref[at, :] = block

        def put_value(at, block):
            vt_ref[:, at] = block.T

        window = (two_ref, odd_ref, even_ref, own_ref)
        lay_window(n, rows, me, odd, 0, *window, put_key)
        lay_window(n, rows, me, odd, 1, *window, put_value)

    q = q_ref[...]
    low = low_ref[...]
    query_at = (rb + 2 * n) * rows + lax.broadcasted_iota(jnp.int32, (1, rows), 1)
    top = jnp.full((1, rows), NEG, F32)
    for c in range(chunks):
        first = pl.multiple_of((rb + c) * rows, rows)
        s = mm(k_ref[pl.ds(first, rows), :], q, NT)
        s = masked(s, first, low, query_at, c == chunks - 1)
        s_ref[c * rows : (c + 1) * rows, :] = s
        top = jnp.maximum(top, jnp.max(s, axis=0, keepdims=True))
    top = top * (SCALE * LOG2E)
    whole = jnp.zeros((1, rows), F32)
    acc = jnp.zeros((HEAD, rows), F32)
    for c in range(chunks):
        first = pl.multiple_of((rb + c) * rows, rows)
        p = jnp.exp2(s_ref[c * rows : (c + 1) * rows, :] * (SCALE * LOG2E) - top)
        whole = whole + jnp.sum(p, axis=0, keepdims=True)
        acc = acc + mm(vt_ref[:, pl.ds(first, rows)], p.astype(BF16))
    o_ref[...] = (acc / whole).T.astype(BF16)
    lse_ref[...] = (top + jnp.log2(whole)).reshape(lse_ref.shape)


def attend(scal, g, q, segments, low, n):
    tokens = q.shape[0]
    part = segments[0].shape[2]
    heads, rows = part // HEAD, tokens // n
    pairs = heads * tokens * (2 * tokens + rows)
    segment = pl.BlockSpec((2, tokens, HEAD), lambda h, r, m: (0, 0, h))
    return call(
        lambda *refs: attend_kernel(n, *refs),
        (heads, n),
        [pl.BlockSpec((rows, HEAD), lambda h, r, m: (r, g * heads + h))]
        + [segment] * 4
        + [pl.BlockSpec((1, rows), lambda h, r, m: (0, r))],
        [
            pl.BlockSpec((rows, HEAD), lambda h, r, m: (r, h)),
            pl.BlockSpec((1, 1, rows), lambda h, r, m: (h, 0, r)),
        ],
        [((tokens, part), BF16), ((heads, 1, tokens), F32)],
        (scal, q, *segments, low),
        "attend",
        scratch=[
            pltpu.VMEM(((2 * n + 1) * rows, rows), F32),
            pltpu.VMEM((3 * tokens, HEAD), BF16),
            pltpu.VMEM((HEAD, 3 * tokens), BF16),
        ],
        flops=8 * pairs * HEAD,
        moved=20 * tokens * part,
        exps=pairs,
    )


def attend_back_kernel(
    n, s_ref_, q_ref, two_ref, odd_ref, even_ref, own_ref, low_ref, o_ref, do_ref, lse_ref, cos_ref, sin_ref,
    dq_ref, d_two_ref, d_one_ref, d_own_ref, dk_acc, dv_acc, k_ref, kt_ref, v_ref,
):
    rows = q_ref.shape[0]
    me, odd = s_ref_[0], s_ref_[1]
    r = pl.program_id(1)
    rb = r ^ me
    chunks = 2 * n + 1

    @pl.when(r == 0)
    def _():
        def put_key(at, block):
            k_ref[at, :] = block
            kt_ref[:, at] = block.T
            dk_acc[at, :] = jnp.zeros((rows, HEAD), F32)
            dv_acc[at, :] = jnp.zeros((rows, HEAD), F32)

        def put_value(at, block):
            v_ref[at, :] = block

        window = (two_ref, odd_ref, even_ref, own_ref)
        lay_window(n, rows, me, odd, 0, *window, put_key)
        lay_window(n, rows, me, odd, 1, *window, put_value)

    q, do = q_ref[...], do_ref[...]
    low = low_ref[...]
    lse = lse_ref[...].reshape(1, rows)
    delta = jnp.sum((do.astype(F32) * o_ref[...].astype(F32)).T, axis=0, keepdims=True)
    query_at = (rb + 2 * n) * rows + lax.broadcasted_iota(jnp.int32, (1, rows), 1)
    dqt = jnp.zeros((HEAD, rows), F32)
    for c in range(chunks):
        first = pl.multiple_of((rb + c) * rows, rows)
        here = pl.ds(first, rows)
        s = mm(k_ref[here, :], q, NT) * (SCALE * LOG2E)
        s = masked(s, first, low, query_at, c == chunks - 1)
        p = jnp.exp2(s - lse)
        dv_acc[here, :] += mm(p.astype(BF16), do)
        dp = mm(v_ref[here, :], do, NT)
        ds = (p * (dp - delta)).astype(BF16)
        dk_acc[here, :] += mm(ds, q)
        dqt = dqt + mm(kt_ref[:, here], ds)
    dq_ref[...] = rotated(dqt.T * SCALE, cos_ref[...], -sin_ref[...]).astype(BF16)

    @pl.when(r == n - 1)
    def _():
        for seg, out_ref in enumerate((d_two_ref, d_one_ref, d_own_ref)):
            for sub in range(n):
                here = pl.ds(pl.multiple_of((sub ^ me) * rows, rows), rows)
                at = slice((seg * n + sub) * rows, (seg * n + sub + 1) * rows)
                out_ref[0, here, :] = (dk_acc[at, :] * SCALE).astype(BF16)
                out_ref[1, here, :] = dv_acc[at, :].astype(BF16)


def attend_back(scal, g, q, segments, low, attended, d_attended, lse, cosine, sine, n):
    tokens = q.shape[0]
    part = segments[0].shape[2]
    heads, rows = part // HEAD, tokens // n
    pairs = heads * tokens * (2 * tokens + rows)
    block = pl.BlockSpec((rows, HEAD), lambda h, r, m: (r, h))
    shared = pl.BlockSpec((rows, HEAD), lambda h, r, m: (r, g * heads + h))
    segment = pl.BlockSpec((2, tokens, HEAD), lambda h, r, m: (0, 0, h))
    table = pl.BlockSpec((rows, HEAD), lambda h, r, m: (r, 0))
    return call(
        lambda *refs: attend_back_kernel(n, *refs),
        (heads, n),
        [shared]
        + [segment] * 4
        + [
            pl.BlockSpec((1, rows), lambda h, r, m: (0, r)),
            block,
            shared,
            pl.BlockSpec((1, 1, rows), lambda h, r, m: (h, 0, r)),
            table,
            table,
        ],
        [block] + [segment] * 3,
        [((tokens, part), BF16)] + [((2, tokens, part), BF16)] * 3,
        (scal, q, *segments, low, attended, d_attended, lse, cosine, sine),
        "attend_back",
        scratch=[
            pltpu.VMEM((3 * tokens, HEAD), F32),
            pltpu.VMEM((3 * tokens, HEAD), F32),
            pltpu.VMEM((3 * tokens, HEAD), BF16),
            pltpu.VMEM((HEAD, 3 * tokens), BF16),
            pltpu.VMEM((3 * tokens, HEAD), BF16),
        ],
        flops=20 * pairs * HEAD,
        moved=36 * tokens * part,
        exps=pairs,
    )


def put_part(value, refs):
    half = refs[0].shape[1]
    value = value.astype(BF16)
    for r in range(len(refs) // 2):

        @pl.when(pl.program_id(0) == r)
        def _():
            refs[2 * r][...] = value[:, :half]
            refs[2 * r + 1][...] = value[:, half:]


def part_outs(n, rows, width):
    half = (rows, width // 2)
    return [pl.BlockSpec(half, lambda *_: (0, 0))] * (2 * n), [(half, BF16)] * (2 * n)


def sum_kernel(count, me_ref, *refs):
    arrays, w_ref, part_refs = refs[:count], refs[count], refs[count + 1 :]
    deep = arrays[0].shape[1]
    acc = mm(arrays[0][...], w_ref[:deep, :])
    for g in range(1, count):
        acc = acc + mm(arrays[g][...], w_ref[g * deep : (g + 1) * deep, :])
    put_part(acc, part_refs)


def project_sum(scal, arrays, weight, n, name):
    tokens, deep = arrays[0].shape
    width = weight.shape[1]
    rows = tokens // n
    specs, outs = part_outs(n, rows, width)
    return call(
        lambda *refs: sum_kernel(len(arrays), *refs),
        (n,),
        [pl.BlockSpec((rows, deep), lambda r, m: (r, 0))] * len(arrays) + [fixed(weight.shape)],
        specs,
        outs,
        (scal, *arrays, weight),
        name,
    )


def own_rows(kernel, scal, outs, args, lists, name):
    rows, half = lists[0][0].shape
    flat = tuple(lists[0]) + tuple(lists[1])
    count = len(args)

    def body(_, *refs):
        left = refs[count : count + len(lists[0])]
        right = refs[count + len(lists[0]) : count + len(flat)]
        summed = jnp.concatenate([total(left), total(right)], axis=1)
        kernel(summed, *refs[:count], *refs[count + len(flat) :])

    own = pl.BlockSpec((rows, 2 * half), lambda i, m: (m[0], 0))
    return call(
        body,
        (1,),
        [own if a.shape[0] > rows else fixed(a.shape) for a in args] + [fixed((rows, half))] * len(flat),
        [fixed(shape) for shape, _ in outs],
        outs,
        (scal, *args, *flat),
        name,
    )


def mid_kernel(summed, x_ref, gain_ref, mid_ref, left_ref, right_ref):
    half = left_ref.shape[1]
    mid = x_ref[...].astype(F32) + summed
    mid_ref[...] = mid
    factor = lax.rsqrt(jnp.mean(mid * mid, axis=-1, keepdims=True) + 1e-06)
    hidden = (mid * factor * gain_ref[...]).astype(BF16)
    left_ref[...] = hidden[:, :half]
    right_ref[...] = hidden[:, half:]


def back_norm(d_hidden, values, gain, d_gain_ref=None):
    factor = lax.rsqrt(jnp.mean(values * values, axis=-1, keepdims=True) + 1e-06)
    normed = values * factor
    if d_gain_ref is not None:
        d_gain_ref[...] = jnp.sum(d_hidden * normed, axis=0, keepdims=True)
    e = d_hidden * gain
    return factor * (e - normed * jnp.mean(e * normed, axis=-1, keepdims=True))


def d_mid_kernel(d_hidden, mid_ref, gain_ref, cot_ref, d_mid_ref, left_ref, right_ref, d_gain_ref):
    half = left_ref.shape[1]
    d_mid = cot_ref[...].astype(F32) + back_norm(d_hidden, mid_ref[...], gain_ref[...], d_gain_ref)
    d_mid_ref[...] = d_mid
    left_ref[...] = d_mid[:, :half].astype(BF16)
    right_ref[...] = d_mid[:, half:].astype(BF16)


def input_kernel(d_hidden, x_ref, gain_ref, d_mid_ref, own_ref, left_ref, right_ref):
    half = left_ref.shape[1]
    grad = d_mid_ref[...] + back_norm(d_hidden, x_ref[...].astype(F32), gain_ref[...])
    own_ref[...] = grad
    left_ref[...] = grad[:, :half].astype(BF16)
    right_ref[...] = grad[:, half:].astype(BF16)


def output_kernel(summed, mid_ref, left_ref, right_ref):
    half = left_ref.shape[1]
    out = (mid_ref[...] + summed).astype(BF16)
    left_ref[...] = out[:, :half]
    right_ref[...] = out[:, half:]


def lay_block(n, left_refs, right_refs, whole_ref):
    half = left_refs[0].shape[1]
    for r in range(n):

        @pl.when(pl.program_id(0) == r)
        def _():
            whole_ref[:, :half] = left_refs[r][...].astype(whole_ref.dtype)
            whole_ref[:, half:] = right_refs[r][...].astype(whole_ref.dtype)


def mlp_kernel(n, me_ref, *refs):
    left, right = refs[:n], refs[n : 2 * n]
    d_act_ref, wg_ref, wu_ref, h_ref, act_ref, dg_ref, du_ref = refs[2 * n : 2 * n + 7]
    lay_block(n, left, right, h_ref)
    hidden = h_ref[...]
    gate = mm(hidden, wg_ref[...], NT)
    up = mm(hidden, wu_ref[...], NT)
    d_act = d_act_ref[...]
    s = 1.0 / (1.0 + jnp.exp(-gate))
    silu = gate * s
    act_ref[...] = (silu * up).astype(BF16)
    d_gate = (d_act * up * s * (1.0 + gate * (1.0 - s))).astype(BF16)
    d_up = (d_act * silu).astype(BF16)
    dg_ref[...] = d_gate
    du_ref[...] = d_up
    put_part(mm(d_gate, wg_ref[...]) + mm(d_up, wu_ref[...]), refs[2 * n + 7 :])


def mlp(scal, halves, d_act, w_gate, w_up, n):
    rows, half = halves[0][0].shape
    hid, width = w_gate.shape
    tokens = rows * n
    mine = lambda r, m: (r, 0)
    specs, outs = part_outs(n, rows, width)
    hidden, act, d_gate, d_up, *parts = call(
        lambda *refs: mlp_kernel(n, *refs),
        (n,),
        [fixed((rows, half))] * (2 * n)
        + [pl.BlockSpec((rows, hid), mine), fixed((hid, width)), fixed((hid, width))],
        [pl.BlockSpec((rows, width), mine)] + [pl.BlockSpec((rows, hid), mine)] * 3 + specs,
        [((tokens, width), BF16)] + [((tokens, hid), BF16)] * 3 + outs,
        (scal, *halves[0], *halves[1], d_act, w_gate, w_up),
        "mlp",
        vmem=56,
    )
    return hidden, act, d_gate, d_up, parts


def d_attended_kernel(n, me_ref, *refs):
    left, right = refs[:n], refs[n : 2 * n]
    w_ref, low_ref, d_ref = refs[2 * n :]
    lay_block(n, left, right, low_ref)
    d_ref[...] = mm(low_ref[...], w_ref[...], NT).astype(BF16)


def project_back(scal, halves, w_out, n):
    rows, half = halves[0][0].shape
    local, width = w_out.shape
    tokens = rows * n
    mine = lambda r, m: (r, 0)
    return call(
        lambda *refs: d_attended_kernel(n, *refs),
        (n,),
        [fixed((rows, half))] * (2 * n) + [fixed((local, width))],
        [pl.BlockSpec((rows, width), mine), pl.BlockSpec((rows, local), mine)],
        [((tokens, width), BF16), ((tokens, local), BF16)],
        (scal, *halves[0], *halves[1], w_out),
        "project_back",
        flops=2 * tokens * width * local,
        moved=4 * tokens * width + 2 * (tokens + width) * local,
    )


def place_kernel(blocks, has_own, me_ref, *refs):
    count = len(blocks)
    left, right, out_ref = refs[:count], refs[count : 2 * count], refs[-1]
    lay_block(count, left, right, out_ref)
    if has_own:

        @pl.when(pl.program_id(0) == 0)
        def _():
            out_ref[...] = refs[2 * count][...]


def place(scal, halves, blocks, kind, n, own=None, whole=None):
    rows, half = halves[0][0].shape
    first = blocks[0]
    arrays = [side[r] for side in halves for r in blocks]
    extra = [] if own is None else [own]
    held = [] if whole is None else [whole]
    return pl.pallas_call(
        lambda *refs: place_kernel(blocks, own is not None, *refs),
        grid_spec=pltpu.PrefetchScalarGridSpec(
            num_scalar_prefetch=1,
            grid=(len(blocks),),
            in_specs=[fixed((rows, half))] * len(arrays)
            + [fixed(e.shape) for e in extra]
            + [pl.BlockSpec(memory_space=pl.ANY)] * len(held),
            out_specs=pl.BlockSpec((rows, 2 * half), lambda r, m: ((r + first) ^ m[0], 0)),
        ),
        out_shape=jax.ShapeDtypeStruct((rows * n, 2 * half), kind),
        input_output_aliases={1 + len(arrays) + len(extra): 0} if held else {},
        compiler_params=pltpu.CompilerParams(vmem_limit_bytes=40 * MIB),
        cost_estimate=pl.CostEstimate(flops=0, bytes_accessed=0, transcendentals=0),
        name="place",
    )(scal, *arrays, *extra, *held)


def finish_kernel(s_ref_, own_ref, across_ref, back_ref, dq_ref, cos_ref, sin_ref, all_ref):
    part = dq_ref.shape[1]
    share = jnp.where(s_ref_[1] != 0, 0.0, 1.0)
    whole = own_ref[...].astype(F32) + back_ref[...].astype(F32) + across_ref[...].astype(F32) * share
    all_ref[:, :part] = dq_ref[...]
    for h, cut in enumerate(heads_of(part)):
        to = slice(part + h * HEAD, part + (h + 1) * HEAD)
        all_ref[:, to] = rotated(whole[0, :, cut], cos_ref[...], -sin_ref[...]).astype(BF16)
    all_ref[:, 2 * part :] = whole[1].astype(BF16)


def finish(scal, own, across, back, dq, cosine, sine, n):
    tokens, part = dq.shape
    rows = tokens // n
    segment = pl.BlockSpec((2, rows, part), lambda r, m: (0, r, 0))
    mine = lambda r, m: (r, 0)
    return call(
        finish_kernel,
        (n,),
        [segment] * 3
        + [pl.BlockSpec((rows, part), mine), pl.BlockSpec((rows, HEAD), mine), pl.BlockSpec((rows, HEAD), mine)],
        [pl.BlockSpec((rows, 3 * part), mine)],
        [((tokens, 3 * part), BF16)],
        (scal, own, across, back, dq, cosine, sine),
        "finish",
        moved=20 * tokens * part,
    )[0]


def d_one_kernel(me_ref, *refs):
    grads, weights = refs[:GROUPS], refs[GROUPS : GROUPS + 3]
    x_ref, gain_ref = refs[GROUPS + 3 : GROUPS + 5]
    part = grads[0].shape[1] // 3
    acc = None
    for g, grad in enumerate(grads):
        for k, w_ref in enumerate(weights):
            term = mm(grad[:, k * part : (k + 1) * part], w_ref[:, g * part : (g + 1) * part], NT)
            acc = term if acc is None else acc + term
    put_part(acc, refs[GROUPS + 5 :])
    x = x_ref[...].astype(F32)
    factor = lax.rsqrt(jnp.mean(x * x, axis=-1, keepdims=True) + 1e-06)

    @pl.when(pl.program_id(0) == 0)
    def _():
        gain_ref[...] = jnp.zeros_like(gain_ref)

    gain_ref[...] += jnp.sum(acc * (x * factor), axis=0, keepdims=True)


def project_one_back(scal, grads, weights, x, n):
    tokens, triple = grads[0].shape
    width, local = weights[0].shape
    rows = tokens // n
    specs, outs = part_outs(n, rows, width)
    d_gain, *parts = call(
        d_one_kernel,
        (n,),
        [pl.BlockSpec((rows, triple), lambda r, m: (r, 0))] * GROUPS
        + [fixed((width, local))] * 3
        + [pl.BlockSpec((rows, width), lambda r, m: (r ^ m[0], 0))],
        [fixed((1, width))] + specs,
        [((1, width), F32)] + outs,
        (scal, *grads, *weights, x),
        "project_one_back",
    )
    return d_gain, parts


def seq_sums(sums):
    peers = lax.axis_size("seq")
    at = lax.axis_index("seq")
    for bit in bits_of(peers)[::-1]:
        half = sums.shape[1] // 2
        upper = (at & bit) != 0
        low_part, high_part = sums[:, :half], sums[:, half:]
        kept = jnp.where(upper, high_part, low_part)
        sums = kept + swap(jnp.where(upper, low_part, high_part), bit, "seq")
    return sums


def scattered(grad, dim):
    return lax.psum_scatter(grad, "seq", scatter_dimension=dim, tiled=True)


def on_device(
    block_input, norm_one, w_query, w_key, w_value, w_out, norm_two, w_gate, w_up, w_down,
    starts, cotangent,
):
    tokens, width = block_input.shape
    hid = w_gate.shape[1]
    n = lax.axis_size("tp")
    me = lax.axis_index("tp")
    peers = lax.axis_size("seq")
    at = lax.axis_index("seq")
    rows = tokens // n
    odd = (at & 1) != 0
    scal = jnp.stack([me, at & 1]).astype(jnp.int32)
    gain_one, gain_two = norm_one[None, :], norm_two[None, :]

    order = to_relative(jnp.arange(tokens, dtype=jnp.int32), me, n)
    starts_here = to_relative(starts, me, n)
    positions = (at * tokens + order - starts_here).astype(F32)
    freqs = 10000.0 ** (-2.0 * jnp.arange(HEAD // 2, dtype=F32) / HEAD)
    angles = positions[:, None] * freqs[None, :]
    cosine, sine = jnp.cos(angles), jnp.sin(angles)
    cosine, sine = jnp.concatenate([cosine, cosine], 1), jnp.concatenate([-sine, sine], 1)
    low = jnp.maximum(starts_here - (at - 2) * tokens, order + 2 * tokens - WINDOW + 1)[None, :]

    hidden_one, *packed = project_keys(scal, block_input, gain_one, w_key, w_value, cosine, sine, n)

    right_two = [(i, i + 2) for i in range(peers - 2)]
    left_two = [(i + 2, i) for i in range(peers - 2)]
    to_odd = [(i, i + 1) for i in range(0, peers, 2)]
    to_even = [(i + 1, i) for i in range(0, peers, 2)]
    query = project_query(scal, hidden_one, w_query, cosine, sine, n)
    cot, d_act = project_cotangent(scal, cotangent, w_down, n)

    segments, attended, lse = [], [], []
    twos = [lax.ppermute(own, "seq", right_two) for own in packed]
    acrosses = [lax.ppermute(own, "seq", to_odd) for own in packed]
    for g, own in enumerate(packed):
        two = tied(twos[g], attended[g - 1] if g else (query, d_act))
        segments.append((two, acrosses[g], lax.ppermute(two, "seq", to_even), own))
        out, peak = attend(scal, g, query, segments[g], low, n)
        attended.append(out)
        lse.append(peak)
    parts = project_sum(scal, attended, w_out, n, "project_out")
    own_f32, own_half = ((rows, width), F32), ((rows, width // 2), BF16)
    mid, *hidden_own = own_rows(
        mid_kernel, scal, [own_f32, own_half, own_half], (block_input, gain_two),
        sum_second(*sum_first(parts, n), n), "mid",
    )
    hidden_halves = all_blocks(hidden_own, n)
    hidden_two, activation, d_gate, d_up, parts = mlp(scal, hidden_halves, d_act, w_gate.T, w_up.T, n)

    d_two_sent, d_two_kept = sum_first(parts, n)
    d_two_sent, act_later, d_gate_later = lax.optimization_barrier((d_two_sent, activation, d_gate))
    d_hidden_two = sum_second(d_two_sent, d_two_kept, n)
    grad_down = mm(act_later, cot, TN).astype(BF16)
    grad_gate = mm(d_gate_later, hidden_two, TN).astype(BF16)
    d_hidden_two, grad_down, grad_gate = lax.optimization_barrier((d_hidden_two, grad_down, grad_gate))
    grad_down, grad_gate = scattered(grad_down, 1), scattered(grad_gate, 1)
    gain_row = ((1, width), F32)
    d_mid, *d_mid_own, d_gain_two = own_rows(
        d_mid_kernel, scal, [own_f32, own_half, own_half, gain_row], (mid, gain_two, cotangent), d_hidden_two, "d_mid"
    )
    d_mid_own, act_later, d_up_later = lax.optimization_barrier((d_mid_own, act_later, d_up))
    d_mid_halves = all_blocks(d_mid_own, n)
    out_parts = project_sum(scal, [act_later], w_down, n, "project_down")
    grad_up = mm(d_up_later, hidden_two, TN).astype(BF16)
    d_mid_halves, out_parts, grad_up = lax.optimization_barrier((d_mid_halves, out_parts, grad_up))
    grad_up = scattered(grad_up, 1)
    out_sent, out_kept = sum_first(out_parts, n)
    d_mid_low, d_attended = project_back(scal, d_mid_halves, w_out, n)

    def sent_back(d_two, d_one, after=()):
        across = tied(swap(d_one, 1, "seq"), after)
        sent = (d_two.astype(F32) + jnp.where(odd, across.astype(F32), 0.0)).astype(BF16)
        return across, sent

    def back(g, d_attended):
        return attend_back(scal, g, query, segments[g], low, attended[g], d_attended, lse[g], cosine, sine, n)

    d_attended, out_sent = lax.optimization_barrier((d_attended, out_sent))
    out_terms = sum_second(out_sent, out_kept, n)
    dq, d_two, d_one, d_own = back(0, d_attended)
    low_later = tied(d_mid_low, dq)
    grad_out = jnp.concatenate([mm(a, low_later, TN).astype(BF16) for a in attended], axis=0)
    across, sent = sent_back(d_two, d_one, grad_out)
    grad_out = scattered(grad_out, 1)
    out_own = own_rows(output_kernel, scal, [own_half, own_half], (mid,), out_terms, "output")
    out_halves = all_blocks(out_own, n)
    d_attended, sent, across, out_own = lax.optimization_barrier((d_attended, sent, across, out_own))
    back_two = lax.ppermute(sent, "seq", left_two)
    dq_1, d_two_1, d_one_1, d_own_1 = back(1, d_attended)
    across_1, sent_1 = sent_back(d_two_1, d_one_1, back_two)
    sent_1, back_two = lax.optimization_barrier((sent_1, back_two))
    back_two_1 = lax.ppermute(sent_1, "seq", left_two)
    first = finish(scal, d_own, across, back_two, dq, cosine, sine, n)
    output = place(scal, out_halves, tuple(range(n)), BF16, n)
    back_two_1 = tied(back_two_1, (first, output, grad_down))
    second = finish(scal, d_own_1, across_1, back_two_1, dq_1, cosine, sine, n)
    d_gain_one, parts = project_one_back(scal, [first, second], (w_query, w_key, w_value), block_input, n)
    d_one_sent, d_one_kept = sum_first(parts, n)
    d_one_sent, first, second = lax.optimization_barrier((d_one_sent, first, second))
    d_hidden_one = sum_second(d_one_sent, d_one_kept, n)
    grad_first = mm(hidden_one, first, TN).astype(BF16)
    grad_second = mm(hidden_one, second, TN).astype(BF16)
    gains = seq_sums(jnp.concatenate([d_gain_one, d_gain_two], axis=0))
    d_hidden_one, gains = tied((d_hidden_one, gains), (grad_first, grad_second, grad_gate))
    grad_qkv = [scattered(grad_first, 0), scattered(grad_second, 0)]
    input_grad, *input_own_halves = own_rows(
        input_kernel, scal, [own_f32, own_half, own_half], (block_input, gain_one, d_mid), d_hidden_one, "input"
    )
    input_halves = all_blocks(input_own_halves, n)
    for bit in bits_of(n):
        gains = gains + swap(gains, bit)
    early, late = tuple(range(n - 1)), (n - 1,)
    early_halves = [side[: n - 1] for side in input_halves]
    grad_input = place(scal, tied(early_halves, grad_up), early, F32, n, own=input_grad)
    grad_input = place(scal, input_halves, late, F32, n, whole=grad_input)

    part = grad_qkv[0].shape[1] // 3
    grad_query, grad_key, grad_value = (
        jnp.concatenate([g[:, k * part : (k + 1) * part] for g in grad_qkv], axis=1).astype(F32)
        for k in range(3)
    )
    return (
        output, grad_input, gains[0], grad_query, grad_key, grad_value, grad_out.astype(F32), gains[1],
        grad_gate.T.astype(F32), grad_up.T.astype(F32), grad_down.astype(F32),
    )


def solution(mesh):
    in_specs = (
        P("seq", None), P(), P(None, "tp"), P(None, "tp"), P(None, "tp"), P("tp", None), P(),
        P(None, "tp"), P(None, "tp"), P("tp", None), P("seq"), P("seq", None),
    )
    out_specs = (
        P("seq", None), P("seq", None), P("seq"), P("seq", "tp"), P("seq", "tp"), P("seq", "tp"),
        P("tp", "seq"), P("seq"), P("seq", "tp"), P("seq", "tp"), P("tp", "seq"),
    )
    return jax.shard_map(
        on_device, mesh=mesh, in_specs=in_specs, out_specs=out_specs, check_vma=False
    )
```

time: 791 us -> 650 us (0.82)
  Pallas kernels: 85.6 us -> 222 us
  matrix products: 177 us -> 41.3 us
  waiting for transfers between devices: 350 us -> 240 us
  other arithmetic: 66.5 us -> 22 us
  starting transfers between devices: 47.7 us -> 80.4 us
  local copies, waits for them, and re-layouts: 43 us -> 21.2 us
    pallas_call x3 -> x21, Pallas kernels: 85.6 us -> 222 us  [the longest x18 211 us: call(): pl.pallas_call(body, grid_spec=pltpu.PrefetchScalarGridSpec(num_scalar_pr...]
    dot_general x18 -> x7, matrix products: 177 us -> 41.3 us  [mm(): return lax.dot_general(a, b, dims, preferred_element_type=F32)]
    ppermute x38 -> x55, waiting for transfers between devices: 258 us -> 174 us  [swap(): return lax.ppermute(array, axis, [(i, i ^ bit) for i in range(size)])]
    ppermute x4 -> x8, waiting for transfers between devices: 92.2 us -> 57.3 us  [the longest x1 48.3 us: on_device(): back_two = lax.ppermute(sent, 'seq', left_two)]
    ppermute x38 -> x55, starting transfers between devices: 35 us -> 56.3 us  [swap(): return lax.ppermute(array, axis, [(i, i ^ bit) for i in range(size)])]
    slice x19 -> x2, local copies, waits for them, and re-layouts: 14.7 us -> 2.12 us  [on_device(): g[:, k * part:(k + 1) * part]]
    ppermute x4 -> x8, starting transfers between devices: 12.2 us -> 23.5 us  [the longest x2 10.9 us: on_device(): twos = [lax.ppermute(own, 'seq', right_two) for own in packed]]
    dynamic_update_slice x7 -> x0, other arithmetic: 10.2 us -> none  [to_natural(): whole = lax.dynamic_update_slice_in_dim(whole, block, (r ^ me) * rows, 0)]
  transfers between devices with their start and end apart: 49 -> 69, of which waited for: 30 -> 33; matrix products, arithmetic and copies ran while one was open for 22% -> 9% of each run, Pallas kernels for 6% -> 23%
where the time goes in v2:
time: 650 us; the launch traced here: 642 us
  waiting for transfers between devices  240 us (37%)
  Pallas kernels  222 us (34%)
  starting transfers between devices  80.4 us (12%)
  matrix products  41.3 us (6%)
  other arithmetic  22 us (3%)
  local copies, waits for them, and re-layouts  21.2 us (3%)
  between operations  15.3 us (2%)
    pallas_call x18, Pallas kernels, call(): pl.pallas_call(body, grid_spec=pltpu.PrefetchScalarGridSpec(num_scalar_pr...  211 us
    ppermute x55, waiting for transfers between devices, swap(): return lax.ppermute(array, axis, [(i, i ^ bit) for i in range(size)])  174 us
    ppermute x55, starting transfers between devices, swap(): return lax.ppermute(array, axis, [(i, i ^ bit) for i in range(size)])  56.3 us
    ppermute x1, waiting for transfers between devices, on_device(): back_two = lax.ppermute(sent, 'seq', left_two)  48.3 us
    dot_general x7, matrix products, mm(): return lax.dot_general(a, b, dims, preferred_element_type=F32)  41.3 us
    unnamed x120, local copies, waits for them, and re-layouts  17.3 us
  transfers between devices with their start and end apart: 69, of which 33 were waited for; matrix products, arithmetic and copies ran while one was open for 9% of the time, Pallas kernels for 23%

profile of v2, /device:TPU:0, one launch (start us, length us, event | category | flops | bytes accessed | tf_op | source)
XLA Modules:
  0.0 642.4 jit_solution(17505972513695329648)
XLA Ops:
  10.9 9.8 %project_keys.1 = (bf16[1024,2048]{1,0:T(8,128)(2,1)}, bf16[2,1024,256]{2,1,0:T(8,128)(2,1)}, bf16[2,1024,256]{2,1,0:T(8,128)(2,1)S(1)}) custom-call(s32[2]{0:T(128)S(1)} %pad_add_fusion.me_ref.refs_0_._.s_ref_, bf16[1024,2048]{1,0:T(8,128)(2,1)} %refs_0_.3, f32[1,2048]{1,0:T(1,128)S(1)} %bitcast.36, bf16[2048,512]{1,0:T(8,128)(2,1)S(1)} %copy-done.1, ...), custom_call_target="tpu_custom_call" | custom-call | tf_op jit(solution)/shard_map/project_keys/pallas_call | solution.py:32
  20.8 5.9 collective-permute-start
  29.1 5.7 project_query.1.refs_1_
  34.8 12.0 %project_cotangent.1 = (bf16[1024,2048]{1,0:T(8,128)(2,1)S(1)}, f32[1024,1376]{1,0:T(8,128)}) custom-call(s32[2]{0:T(128)S(1)} %pad_add_fusion.me_ref.refs_0_._.s_ref_, bf16[1024,2048]{1,0:T(8,128)(2,1)} %refs_2_.3, bf16[1376,2048]{1,0:T(8,128)(2,1)} %refs_2_.4), custom_call_target="tpu_custom_call" | custom-call | tf_op jit(solution)/shard_map/project_cotangent/pallas_call | solution.py:32
  50.2 5.0 collective-permute-start.3
  55.1 4.7 collective-permute-start.4
  59.8 14.8 %attend.2 = (bf16[1024,256]{1,0:T(8,128)(2,1)S(1)}, f32[2,1,1024]{2,1,0:T(1,128)S(1)}) custom-call(s32[2]{0:T(128)S(1)} %pad_add_fusion.me_ref.refs_0_._.s_ref_, bf16[1024,512]{1,0:T(8,128)(2,1)S(1)} %project_query.1.refs_1_, bf16[2,1024,256]{2,1,0:T(8,128)(2,1)} %collective-permute-done.refs_2_, bf16[2,1024,256]{2,1,0:T(8,128)(2,1)} %collective-permute-done.1.refs_3_, ...), custom_call_target="tpu_custom_call" | custom-call | tf_op jit(solution)/shard_map/attend/pallas_call | solution.py:32
  78.0 3.4 collective-permute-done.5.refs_4_
  81.4 14.7 %attend.3 = (bf16[1024,256]{1,0:T(8,128)(2,1)S(1)}, f32[2,1,1024]{2,1,0:T(1,128)S(1)}) custom-call(s32[2]{0:T(128)S(1)} %pad_add_fusion.me_ref.refs_0_._.s_ref_, bf16[1024,512]{1,0:T(8,128)(2,1)S(1)} %project_query.1.refs_1_, bf16[2,1024,256]{2,1,0:T(8,128)(2,1)} %collective-permute-done.3.refs_2_, bf16[2,1024,256]{2,1,0:T(8,128)(2,1)} %collective-permute-done.4.refs_3_, ...), custom_call_target="tpu_custom_call" | custom-call | tf_op jit(solution)/shard_map/attend/pallas_call | solution.py:32
  96.1 5.5 project_out.1
  105.7 10.7 %collective-permute-done.7 = bf16[256,1024]{1,0:T(8,128)(2,1)S(1)} collective-permute-done((bf16[256,1024]{1,0:T(8,128)(2,1)S(1)}, bf16[256,1024]{1,0:T(8,128)(2,1)S(1)}, u32[]{:S(2)}, u32[]{:S(2)}) %collective-permute-start.7) | collective-permute-done | bytes 524320 | tf_op jit(solution)/shard_map/ppermute | solution.py:61
  120.0 7.7 %collective-permute-done.6.refs_3_ = bf16[256,1024]{1,0:T(8,128)(2,1)S(1)} collective-permute-done((bf16[256,1024]{1,0:T(8,128)(2,1)S(1)}, bf16[256,1024]{1,0:T(8,128)(2,1)S(1)}, u32[]{:S(2)}, u32[]{:S(2)}) %collective-permute-start.6) | collective-permute-done | bytes 524320 | tf_op jit(solution)/shard_map/ppermute | solution.py:61
  129.2 10.1 %collective-permute-done.8.refs_4_ = bf16[256,1024]{1,0:T(8,128)(2,1)S(1)} collective-permute-done((bf16[256,1024]{1,0:T(8,128)(2,1)S(1)}, bf16[256,1024]{1,0:T(8,128)(2,1)S(1)}, u32[]{:S(2)}, u32[]{:S(2)}) %collective-permute-start.8) | collective-permute-done | bytes 524320 | tf_op jit(solution)/shard_map/ppermute | solution.py:61
  139.3 3.7 mid.1
  147.1 10.8 %collective-permute-done.13.refs_3_ = bf16[256,1024]{1,0:T(8,128)(2,1)S(1)} collective-permute-done((bf16[256,1024]{1,0:T(8,128)(2,1)S(1)}, bf16[256,1024]{1,0:T(8,128)(2,1)S(1)}, u32[]{:S(2)}, u32[]{:S(2)}) %collective-permute-start.13) | collective-permute-done | bytes 524320 | tf_op jit(solution)/shard_map/ppermute | solution.py:61
  160.0 10.7 %collective-permute-done.12.refs_2_ = bf16[256,1024]{1,0:T(8,128)(2,1)S(1)} collective-permute-done((bf16[256,1024]{1,0:T(8,128)(2,1)S(1)}, bf16[256,1024]{1,0:T(8,128)(2,1)S(1)}, u32[]{:S(2)}, u32[]{:S(2)}) %collective-permute-start.12) | collective-permute-done | bytes 524320 | tf_op jit(solution)/shard_map/ppermute | solution.py:61
  170.7 8.9 %collective-permute-done.14.refs_4_ = bf16[256,1024]{1,0:T(8,128)(2,1)S(1)} collective-permute-done((bf16[256,1024]{1,0:T(8,128)(2,1)S(1)}, bf16[256,1024]{1,0:T(8,128)(2,1)S(1)}, u32[]{:S(2)}, u32[]{:S(2)}) %collective-permute-start.14) | collective-permute-done | bytes 524320 | tf_op jit(solution)/shard_map/ppermute | solution.py:61
  180.6 39.4 %mlp.1 = (bf16[1024,2048]{1,0:T(8,128)(2,1)}, bf16[1024,1376]{1,0:T(8,128)(2,1)}, bf16[1024,1376]{1,0:T(8,128)(2,1)}, bf16[1024,1376]{1,0:T(8,128)(2,1)}, bf16[2...) custom-call(s32[2]{0:T(128)} %copy-done.37, ...), custom_call_target="tpu_custom_call" | custom-call | tf_op jit(solution)/shard_map/mlp/pallas_call | solution.py:32
  224.2 11.0 %collective-permute-done.19 = bf16[256,1024]{1,0:T(8,128)(2,1)S(1)} collective-permute-done((bf16[256,1024]{1,0:T(8,128)(2,1)}, bf16[256,1024]{1,0:T(8,128)(2,1)S(1)}, u32[]{:S(2)}, u32[]{:S(2)}) %collective-permute-start.19) | collective-permute-done | bytes 524320 | tf_op jit(solution)/shard_map/ppermute | solution.py:61
  240.4 8.0 %convolution_convert_fusion.2 = bf16[1376,2048]{1,0:T(8,128)(2,1)} fusion(bf16[1024,1376]{1,0:T(8,128)(2,1)S(1)} %copy-done.48, bf16[1024,2048]{1,0:T(8,128)(2,1)S(1)} %copy-done.42), kind=kOutput, calls=%fused_computation.2 | convolution fusion | flops 5774180352 | bytes 12648448 | tf_op jit(solution)/shard_map/dot_general | solution.py:24
  248.3 10.3 %convolution_convert_fusion.1 = bf16[1376,2048]{1,0:T(8,128)(2,1)} fusion(bf16[1024,1376]{1,0:T(8,128)(2,1)} %get-tuple-element.176, bf16[1024,2048]{1,0:T(8,128)(2,1)} %get-tuple-element.177), kind=kOutput, calls=%fused_computation.1 | convolution fusion | flops 5774180352 | bytes 12648448 | tf_op jit(solution)/shard_map/dot_general | solution.py:24
  262.3 6.2 d_mid.1
  272.5 10.8 %collective-permute-done.25.refs_3_ = bf16[256,1024]{1,0:T(8,128)(2,1)S(1)} collective-permute-done((bf16[256,1024]{1,0:T(8,128)(2,1)S(1)}, bf16[256,1024]{1,0:T(8,128)(2,1)S(1)}, u32[]{:S(2)}, u32[]{:S(2)}) %collective-permute-start.25) | collective-permute-done | bytes 524320 | tf_op jit(solution)/shard_map/ppermute | solution.py:61
  286.3 8.2 %convolution_convert_fusion = bf16[1376,2048]{1,0:T(8,128)(2,1)} fusion(bf16[1024,1376]{1,0:T(8,128)(2,1)S(1)} %copy-done.59, bf16[1024,2048]{1,0:T(8,128)(2,1)S(1)} %copy-done.57), kind=kOutput, calls=%fused_computation | convolution fusion | flops 5774180352 | bytes 12648448 | tf_op jit(solution)/shard_map/dot_general | solution.py:24
  294.5 11.1 %project_down.1 = (bf16[256,1024]{1,0:T(8,128)(2,1)S(1)}, bf16[256,1024]{1,0:T(8,128)(2,1)S(1)}, bf16[256,1024]{1,0:T(8,128)(2,1)S(1)}, bf16[256,1024]{1,0:T(8,1...) custom-call(s32[2]{0:T(128)S(1)} %copy-done.38, ...), custom_call_target="tpu_custom_call" | custom-call | tf_op jit(solution)/shard_map/project_down/pallas_call | solution.py:32
  307.8 6.5 %project_back.1 = (bf16[1024,2048]{1,0:T(8,128)(2,1)}, bf16[1024,512]{1,0:T(8,128)(2,1)S(1)}) custom-call(s32[2]{0:T(128)S(1)} %copy-done.38, bf16[256,1024]{1,0:T(8,128)(2,1)S(1)} %get-tuple-element.201.refs_1_, bf16[256,1024]{1,0:T(8,128)(2,1)} %collective-permute-done.24.refs_2_, bf16[256,1024]{1,0:T(8,128)(2,1)S(1)} %collective-permute-done.25.refs_3_, ...), custom_call_target="tpu_custom_call" | custom-call | tf_op jit(solution)/shard_map/project_back/pallas_call | solution.py:32
  317.2 26.2 %attend_back.2 = (bf16[1024,256]{1,0:T(8,128)(2,1)S(1)}, bf16[2,1024,256]{2,1,0:T(8,128)(2,1)S(1)}, bf16[2,1024,256]{2,1,0:T(8,128)(2,1)S(1)}, bf16[2,1024,256]{2,1,0:T(8,128)(2,1)S(1)}) custom-call(s32[2]{0:T(128)S(1)} %copy-done.38, bf16[1024,512]{1,0:T(8,128)(2,1)} %copy-done, bf16[2,1024,256]{2,1,0:T(8,128)(2,1)} %collective-permute-done.refs_2_, ...), custom_call_target="tpu_custom_call" | custom-call | tf_op jit(solution)/shard_map/attend_back/pallas_call | solution.py:32
  354.3 11.0 %collective-permute-done.30.refs_2_ = bf16[256,1024]{1,0:T(8,128)(2,1)} collective-permute-done((bf16[256,1024]{1,0:T(8,128)(2,1)}, bf16[256,1024]{1,0:T(8,128)(2,1)}, u32[]{:S(2)}, u32[]{:S(2)}) %collective-permute-start.30) | collective-permute-done | bytes 524320 | tf_op jit(solution)/shard_map/ppermute | solution.py:61
  366.1 10.5 %collective-permute-done.33.refs_3_ = bf16[256,1024]{1,0:T(8,128)(2,1)} collective-permute-done((bf16[256,1024]{1,0:T(8,128)(2,1)}, bf16[256,1024]{1,0:T(8,128)(2,1)}, u32[]{:S(2)}, u32[]{:S(2)}) %collective-permute-start.33) | collective-permute-done | bytes 524320 | tf_op jit(solution)/shard_map/ppermute | solution.py:61
  377.6 3.2 output.1
  381.1 25.9 %attend_back.3 = (bf16[1024,256]{1,0:T(8,128)(2,1)S(1)}, bf16[2,1024,256]{2,1,0:T(8,128)(2,1)S(1)}, bf16[2,1024,256]{2,1,0:T(8,128)(2,1)S(1)}, bf16[2,1024,256]{2,1,0:T(8,128)(2,1)S(1)}) custom-call(s32[2]{0:T(128)S(1)} %copy-done.38, bf16[1024,512]{1,0:T(8,128)(2,1)} %copy-done, bf16[2,1024,256]{2,1,0:T(8,128)(2,1)} %collective-permute-done.3.refs_2_, ...), custom_call_target="tpu_custom_call" | custom-call | tf_op jit(solution)/shard_map/attend_back/pallas_call | solution.py:32
  412.1 48.3 %collective-permute-done.44.back_ref = bf16[2,1024,256]{2,1,0:T(8,128)(2,1)S(1)} collective-permute-done((bf16[2,1024,256]{2,1,0:T(8,128)(2,1)S(1)}, bf16[2,1024,256]{2,1,0:T(8,128)(2,1)S(1)}, u32[]{:S(2)}, u32[]{:S(2)}) %collective-permute-start.44) | collective-permute-done | bytes 1048608 | tf_op jit(solution)/shard_map/ppermute | solution.py:797
  466.3 10.7 %collective-permute-done.36.refs_2_ = bf16[256,1024]{1,0:T(8,128)(2,1)S(1)} collective-permute-done((bf16[256,1024]{1,0:T(8,128)(2,1)S(1)}, bf16[256,1024]{1,0:T(8,128)(2,1)S(1)}, u32[]{:S(2)}, u32[]{:S(2)}) %collective-permute-start.36) | collective-permute-done | bytes 524320 | tf_op jit(solution)/shard_map/ppermute | solution.py:61
  478.3 9.2 %collective-permute-done.38.refs_4_ = bf16[256,1024]{1,0:T(8,128)(2,1)S(1)} collective-permute-done((bf16[256,1024]{1,0:T(8,128)(2,1)S(1)}, bf16[256,1024]{1,0:T(8,128)(2,1)S(1)}, u32[]{:S(2)}, u32[]{:S(2)}) %collective-permute-start.38) | collective-permute-done | bytes 524320 | tf_op jit(solution)/shard_map/ppermute | solution.py:61
  488.5 3.0 place.3
  494.3 3.9 collective-permute-done.45.back_ref
  502.7 2.9 finish.3.refs_1_
  505.6 15.4 %project_one_back.1 = (f32[1,2048]{1,0:T(1,128)S(1)}, bf16[256,1024]{1,0:T(8,128)(2,1)S(1)}, bf16[256,1024]{1,0:T(8,128)(2,1)S(1)}, bf16[256,1024]{1,0:T(8,128)(...) custom-call(s32[2]{0:T(128)S(1)} %copy-done.38, ...), custom_call_target="tpu_custom_call" | custom-call | tf_op jit(solution)/shard_map/project_one_back/pallas_call | solution.py:32
  523.9 10.8 %collective-permute-done.47 = bf16[256,1024]{1,0:T(8,128)(2,1)S(1)} collective-permute-done((bf16[256,1024]{1,0:T(8,128)(2,1)S(1)}, bf16[256,1024]{1,0:T(8,128)(2,1)S(1)}, u32[]{:S(2)}, u32[]{:S(2)}) %collective-permute-start.47) | collective-permute-done | bytes 524320 | tf_op jit(solution)/shard_map/ppermute | solution.py:61
  536.9 5.0 convolution_convert_fusion.3
  543.3 7.4 %convolution_convert_fusion.4 = bf16[2048,768]{1,0:T(8,128)(2,1)} fusion(bf16[1024,2048]{1,0:T(8,128)(2,1)} %get-tuple-element.143.h_ref, bf16[1024,768]{1,0:T(8,128)(2,1)S(1)} %copy-done.4), kind=kOutput, calls=%fused_computation.4 | convolution fusion | flops 3222798336 | bytes 8912896 | tf_op jit(solution)/shard_map/dot_general | solution.py:24
  563.0 9.1 %collective-permute-done.46.refs_4_ = bf16[256,1024]{1,0:T(8,128)(2,1)S(1)} collective-permute-done((bf16[256,1024]{1,0:T(8,128)(2,1)}, bf16[256,1024]{1,0:T(8,128)(2,1)S(1)}, u32[]{:S(2)}, u32[]{:S(2)}) %collective-permute-start.46) | collective-permute-done | bytes 524320 | tf_op jit(solution)/shard_map/ppermute | solution.py:61
  573.5 7.0 %collective-permute-done.49.refs_5_ = bf16[256,1024]{1,0:T(8,128)(2,1)S(1)} collective-permute-done((bf16[256,1024]{1,0:T(8,128)(2,1)}, bf16[256,1024]{1,0:T(8,128)(2,1)S(1)}, u32[]{:S(2)}, u32[]{:S(2)}) %collective-permute-start.49) | collective-permute-done | bytes 524320 | tf_op jit(solution)/shard_map/ppermute | solution.py:61
  581.2 5.5 input.1
  594.5 7.4 %collective-permute-done.55.refs_3_ = bf16[256,1024]{1,0:T(8,128)(2,1)} collective-permute-done((bf16[256,1024]{1,0:T(8,128)(2,1)}, bf16[256,1024]{1,0:T(8,128)(2,1)}, u32[]{:S(2)}, u32[]{:S(2)}) %collective-permute-start.55) | collective-permute-done | bytes 524320 | tf_op jit(solution)/shard_map/ppermute | solution.py:61
  607.1 6.0 collective-permute-done.62
  614.5 5.5 place.4.refs_3_
  623.3 8.2 %reduce-scatter.13.cloned.1.call-done = bf16[256,768]{1,0:T(8,128)(2,1)} async-done(((bf16[2048,768]{1,0:T(8,128)(2,1)}), bf16[256,768]{1,0:T(8,128)(2,1)}) %reduce-scatter.13.cloned.1.call-update) | async-done | bytes 393232 | tf_op jit(solution)/shard_map/reduce_scatter | solution.py:705
  (288 shorter events, 129.7 us)
Async XLA Ops:
  7.2 492.0 %reduce-scatter.7.cloned.1.call-start = ((), (), s32[]{:S(2)}) async-start(), calls=%async_computation.6 | async-start | bytes 6340608 | tf_op jit(solution)/shard_map/reduce_scatter | solution.py:705
  20.8 28.1 %collective-permute-start = (bf16[2,1024,256]{2,1,0:T(8,128)(2,1)}, bf16[2,1024,256]{2,1,0:T(8,128)(2,1)}, u32[]{:S(2)}, u32[]{:S(2)}) collective-permute-start(bf16[2,1024,256]{2,1,0:T(8,128)(2,1)} %get-tuple-element.144.refs_5_), channel_id=1, source_target_pairs={{0,8},{4,12},{8,16},{12,20},{16,24},{20,28},{1,9},{5,13},{9,17},{1... | collective-permute-start | bytes 3145736 | tf_op jit(solution)/shard_map/ppermute | solution.py:742
  26.7 33.1 %collective-permute-start.1 = (bf16[2,1024,256]{2,1,0:T(8,128)(2,1)}, bf16[2,1024,256]{2,1,0:T(8,128)(2,1)}, u32[]{:S(2)}, u32[]{:S(2)}) collective-permute-start(bf16[2,1024,256]{2,1,0:T(8,128)(2,1)} %get-tuple-element.144.refs_5_), channel_id=1, source_target_pairs={{0,4},{8,12},{16,20},{24,28},{1,5},{9,13},{17,21},{25,29},{2,6},{1... | collective-permute-start | bytes 3145736 | tf_op jit(solution)/shard_map/ppermute | solution.py:743
  50.2 26.3 %collective-permute-start.3 = (bf16[2,1024,256]{2,1,0:T(8,128)(2,1)S(1)}, bf16[2,1024,256]{2,1,0:T(8,128)(2,1)}, u32[]{:S(2)}, u32[]{:S(2)}) collective-permute-start(bf16[2,1024,256]{2,1,0:T(8,128)(2,1)S(1)} %get-tuple-element.148.refs_5_), channel_id=1, source_target_pairs={{0,8},{4,12},{8,16},{12,20},{16,24},{20,28},{1,9},{5,13},{9,17},{1... | collective-permute-start | bytes 3145736 | tf_op jit(solution)/shard_map/ppermute | solution.py:742
  55.1 22.8 %collective-permute-start.4 = (bf16[2,1024,256]{2,1,0:T(8,128)(2,1)S(1)}, bf16[2,1024,256]{2,1,0:T(8,128)(2,1)}, u32[]{:S(2)}, u32[]{:S(2)}) collective-permute-start(bf16[2,1024,256]{2,1,0:T(8,128)(2,1)S(1)} %get-tuple-element.148.refs_5_), channel_id=1, source_target_pairs={{0,4},{8,12},{16,20},{24,28},{1,5},{9,13},{17,21},{25,29},{2,6},{1... | collective-permute-start | bytes 3145736 | tf_op jit(solution)/shard_map/ppermute | solution.py:743
  104.7 23.0 %collective-permute-start.6 = (bf16[256,1024]{1,0:T(8,128)(2,1)S(1)}, bf16[256,1024]{1,0:T(8,128)(2,1)S(1)}, u32[]{:S(2)}, u32[]{:S(2)}) collective-permute-start(bf16[256,1024]{1,0:T(8,128)(2,1)S(1)} %get-tuple-element.152), channel_id=1, source_target_pairs={{0,1},{1,0},{2,3},{3,2},{4,5},{5,4},{6,7},{7,6},{8,9},{9,8},{10,11... | collective-permute-start | bytes 1572872 | tf_op jit(solution)/shard_map/ppermute | solution.py:61
  105.2 24.0 %collective-permute-start.9 = (bf16[256,1024]{1,0:T(8,128)(2,1)S(1)}, bf16[256,1024]{1,0:T(8,128)(2,1)S(1)}, u32[]{:S(2)}, u32[]{:S(2)}) collective-permute-start(bf16[256,1024]{1,0:T(8,128)(2,1)S(1)} %get-tuple-element.156), channel_id=1, source_target_pairs={{0,2},{1,3},{2,0},{3,1},{4,6},{5,7},{6,4},{7,5},{8,10},{9,11},{10,... | collective-permute-start | bytes 1572872 | tf_op jit(solution)/shard_map/ppermute | solution.py:61
  116.6 22.7 %collective-permute-start.8 = (bf16[256,1024]{1,0:T(8,128)(2,1)S(1)}, bf16[256,1024]{1,0:T(8,128)(2,1)S(1)}, u32[]{:S(2)}, u32[]{:S(2)}) collective-permute-start(bf16[256,1024]{1,0:T(8,128)(2,1)S(1)} %add_convert_fusion.9), channel_id=1, source_target_pairs={{0,2},{1,3},{2,0},{3,1},{4,6},{5,7},{6,4},{7,5},{8,10},{9,11},{10,... | collective-permute-start | bytes 1572872 | tf_op jit(solution)/shard_map/ppermute | solution.py:61
  118.4 20.9 %collective-permute-start.11 = (bf16[256,1024]{1,0:T(8,128)(2,1)S(1)}, bf16[256,1024]{1,0:T(8,128)(2,1)S(1)}, u32[]{:S(2)}, u32[]{:S(2)}) collective-permute-start(bf16[256,1024]{1,0:T(8,128)(2,1)S(1)} %add_convert_fusion.8), channel_id=1, source_target_pairs={{0,1},{1,0},{2,3},{3,2},{4,5},{5,4},{6,7},{7,6},{8,9},{9,8},{10,11... | collective-permute-start | bytes 1572872 | tf_op jit(solution)/shard_map/ppermute | solution.py:61
  145.1 25.6 %collective-permute-start.12 = (bf16[256,1024]{1,0:T(8,128)(2,1)S(1)}, bf16[256,1024]{1,0:T(8,128)(2,1)S(1)}, u32[]{:S(2)}, u32[]{:S(2)}) collective-permute-start(bf16[256,1024]{1,0:T(8,128)(2,1)S(1)} %get-tuple-element.160.refs_1_), channel_id=1, source_target_pairs={{0,1},{1,0},{2,3},{3,2},{4,5},{5,4},{6,7},{7,6},{8,9},{9,8},{10,11... | collective-permute-start | bytes 1572872 | tf_op jit(solution)/shard_map/ppermute | solution.py:61
  146.6 24.1 %collective-permute-start.16 = (bf16[256,1024]{1,0:T(8,128)(2,1)S(1)}, bf16[256,1024]{1,0:T(8,128)(2,1)S(1)}, u32[]{:S(2)}, u32[]{:S(2)}) collective-permute-start(bf16[256,1024]{1,0:T(8,128)(2,1)S(1)} %get-tuple-element.161.refs_5_), channel_id=1, source_target_pairs={{0,2},{1,3},{2,0},{3,1},{4,6},{5,7},{6,4},{7,5},{8,10},{9,11},{10,... | collective-permute-start | bytes 1572872 | tf_op jit(solution)/shard_map/ppermute | solution.py:61
  157.9 21.7 %collective-permute-start.14 = (bf16[256,1024]{1,0:T(8,128)(2,1)S(1)}, bf16[256,1024]{1,0:T(8,128)(2,1)S(1)}, u32[]{:S(2)}, u32[]{:S(2)}) collective-permute-start(bf16[256,1024]{1,0:T(8,128)(2,1)S(1)} %collective-permute-done.13.refs_3_), channel_id=1, source_target_pairs={{0,1},{1,0},{2,3},{3,2},{4,5},{5,4},{6,7},{7,6},{8,9},{9,8},{10,11... | collective-permute-start | bytes 1572872 | tf_op jit(solution)/shard_map/ppermute | solution.py:61
  159.4 20.1 %collective-permute-start.17 = (bf16[256,1024]{1,0:T(8,128)(2,1)S(1)}, bf16[256,1024]{1,0:T(8,128)(2,1)S(1)}, u32[]{:S(2)}, u32[]{:S(2)}) collective-permute-start(bf16[256,1024]{1,0:T(8,128)(2,1)S(1)} %collective-permute-done.15.refs_6_), channel_id=1, source_target_pairs={{0,2},{1,3},{2,0},{3,1},{4,6},{5,7},{6,4},{7,5},{8,10},{9,11},{10,... | collective-permute-start | bytes 1572872 | tf_op jit(solution)/shard_map/ppermute | solution.py:61
  220.0 15.1 %collective-permute-start.19 = (bf16[256,1024]{1,0:T(8,128)(2,1)}, bf16[256,1024]{1,0:T(8,128)(2,1)S(1)}, u32[]{:S(2)}, u32[]{:S(2)}) collective-permute-start(bf16[256,1024]{1,0:T(8,128)(2,1)} %get-tuple-element.165), channel_id=1, source_target_pairs={{0,2},{1,3},{2,0},{3,1},{4,6},{5,7},{6,4},{7,5},{8,10},{9,11},{10,... | collective-permute-start | bytes 1572872 | tf_op jit(solution)/shard_map/ppermute | solution.py:61
  220.6 16.6 %collective-permute-start.20 = (bf16[256,1024]{1,0:T(8,128)(2,1)}, bf16[256,1024]{1,0:T(8,128)(2,1)S(1)}, u32[]{:S(2)}, u32[]{:S(2)}) collective-permute-start(bf16[256,1024]{1,0:T(8,128)(2,1)} %get-tuple-element.167), channel_id=1, source_target_pairs={{0,1},{1,0},{2,3},{3,2},{4,5},{5,4},{6,7},{7,6},{8,9},{9,8},{10,11... | collective-permute-start | bytes 1572872 | tf_op jit(solution)/shard_map/ppermute | solution.py:61
  221.2 37.4 %collective-permute-start.18 = (bf16[256,1024]{1,0:T(8,128)(2,1)}, bf16[256,1024]{1,0:T(8,128)(2,1)S(1)}, u32[]{:S(2)}, u32[]{:S(2)}) collective-permute-start(bf16[256,1024]{1,0:T(8,128)(2,1)} %get-tuple-element.163), channel_id=1, source_target_pairs={{0,1},{1,0},{2,3},{3,2},{4,5},{5,4},{6,7},{7,6},{8,9},{9,8},{10,11... | collective-permute-start | bytes 1572872 | tf_op jit(solution)/shard_map/ppermute | solution.py:61
  222.7 36.0 %collective-permute-start.22 = (bf16[256,1024]{1,0:T(8,128)(2,1)}, bf16[256,1024]{1,0:T(8,128)(2,1)S(1)}, u32[]{:S(2)}, u32[]{:S(2)}) collective-permute-start(bf16[256,1024]{1,0:T(8,128)(2,1)} %get-tuple-element.172), channel_id=1, source_target_pairs={{0,2},{1,3},{2,0},{3,1},{4,6},{5,7},{6,4},{7,5},{8,10},{9,11},{10,... | collective-permute-start | bytes 1572872 | tf_op jit(solution)/shard_map/ppermute | solution.py:61
  239.2 19.4 %collective-permute-start.21 = (bf16[256,1024]{1,0:T(8,128)(2,1)}, bf16[256,1024]{1,0:T(8,128)(2,1)}, u32[]{:S(2)}, u32[]{:S(2)}) collective-permute-start(bf16[256,1024]{1,0:T(8,128)(2,1)} %add_convert_fusion.6), channel_id=1, source_target_pairs={{0,2},{1,3},{2,0},{3,1},{4,6},{5,7},{6,4},{7,5},{8,10},{9,11},{10,... | collective-permute-start | bytes 1572872 | tf_op jit(solution)/shard_map/ppermute | solution.py:61
  239.8 18.9 %collective-permute-start.23 = (bf16[256,1024]{1,0:T(8,128)(2,1)}, bf16[256,1024]{1,0:T(8,128)(2,1)}, u32[]{:S(2)}, u32[]{:S(2)}) collective-permute-start(bf16[256,1024]{1,0:T(8,128)(2,1)} %add_convert_fusion.7), channel_id=1, source_target_pairs={{0,1},{1,0},{2,3},{3,2},{4,5},{5,4},{6,7},{7,6},{8,9},{9,8},{10,11... | collective-permute-start | bytes 1572872 | tf_op jit(solution)/shard_map/ppermute | solution.py:61
  258.7 302.4 %reduce-scatter.17.cloned.1.call-start = ((), (), s32[]{:S(2)}) async-start(), calls=%async_computation.11 | async-start | bytes 2359296 | tf_op jit(solution)/shard_map/reduce_scatter | solution.py:705
  271.4 34.2 %collective-permute-start.24 = (bf16[256,1024]{1,0:T(8,128)(2,1)S(1)}, bf16[256,1024]{1,0:T(8,128)(2,1)}, u32[]{:S(2)}, u32[]{:S(2)}) collective-permute-start(bf16[256,1024]{1,0:T(8,128)(2,1)S(1)} %get-tuple-element.201.refs_1_), channel_id=1, source_target_pairs={{0,1},{1,0},{2,3},{3,2},{4,5},{5,4},{6,7},{7,6},{8,9},{9,8},{10,11... | collective-permute-start | bytes 1572872 | tf_op jit(solution)/shard_map/ppermute | solution.py:61
  272.0 33.6 %collective-permute-start.28 = (bf16[256,1024]{1,0:T(8,128)(2,1)S(1)}, bf16[256,1024]{1,0:T(8,128)(2,1)}, u32[]{:S(2)}, u32[]{:S(2)}) collective-permute-start(bf16[256,1024]{1,0:T(8,128)(2,1)S(1)} %get-tuple-element.205.refs_5_), channel_id=1, source_target_pairs={{0,2},{1,3},{2,0},{3,1},{4,6},{5,7},{6,4},{7,5},{8,10},{9,11},{10,... | collective-permute-start | bytes 1572872 | tf_op jit(solution)/shard_map/ppermute | solution.py:61
  283.4 22.3 %collective-permute-start.26 = (bf16[256,1024]{1,0:T(8,128)(2,1)S(1)}, bf16[256,1024]{1,0:T(8,128)(2,1)}, u32[]{:S(2)}, u32[]{:S(2)}) collective-permute-start(bf16[256,1024]{1,0:T(8,128)(2,1)S(1)} %collective-permute-done.25.refs_3_), channel_id=1, source_target_pairs={{0,1},{1,0},{2,3},{3,2},{4,5},{5,4},{6,7},{7,6},{8,9},{9,8},{10,11... | collective-permute-start | bytes 1572872 | tf_op jit(solution)/shard_map/ppermute | solution.py:61
  284.9 20.8 %collective-permute-start.29 = (bf16[256,1024]{1,0:T(8,128)(2,1)S(1)}, bf16[256,1024]{1,0:T(8,128)(2,1)}, u32[]{:S(2)}, u32[]{:S(2)}) collective-permute-start(bf16[256,1024]{1,0:T(8,128)(2,1)S(1)} %collective-permute-done.27.refs_6_), channel_id=1, source_target_pairs={{0,2},{1,3},{2,0},{3,1},{4,6},{5,7},{6,4},{7,5},{8,10},{9,11},{10,... | collective-permute-start | bytes 1572872 | tf_op jit(solution)/shard_map/ppermute | solution.py:61
  348.5 214.4 %reduce-scatter.9.cloned.1.call-start = ((), (), s32[]{:S(2)}) async-start(), calls=%async_computation.7 | async-start | bytes 6340608 | tf_op jit(solution)/shard_map/reduce_scatter | solution.py:705
  349.3 255.5 %reduce-scatter.11.cloned.1.call-start = ((), (), s32[]{:S(2)}) async-start(), calls=%async_computation.8 | async-start | bytes 6340608 | tf_op jit(solution)/shard_map/reduce_scatter | solution.py:705
  349.9 272.4 %reduce-scatter.15.cloned.1.call-start = ((), (), s32[]{:S(2)}) async-start(), calls=%async_computation.10 | async-start | bytes 3538944 | tf_op jit(solution)/shard_map/reduce_scatter | solution.py:705
  350.1 30.6 %collective-permute-start.42 = (bf16[2,1024,256]{2,1,0:T(8,128)(2,1)}, bf16[2,1024,256]{2,1,0:T(8,128)(2,1)S(1)}, u32[]{:S(2)}, u32[]{:S(2)}) collective-permute-start(bf16[2,1024,256]{2,1,0:T(8,128)(2,1)} %copy-done.43), channel_id=1, source_target_pairs={{0,4},{4,0},{8,12},{12,8},{16,20},{20,16},{24,28},{28,24},{1,5},{5... | collective-permute-start | bytes 3145736 | tf_op jit(solution)/shard_map/ppermute | solution.py:61
  350.2 15.1 %collective-permute-start.30 = (bf16[256,1024]{1,0:T(8,128)(2,1)}, bf16[256,1024]{1,0:T(8,128)(2,1)}, u32[]{:S(2)}, u32[]{:S(2)}) collective-permute-start(bf16[256,1024]{1,0:T(8,128)(2,1)} %copy-done.45), channel_id=1, source_target_pairs={{0,1},{1,0},{2,3},{3,2},{4,5},{5,4},{6,7},{7,6},{8,9},{9,8},{10,11... | collective-permute-start | bytes 1572872 | tf_op jit(solution)/shard_map/ppermute | solution.py:61
  351.0 15.1 %collective-permute-start.34 = (bf16[256,1024]{1,0:T(8,128)(2,1)}, bf16[256,1024]{1,0:T(8,128)(2,1)}, u32[]{:S(2)}, u32[]{:S(2)}) collective-permute-start(bf16[256,1024]{1,0:T(8,128)(2,1)} %copy-done.44), channel_id=1, source_target_pairs={{0,2},{1,3},{2,0},{3,1},{4,6},{5,7},{6,4},{7,5},{8,10},{9,11},{10,... | collective-permute-start | bytes 1572872 | tf_op jit(solution)/shard_map/ppermute | solution.py:61
  352.2 24.3 %collective-permute-start.33 = (bf16[256,1024]{1,0:T(8,128)(2,1)}, bf16[256,1024]{1,0:T(8,128)(2,1)}, u32[]{:S(2)}, u32[]{:S(2)}) collective-permute-start(bf16[256,1024]{1,0:T(8,128)(2,1)} %add_convert_fusion.4), channel_id=1, source_target_pairs={{0,2},{1,3},{2,0},{3,1},{4,6},{5,7},{6,4},{7,5},{8,10},{9,11},{10,... | collective-permute-start | bytes 1572872 | tf_op jit(solution)/shard_map/ppermute | solution.py:61
  353.0 23.5 %collective-permute-start.35 = (bf16[256,1024]{1,0:T(8,128)(2,1)}, bf16[256,1024]{1,0:T(8,128)(2,1)}, u32[]{:S(2)}, u32[]{:S(2)}) collective-permute-start(bf16[256,1024]{1,0:T(8,128)(2,1)} %add_convert_fusion.5), channel_id=1, source_target_pairs={{0,1},{1,0},{2,3},{3,2},{4,5},{5,4},{6,7},{7,6},{8,9},{9,8},{10,11... | collective-permute-start | bytes 1572872 | tf_op jit(solution)/shard_map/ppermute | solution.py:61
  408.8 51.6 %collective-permute-start.44 = (bf16[2,1024,256]{2,1,0:T(8,128)(2,1)S(1)}, bf16[2,1024,256]{2,1,0:T(8,128)(2,1)S(1)}, u32[]{:S(2)}, u32[]{:S(2)}) collective-permute-start(bf16[2,1024,256]{2,1,0:T(8,128)(2,1)S(1)} %add_convert_fusion.1), channel_id=1, source_target_pairs={{8,0},{12,4},{16,8},{20,12},{24,16},{28,20},{9,1},{13,5},{17,9},{2... | collective-permute-start | bytes 3145736 | tf_op jit(solution)/shard_map/ppermute | solution.py:797
  410.1 54.1 %collective-permute-start.37 = (bf16[256,1024]{1,0:T(8,128)(2,1)S(1)}, bf16[256,1024]{1,0:T(8,128)(2,1)S(1)}, u32[]{:S(2)}, u32[]{:S(2)}) collective-permute-start(bf16[256,1024]{1,0:T(8,128)(2,1)S(1)} %get-tuple-element.218.refs_1_), channel_id=1, source_target_pairs={{0,2},{1,3},{2,0},{3,1},{4,6},{5,7},{6,4},{7,5},{8,10},{9,11},{10,... | collective-permute-start | bytes 1572872 | tf_op jit(solution)/shard_map/ppermute | solution.py:61
  411.3 54.1 %collective-permute-start.39 = (bf16[256,1024]{1,0:T(8,128)(2,1)S(1)}, bf16[256,1024]{1,0:T(8,128)(2,1)S(1)}, u32[]{:S(2)}, u32[]{:S(2)}) collective-permute-start(bf16[256,1024]{1,0:T(8,128)(2,1)S(1)} %get-tuple-element.219.refs_5_), channel_id=1, source_target_pairs={{0,1},{1,0},{2,3},{3,2},{4,5},{5,4},{6,7},{7,6},{8,9},{9,8},{10,11... | collective-permute-start | bytes 1572872 | tf_op jit(solution)/shard_map/ppermute | solution.py:61
  460.7 37.5 %collective-permute-start.45 = (bf16[2,1024,256]{2,1,0:T(8,128)(2,1)S(1)}, bf16[2,1024,256]{2,1,0:T(8,128)(2,1)S(1)}, u32[]{:S(2)}, u32[]{:S(2)}) collective-permute-start(bf16[2,1024,256]{2,1,0:T(8,128)(2,1)S(1)} %add_convert_fusion), channel_id=1, source_target_pairs={{8,0},{12,4},{16,8},{20,12},{24,16},{28,20},{9,1},{13,5},{17,9},{2... | collective-permute-start | bytes 3145736 | tf_op jit(solution)/shard_map/ppermute | solution.py:801
  464.2 23.3 %collective-permute-start.38 = (bf16[256,1024]{1,0:T(8,128)(2,1)S(1)}, bf16[256,1024]{1,0:T(8,128)(2,1)S(1)}, u32[]{:S(2)}, u32[]{:S(2)}) collective-permute-start(bf16[256,1024]{1,0:T(8,128)(2,1)S(1)} %collective-permute-done.37.refs_3_), channel_id=1, source_target_pairs={{0,1},{1,0},{2,3},{3,2},{4,5},{5,4},{6,7},{7,6},{8,9},{9,8},{10,11... | collective-permute-start | bytes 1572872 | tf_op jit(solution)/shard_map/ppermute | solution.py:61
  465.5 23.0 %collective-permute-start.41 = (bf16[256,1024]{1,0:T(8,128)(2,1)S(1)}, bf16[256,1024]{1,0:T(8,128)(2,1)S(1)}, u32[]{:S(2)}, u32[]{:S(2)}) collective-permute-start(bf16[256,1024]{1,0:T(8,128)(2,1)S(1)} %collective-permute-done.39.refs_6_), channel_id=1, source_target_pairs={{0,2},{1,3},{2,0},{3,1},{4,6},{5,7},{6,4},{7,5},{8,10},{9,11},{10,... | collective-permute-start | bytes 1572872 | tf_op jit(solution)/shard_map/ppermute | solution.py:61
  541.9 89.6 %reduce-scatter.13.cloned.1.call-start = ((), (), s32[]{:S(2)}) async-start(), calls=%async_computation.9 | async-start | bytes 3538944 | tf_op jit(solution)/shard_map/reduce_scatter | solution.py:705
  559.8 20.8 %collective-permute-start.49 = (bf16[256,1024]{1,0:T(8,128)(2,1)}, bf16[256,1024]{1,0:T(8,128)(2,1)S(1)}, u32[]{:S(2)}, u32[]{:S(2)}) collective-permute-start(bf16[256,1024]{1,0:T(8,128)(2,1)} %add_convert_fusion.2), channel_id=1, source_target_pairs={{0,2},{1,3},{2,0},{3,1},{4,6},{5,7},{6,4},{7,5},{8,10},{9,11},{10,... | collective-permute-start | bytes 1572872 | tf_op jit(solution)/shard_map/ppermute | solution.py:61
  560.5 20.1 %collective-permute-start.51 = (bf16[256,1024]{1,0:T(8,128)(2,1)}, bf16[256,1024]{1,0:T(8,128)(2,1)S(1)}, u32[]{:S(2)}, u32[]{:S(2)}) collective-permute-start(bf16[256,1024]{1,0:T(8,128)(2,1)} %add_convert_fusion.3), channel_id=1, source_target_pairs={{0,1},{1,0},{2,3},{3,2},{4,5},{5,4},{6,7},{7,6},{8,9},{9,8},{10,11... | collective-permute-start | bytes 1572872 | tf_op jit(solution)/shard_map/ppermute | solution.py:61
  586.7 15.2 %collective-permute-start.55 = (bf16[256,1024]{1,0:T(8,128)(2,1)}, bf16[256,1024]{1,0:T(8,128)(2,1)}, u32[]{:S(2)}, u32[]{:S(2)}) collective-permute-start(bf16[256,1024]{1,0:T(8,128)(2,1)} %get-tuple-element.267.refs_1_), channel_id=1, source_target_pairs={{0,2},{1,3},{2,0},{3,1},{4,6},{5,7},{6,4},{7,5},{8,10},{9,11},{10,... | collective-permute-start | bytes 1572872 | tf_op jit(solution)/shard_map/ppermute | solution.py:61
  588.1 15.2 %collective-permute-start.57 = (bf16[256,1024]{1,0:T(8,128)(2,1)}, bf16[256,1024]{1,0:T(8,128)(2,1)}, u32[]{:S(2)}, u32[]{:S(2)}) collective-permute-start(bf16[256,1024]{1,0:T(8,128)(2,1)} %get-tuple-element.270.refs_4_), channel_id=1, source_target_pairs={{0,1},{1,0},{2,3},{3,2},{4,5},{5,4},{6,7},{7,6},{8,9},{9,8},{10,11... | collective-permute-start | bytes 1572872 | tf_op jit(solution)/shard_map/ppermute | solution.py:61
  592.0 22.5 %collective-permute-start.59 = (bf16[256,1024]{1,0:T(8,128)(2,1)}, bf16[256,1024]{1,0:T(8,128)(2,1)}, u32[]{:S(2)}, u32[]{:S(2)}) collective-permute-start(bf16[256,1024]{1,0:T(8,128)(2,1)} %get-tuple-element.267.refs_1_), channel_id=1, source_target_pairs={{0,1},{1,0},{2,3},{3,2},{4,5},{5,4},{6,7},{7,6},{8,9},{9,8},{10,11... | collective-permute-start | bytes 1572872 | tf_op jit(solution)/shard_map/ppermute | solution.py:61
  592.5 22.0 %collective-permute-start.60 = (bf16[256,1024]{1,0:T(8,128)(2,1)}, bf16[256,1024]{1,0:T(8,128)(2,1)}, u32[]{:S(2)}, u32[]{:S(2)}) collective-permute-start(bf16[256,1024]{1,0:T(8,128)(2,1)} %get-tuple-element.270.refs_4_), channel_id=1, source_target_pairs={{0,2},{1,3},{2,0},{3,1},{4,6},{5,7},{6,4},{7,5},{8,10},{9,11},{10,... | collective-permute-start | bytes 1572872 | tf_op jit(solution)/shard_map/ppermute | solution.py:61
  593.2 20.0 %collective-permute-start.62 = (f32[2,256]{1,0:T(2,128)S(1)}, f32[2,256]{1,0:T(2,128)S(1)}, u32[]{:S(2)}, u32[]{:S(2)}) collective-permute-start(f32[2,256]{1,0:T(2,128)S(1)} %add.126), channel_id=1, source_target_pairs={{0,2},{1,3},{2,0},{3,1},{4,6},{5,7},{6,4},{7,5},{8,10},{9,11},{10,... | collective-permute-start | bytes 6152 | tf_op jit(solution)/shard_map/ppermute | solution.py:61
  601.9 18.4 %collective-permute-start.56 = (bf16[256,1024]{1,0:T(8,128)(2,1)}, bf16[256,1024]{1,0:T(8,128)(2,1)S(1)}, u32[]{:S(2)}, u32[]{:S(2)}) collective-permute-start(bf16[256,1024]{1,0:T(8,128)(2,1)} %collective-permute-done.55.refs_3_), channel_id=1, source_target_pairs={{0,1},{1,0},{2,3},{3,2},{4,5},{5,4},{6,7},{7,6},{8,9},{9,8},{10,11... | collective-permute-start | bytes 1572872 | tf_op jit(solution)/shard_map/ppermute | solution.py:61
  603.3 17.0 %collective-permute-start.58 = (bf16[256,1024]{1,0:T(8,128)(2,1)}, bf16[256,1024]{1,0:T(8,128)(2,1)S(1)}, u32[]{:S(2)}, u32[]{:S(2)}) collective-permute-start(bf16[256,1024]{1,0:T(8,128)(2,1)} %collective-permute-done.57.refs_5_), channel_id=1, source_target_pairs={{0,2},{1,3},{2,0},{3,1},{4,6},{5,7},{6,4},{7,5},{8,10},{9,11},{10,... | collective-permute-start | bytes 1572872 | tf_op jit(solution)/shard_map/ppermute | solution.py:61
  (81 other events, 1165.2 us)
Sparse Core Ops, SparseCore 0:
  258.8 65.6 reduce-scatter.6
  348.6 36.7 reduce-scatter.16
  388.4 89.9 reduce-scatter.8
  480.6 68.3 reduce-scatter.10
  551.2 38.5 reduce-scatter.14
  592.1 39.3 reduce-scatter.12

commit v3 on v2

--- a/solution.py
+++ b/solution.py
@@ -13,6 +13,7 @@
 F32 = jnp.float32
 BF16 = jnp.bfloat16
 MIB = 1024 * 1024
+STEPS = 4
 GROUPS = 2
 
 NN = (((1,), (0,)), ((), ()))
@@ -28,21 +29,26 @@
     return lax.optimization_barrier((values, after))[0]
 
 
-def call(body, grid, in_specs, out_specs, outs, args, name, scratch=(), flops=0, moved=0, exps=0, vmem=48):
+def call(body, grid, in_specs, out_specs, outs, args, name, scratch=(), vmem=48, into=(), weight=0):
+    count = len(args)
+    if into:
+        inner = body
+        body = lambda *refs: inner(*refs[:count], *refs[count + len(into) :])
     return pl.pallas_call(
         body,
         grid_spec=pltpu.PrefetchScalarGridSpec(
             num_scalar_prefetch=1,
             grid=grid,
-            in_specs=in_specs,
+            in_specs=list(in_specs) + [pl.BlockSpec(memory_space=pl.ANY)] * len(into),
             out_specs=out_specs,
             scratch_shapes=list(scratch),
         ),
+        input_output_aliases={count + k: k for k in range(len(into))},
         out_shape=[jax.ShapeDtypeStruct(shape, kind) for shape, kind in outs],
         compiler_params=pltpu.CompilerParams(vmem_limit_bytes=vmem * MIB),
-        cost_estimate=pl.CostEstimate(flops=0, bytes_accessed=0, transcendentals=0),
+        cost_estimate=pl.CostEstimate(flops=weight, bytes_accessed=0, transcendentals=0),
         name=name,
-    )(*args)
+    )(*args, *into)
 
 
 def fixed(shape):
@@ -130,7 +136,7 @@
     return [slice(h * HEAD, (h + 1) * HEAD) for h in range(width // HEAD)]
 
 
-def keys_kernel(me_ref, x_ref, gain_ref, wk_ref, wv_ref, cos_ref, sin_ref, h_ref, *kv_refs):
+def keys_kernel(me_ref, x_ref, gain_ref, wk_ref, wv_ref, cos_ref, sin_ref, h_ref, all_ref, *kv_refs):
     x = x_ref[...].astype(F32)
     factor = lax.rsqrt(jnp.mean(x * x, axis=-1, keepdims=True) + 1e-06)
     hidden = (x * factor * gain_ref[...]).astype(BF16)
@@ -143,6 +149,7 @@
         for cut in heads_of(width):
             kv_ref[0, :, cut] = rotated(key[:, cut], cosine, sine).astype(BF16)
         kv_ref[1] = mm(hidden, wv_ref[:, cols]).astype(BF16)
+        all_ref[2 * g : 2 * g + 2] = kv_ref[...]
 
 
 def project_keys(scal, x, gain, wk, wv, cosine, sine, n):
@@ -162,12 +169,11 @@
             pl.BlockSpec((rows, HEAD), mine),
         ],
         [pl.BlockSpec((rows, width), mine)]
+        + [pl.BlockSpec((2 * GROUPS, rows, part), lambda r, m: (0, r, 0))]
         + [pl.BlockSpec((2, rows, part), lambda r, m: (0, r, 0))] * GROUPS,
-        [((tokens, width), BF16)] + [((2, tokens, part), BF16)] * GROUPS,
+        [((tokens, width), BF16), ((2 * GROUPS, tokens, part), BF16)] + [((2, tokens, part), BF16)] * GROUPS,
         (scal, x, gain, wk, wv, cosine, sine),
         "project_keys",
-        flops=4 * tokens * width * local,
-        moved=4 * tokens * width + 4 * (tokens + width) * local,
     )
 
 
@@ -195,8 +201,6 @@
         [((tokens, local), BF16)],
         (scal, hidden, wq, cosine, sine),
         "project_query",
-        flops=2 * tokens * width * local,
-        moved=2 * tokens * width + 2 * (tokens + width) * local,
     )[0]
 
 
@@ -219,8 +223,6 @@
         [((tokens, width), BF16), ((tokens, hid), F32)],
         (scal, cot, w_down),
         "project_cotangent",
-        flops=2 * tokens * width * hid,
-        moved=4 * tokens * width + 4 * tokens * hid + 2 * width * hid,
     )
 
 
@@ -243,74 +245,85 @@
                 put(at, jnp.where(odd != 0, refs[0][which, here, :], refs[1][which, here, :]))
 
 
-def attend_kernel(n, s_ref_, q_ref, two_ref, odd_ref, even_ref, own_ref, low_ref, o_ref, lse_ref, s_ref, k_ref, vt_ref):
+def lanes(array):
+    return [array[:, j * HEAD : (j + 1) * HEAD] for j in range(array.shape[1] // HEAD)]
+
+
+def attend_kernel(n, at, s_ref_, q_ref, two_ref, odd_ref, even_ref, own_ref, low_ref, o_ref, lse_ref, s_ref, k_ref, v_ref):
     rows = q_ref.shape[0]
     me, odd = s_ref_[0], s_ref_[1]
-    r = pl.program_id(1)
-    rb = r ^ me
+    start = ((pl.program_id(1) + at) ^ me) * rows
     chunks = 2 * n + 1
 
-    @pl.when(r == 0)
+    @pl.when(pl.program_id(1) == 0)
     def _():
         def put_key(at, block):
             k_ref[at, :] = block
 
         def put_value(at, block):
-            vt_ref[:, at] = block.T
+            v_ref[at, :] = block
 
         window = (two_ref, odd_ref, even_ref, own_ref)
         lay_window(n, rows, me, odd, 0, *window, put_key)
         lay_window(n, rows, me, odd, 1, *window, put_value)
 
     q = q_ref[...]
-    low = low_ref[...]
-    query_at = (rb + 2 * n) * rows + lax.broadcasted_iota(jnp.int32, (1, rows), 1)
-    top = jnp.full((1, rows), NEG, F32)
+    low = low_ref[...] - start
+    low = jnp.concatenate([low] * (rows // HEAD), axis=1)
+    key_at = lax.broadcasted_iota(jnp.int32, (rows, rows), 1)
+    query_at = lax.broadcasted_iota(jnp.int32, (rows, rows), 0)
+    top = jnp.full((rows, HEAD), NEG, F32)
     for c in range(chunks):
-        first = pl.multiple_of((rb + c) * rows, rows)
-        s = mm(k_ref[pl.ds(first, rows), :], q, NT)
-        s = masked(s, first, low, query_at, c == chunks - 1)
-        s_ref[c * rows : (c + 1) * rows, :] = s
-        top = jnp.maximum(top, jnp.max(s, axis=0, keepdims=True))
-    top = top * (SCALE * LOG2E)
-    whole = jnp.zeros((1, rows), F32)
-    acc = jnp.zeros((HEAD, rows), F32)
+        here = pl.ds(pl.multiple_of(start + c * rows, rows), rows)
+        s = mm(q, k_ref[here, :], NT)
+        keep = key_at >= low - c * rows
+        if c == chunks - 1:
+            keep = keep & (key_at <= query_at)
+        s = jnp.where(keep, s, NEG)
+        s_ref[:, c * rows : (c + 1) * rows] = s
+        for lane in lanes(s):
+            top = jnp.maximum(top, lane)
+    top = jnp.max(top, axis=1, keepdims=True) * (SCALE * LOG2E)
+    whole = jnp.zeros((rows, HEAD), F32)
+    acc = jnp.zeros((rows, HEAD), F32)
     for c in range(chunks):
-        first = pl.multiple_of((rb + c) * rows, rows)
-        p = jnp.exp2(s_ref[c * rows : (c + 1) * rows, :] * (SCALE * LOG2E) - top)
-        whole = whole + jnp.sum(p, axis=0, keepdims=True)
-        acc = acc + mm(vt_ref[:, pl.ds(first, rows)], p.astype(BF16))
-    o_ref[...] = (acc / whole).T.astype(BF16)
-    lse_ref[...] = (top + jnp.log2(whole)).reshape(lse_ref.shape)
-
-
-def attend(scal, g, q, segments, low, n):
+        here = pl.ds(pl.multiple_of(start + c * rows, rows), rows)
+        p = jnp.exp2(s_ref[:, c * rows : (c + 1) * rows] * (SCALE * LOG2E) - top)
+        for lane in lanes(p):
+            whole = whole + lane
+        acc = acc + mm(p.astype(BF16), v_ref[here, :])
+    whole = jnp.sum(whole, axis=1, keepdims=True)
+    o_ref[...] = (acc / whole).astype(BF16)
+    lse = jnp.broadcast_to(top + jnp.log2(whole), (rows, HEAD)).T
+    lse_ref[...] = lse[:1, :].reshape(lse_ref.shape)
+
+
+def attend(scal, g, q, segments, low, n, at, count, into=()):
     tokens = q.shape[0]
     part = segments[0].shape[2]
     heads, rows = part // HEAD, tokens // n
     pairs = heads * tokens * (2 * tokens + rows)
     segment = pl.BlockSpec((2, tokens, HEAD), lambda h, r, m: (0, 0, h))
-    return call(
-        lambda *refs: attend_kernel(n, *refs),
-        (heads, n),
-        [pl.BlockSpec((rows, HEAD), lambda h, r, m: (r, g * heads + h))]
-        + [segment] * 4
-        + [pl.BlockSpec((1, rows), lambda h, r, m: (0, r))],
+    across = pl.BlockSpec((2, tokens, HEAD), lambda h, r, m: (g, 0, h))
+    return call(
+        lambda *refs: attend_kernel(n, at, *refs),
+        (heads, count),
+        [pl.BlockSpec((rows, HEAD), lambda h, r, m: (r + at, g * heads + h))]
+        + [segment, across, segment, segment]
+        + [pl.BlockSpec((rows, HEAD), lambda h, r, m: (r + at, 0))],
         [
-            pl.BlockSpec((rows, HEAD), lambda h, r, m: (r, h)),
-            pl.BlockSpec((1, 1, rows), lambda h, r, m: (h, 0, r)),
+            pl.BlockSpec((rows, HEAD), lambda h, r, m: (r + at, h)),
+            pl.BlockSpec((1, 1, rows), lambda h, r, m: (h, 0, r + at)),
         ],
         [((tokens, part), BF16), ((heads, 1, tokens), F32)],
         (scal, q, *segments, low),
         "attend",
         scratch=[
-            pltpu.VMEM(((2 * n + 1) * rows, rows), F32),
+            pltpu.VMEM((rows, (2 * n + 1) * rows), F32),
             pltpu.VMEM((3 * tokens, HEAD), BF16),
-            pltpu.VMEM((HEAD, 3 * tokens), BF16),
+            pltpu.VMEM((3 * tokens, HEAD), BF16),
         ],
-        flops=8 * pairs * HEAD,
-        moved=20 * tokens * part,
-        exps=pairs,
+        into=into,
     )
 
 
@@ -344,16 +357,18 @@
     lse = lse_ref[...].reshape(1, rows)
     delta = jnp.sum((do.astype(F32) * o_ref[...].astype(F32)).T, axis=0, keepdims=True)
     query_at = (rb + 2 * n) * rows + lax.broadcasted_iota(jnp.int32, (1, rows), 1)
-    dqt = jnp.zeros((HEAD, rows), F32)
+    steps = []
     for c in range(chunks):
         first = pl.multiple_of((rb + c) * rows, rows)
         here = pl.ds(first, rows)
         s = mm(k_ref[here, :], q, NT) * (SCALE * LOG2E)
         s = masked(s, first, low, query_at, c == chunks - 1)
         p = jnp.exp2(s - lse)
-        dv_acc[here, :] += mm(p.astype(BF16), do)
         dp = mm(v_ref[here, :], do, NT)
-        ds = (p * (dp - delta)).astype(BF16)
+        steps.append((here, p.astype(BF16), (p * (dp - delta)).astype(BF16)))
+    dqt = jnp.zeros((HEAD, rows), F32)
+    for here, p, ds in steps:
+        dv_acc[here, :] += mm(p, do)
         dk_acc[here, :] += mm(ds, q)
         dqt = dqt + mm(kt_ref[:, here], ds)
     dq_ref[...] = rotated(dqt.T * SCALE, cos_ref[...], -sin_ref[...]).astype(BF16)
@@ -376,12 +391,13 @@
     block = pl.BlockSpec((rows, HEAD), lambda h, r, m: (r, h))
     shared = pl.BlockSpec((rows, HEAD), lambda h, r, m: (r, g * heads + h))
     segment = pl.BlockSpec((2, tokens, HEAD), lambda h, r, m: (0, 0, h))
+    across = pl.BlockSpec((2, tokens, HEAD), lambda h, r, m: (g, 0, h))
     table = pl.BlockSpec((rows, HEAD), lambda h, r, m: (r, 0))
     return call(
         lambda *refs: attend_back_kernel(n, *refs),
         (heads, n),
         [shared]
-        + [segment] * 4
+        + [segment, across, segment, segment]
         + [
             pl.BlockSpec((1, rows), lambda h, r, m: (0, r)),
             block,
@@ -394,6 +410,7 @@
         [((tokens, part), BF16)] + [((2, tokens, part), BF16)] * 3,
         (scal, q, *segments, low, attended, d_attended, lse, cosine, sine),
         "attend_back",
+        weight=69_000_000_000,
         scratch=[
             pltpu.VMEM((3 * tokens, HEAD), F32),
             pltpu.VMEM((3 * tokens, HEAD), F32),
@@ -401,9 +418,6 @@
             pltpu.VMEM((HEAD, 3 * tokens), BF16),
             pltpu.VMEM((3 * tokens, HEAD), BF16),
         ],
-        flops=20 * pairs * HEAD,
-        moved=36 * tokens * part,
-        exps=pairs,
     )
 
 
@@ -432,15 +446,16 @@
     put_part(acc, part_refs)
 
 
-def project_sum(scal, arrays, weight, n, name):
+def project_sum(scal, arrays, weight, n, name, at=0, count=None):
     tokens, deep = arrays[0].shape
     width = weight.shape[1]
     rows = tokens // n
-    specs, outs = part_outs(n, rows, width)
+    count = n if count is None else count
+    specs, outs = part_outs(count, rows, width)
     return call(
         lambda *refs: sum_kernel(len(arrays), *refs),
-        (n,),
-        [pl.BlockSpec((rows, deep), lambda r, m: (r, 0))] * len(arrays) + [fixed(weight.shape)],
+        (count,),
+        [pl.BlockSpec((rows, deep), lambda r, m: (r + at, 0))] * len(arrays) + [fixed(weight.shape)],
         specs,
         outs,
         (scal, *arrays, weight),
@@ -459,12 +474,18 @@
         summed = jnp.concatenate([total(left), total(right)], axis=1)
         kernel(summed, *refs[:count], *refs[count + len(flat) :])
 
-    own = pl.BlockSpec((rows, 2 * half), lambda i, m: (m[0], 0))
+    def spec(shape):
+        if shape[0] == 1:
+            return pl.BlockSpec(shape, lambda i, m: (0, 0))
+        if shape[0] == rows:
+            return pl.BlockSpec((rows // STEPS, shape[1]), lambda i, m: (i, 0))
+        return pl.BlockSpec((rows // STEPS, shape[1]), lambda i, m: (m[0] * STEPS + i, 0))
+
     return call(
         body,
-        (1,),
-        [own if a.shape[0] > rows else fixed(a.shape) for a in args] + [fixed((rows, half))] * len(flat),
-        [fixed(shape) for shape, _ in outs],
+        (STEPS,),
+        [spec(a.shape) for a in args] + [spec((rows, half))] * len(flat),
+        [spec(shape) for shape, _ in outs],
         outs,
         (scal, *args, *flat),
         name,
@@ -481,11 +502,19 @@
     right_ref[...] = hidden[:, half:]
 
 
+def add_rows(out_ref, values):
+    @pl.when(pl.program_id(0) == 0)
+    def _():
+        out_ref[...] = jnp.zeros_like(out_ref)
+
+    out_ref[...] += jnp.sum(values, axis=0, keepdims=True)
+
+
 def back_norm(d_hidden, values, gain, d_gain_ref=None):
     factor = lax.rsqrt(jnp.mean(values * values, axis=-1, keepdims=True) + 1e-06)
     normed = values * factor
     if d_gain_ref is not None:
-        d_gain_ref[...] = jnp.sum(d_hidden * normed, axis=0, keepdims=True)
+        add_rows(d_gain_ref, d_hidden * normed)
     e = d_hidden * gain
     return factor * (e - normed * jnp.mean(e * normed, axis=-1, keepdims=True))
 
@@ -541,24 +570,49 @@
     put_part(mm(d_gate, wg_ref[...]) + mm(d_up, wu_ref[...]), refs[2 * n + 7 :])
 
 
-def mlp(scal, halves, d_act, w_gate, w_up, n):
-    rows, half = halves[0][0].shape
+def mlp(scal, halves, d_act, w_gate, w_up, n, at, count, into=()):
+    left, right = (side[at : at + count] for side in halves)
+    rows, half = left[0].shape
     hid, width = w_gate.shape
     tokens = rows * n
-    mine = lambda r, m: (r, 0)
-    specs, outs = part_outs(n, rows, width)
-    hidden, act, d_gate, d_up, *parts = call(
-        lambda *refs: mlp_kernel(n, *refs),
-        (n,),
-        [fixed((rows, half))] * (2 * n)
+    mine = lambda r, m: (r + at, 0)
+    specs, outs = part_outs(count, rows, width)
+    results = call(
+        lambda *refs: mlp_kernel(count, *refs),
+        (count,),
+        [fixed((rows, half))] * (2 * count)
         + [pl.BlockSpec((rows, hid), mine), fixed((hid, width)), fixed((hid, width))],
         [pl.BlockSpec((rows, width), mine)] + [pl.BlockSpec((rows, hid), mine)] * 3 + specs,
         [((tokens, width), BF16)] + [((tokens, hid), BF16)] * 3 + outs,
-        (scal, *halves[0], *halves[1], d_act, w_gate, w_up),
+        (scal, *left, *right, d_act, w_gate, w_up),
         "mlp",
         vmem=56,
-    )
-    return hidden, act, d_gate, d_up, parts
+        into=into,
+    )
+    return results[:4], results[4:]
+
+
+def outer_kernel(me_ref, *refs):
+    *left, right_ref, out_ref = refs
+    deep = left[0].shape[1]
+    for g, ref in enumerate(left):
+        out_ref[g * deep : (g + 1) * deep, :] = mm(ref[...], right_ref[...], TN).astype(BF16)
+
+
+def outer(scal, left, right, name):
+    tokens, deep = left[0].shape
+    width = right.shape[1]
+    steps = 4 if width % 512 == 0 else 3
+    step = width // steps
+    return call(
+        outer_kernel,
+        (steps,),
+        [fixed((tokens, deep))] * len(left) + [pl.BlockSpec((tokens, step), lambda j, m: (0, j))],
+        [pl.BlockSpec((len(left) * deep, step), lambda j, m: (0, j))],
+        [((len(left) * deep, width), BF16)],
+        (scal, *left, right),
+        name,
+    )[0]
 
 
 def d_attended_kernel(n, me_ref, *refs):
@@ -581,8 +635,6 @@
         [((tokens, width), BF16), ((tokens, local), BF16)],
         (scal, *halves[0], *halves[1], w_out),
         "project_back",
-        flops=2 * tokens * width * local,
-        moved=4 * tokens * width + 2 * (tokens + width) * local,
     )
 
 
@@ -646,47 +698,64 @@
         [((tokens, 3 * part), BF16)],
         (scal, own, across, back, dq, cosine, sine),
         "finish",
-        moved=20 * tokens * part,
     )[0]
 
 
 def d_one_kernel(me_ref, *refs):
     grads, weights = refs[:GROUPS], refs[GROUPS : GROUPS + 3]
-    x_ref, gain_ref = refs[GROUPS + 3 : GROUPS + 5]
     part = grads[0].shape[1] // 3
     acc = None
     for g, grad in enumerate(grads):
         for k, w_ref in enumerate(weights):
             term = mm(grad[:, k * part : (k + 1) * part], w_ref[:, g * part : (g + 1) * part], NT)
             acc = term if acc is None else acc + term
-    put_part(acc, refs[GROUPS + 5 :])
-    x = x_ref[...].astype(F32)
-    factor = lax.rsqrt(jnp.mean(x * x, axis=-1, keepdims=True) + 1e-06)
-
-    @pl.when(pl.program_id(0) == 0)
-    def _():
-        gain_ref[...] = jnp.zeros_like(gain_ref)
-
-    gain_ref[...] += jnp.sum(acc * (x * factor), axis=0, keepdims=True)
-
-
-def project_one_back(scal, grads, weights, x, n):
+    put_part(acc, refs[GROUPS + 3 :])
+
+
+def project_one_back(scal, grads, weights, n, at, count):
     tokens, triple = grads[0].shape
     width, local = weights[0].shape
     rows = tokens // n
-    specs, outs = part_outs(n, rows, width)
-    d_gain, *parts = call(
+    specs, outs = part_outs(count, rows, width)
+    return call(
         d_one_kernel,
-        (n,),
-        [pl.BlockSpec((rows, triple), lambda r, m: (r, 0))] * GROUPS
-        + [fixed((width, local))] * 3
-        + [pl.BlockSpec((rows, width), lambda r, m: (r ^ m[0], 0))],
-        [fixed((1, width))] + specs,
-        [((1, width), F32)] + outs,
-        (scal, *grads, *weights, x),
+        (count,),
+        [pl.BlockSpec((rows, triple), lambda r, m: (r + at, 0))] * GROUPS + [fixed((width, local))] * 3,
+        specs,
+        outs,
+        (scal, *grads, *weights),
         "project_one_back",
     )
-    return d_gain, parts
+
+
+def gain_kernel(n, me_ref, x_ref, *refs):
+    parts, gain_ref = refs[:-1], refs[-1]
+    half = parts[0].shape[1]
+    x = x_ref[...].astype(F32)
+    normed = x * lax.rsqrt(jnp.mean(x * x, axis=-1, keepdims=True) + 1e-06)
+    part = jnp.concatenate([parts[0][...], parts[1][...]], axis=1)
+    for r in range(1, n):
+        this = jnp.concatenate([parts[2 * r][...], parts[2 * r + 1][...]], axis=1)
+        part = jnp.where(lax.div(pl.program_id(0), STEPS) == r, this, part)
+    add_rows(gain_ref, part.astype(F32) * normed)
+
+
+def gain_back(scal, x, parts, n):
+    rows, half = parts[0].shape
+    step = rows // STEPS
+    return call(
+        lambda *refs: gain_kernel(n, *refs),
+        (n * STEPS,),
+        [pl.BlockSpec((step, 2 * half), lambda i, m: ((lax.div(i, STEPS) ^ m[0]) * STEPS + lax.rem(i, STEPS), 0))]
+        + [
+            pl.BlockSpec((step, half), lambda i, m, r=k // 2: (jnp.clip(i - r * STEPS, 0, STEPS - 1), 0))
+            for k in range(2 * n)
+        ],
+        [pl.BlockSpec((1, 2 * half), lambda i, m: (0, 0))],
+        [((1, 2 * half), F32)],
+        (scal, x, *parts),
+        "gain_back",
+    )[0]
 
 
 def seq_sums(sums):
@@ -729,55 +798,70 @@
     cosine, sine = jnp.concatenate([cosine, cosine], 1), jnp.concatenate([-sine, sine], 1)
     low = jnp.maximum(starts_here - (at - 2) * tokens, order + 2 * tokens - WINDOW + 1)[None, :]
 
-    hidden_one, *packed = project_keys(scal, block_input, gain_one, w_key, w_value, cosine, sine, n)
+    low_wide = jnp.broadcast_to(low.reshape(tokens, 1), (tokens, HEAD))
+    hidden_one, packed_all, *packed = project_keys(scal, block_input, gain_one, w_key, w_value, cosine, sine, n)
 
     right_two = [(i, i + 2) for i in range(peers - 2)]
     left_two = [(i + 2, i) for i in range(peers - 2)]
     to_odd = [(i, i + 1) for i in range(0, peers, 2)]
     to_even = [(i + 1, i) for i in range(0, peers, 2)]
     query = project_query(scal, hidden_one, w_query, cosine, sine, n)
-    cot, d_act = project_cotangent(scal, cotangent, w_down, n)
 
     segments, attended, lse = [], [], []
     twos = [lax.ppermute(own, "seq", right_two) for own in packed]
-    acrosses = [lax.ppermute(own, "seq", to_odd) for own in packed]
+    across_all = lax.ppermute(packed_all, "seq", to_odd)
     for g, own in enumerate(packed):
-        two = tied(twos[g], attended[g - 1] if g else (query, d_act))
-        segments.append((two, acrosses[g], lax.ppermute(two, "seq", to_even), own))
-        out, peak = attend(scal, g, query, segments[g], low, n)
-        attended.append(out)
-        lse.append(peak)
-    parts = project_sum(scal, attended, w_out, n, "project_out")
+        two = tied(twos[g], attended[g - 1] if g else query)
+        segments.append((two, across_all, lax.ppermute(two, "seq", to_even), own))
+        if g < GROUPS - 1:
+            out, peak = attend(scal, g, query, segments[g], low_wide, n, 0, n)
+            attended.append(out)
+            lse.append(peak)
+    some = attend(scal, g, query, segments[g], low_wide, n, n - 1, 1)
+    last_part = project_sum(scal, attended + [some[0]], w_out, n, "project_out", n - 1, 1)
+    out, peak = attend(scal, g, query, segments[g], low_wide, n, 0, n - 1, into=tied(some, last_part))
+    attended.append(out)
+    lse.append(peak)
+    parts = project_sum(scal, attended, w_out, n, "project_out", 0, n - 1)
+    sent, kept = sum_first(list(parts) + list(last_part), n)
+    sent, cot_later = lax.optimization_barrier((sent, cotangent))
+    terms = sum_second(sent, kept, n)
+    cot, d_act = project_cotangent(scal, cot_later, w_down, n)
     own_f32, own_half = ((rows, width), F32), ((rows, width // 2), BF16)
     mid, *hidden_own = own_rows(
-        mid_kernel, scal, [own_f32, own_half, own_half], (block_input, gain_two),
-        sum_second(*sum_first(parts, n), n), "mid",
+        mid_kernel, scal, [own_f32, own_half, own_half], (block_input, gain_two), tied(terms, (cot, d_act)), "mid"
     )
     hidden_halves = all_blocks(hidden_own, n)
-    hidden_two, activation, d_gate, d_up, parts = mlp(scal, hidden_halves, d_act, w_gate.T, w_up.T, n)
+    weights = (w_gate.T, w_up.T)
+    whole, own_part = mlp(scal, hidden_halves, d_act, *weights, n, 0, 1)
+    whole, last_part = mlp(scal, hidden_halves, d_act, *weights, n, n - 1, 1, into=whole)
+    whole, parts = mlp(scal, hidden_halves, d_act, *weights, n, 1, n - 2, into=tied(whole, last_part))
+    hidden_two, activation, d_gate, d_up = whole
+    parts = list(own_part) + list(parts) + list(last_part)
 
     d_two_sent, d_two_kept = sum_first(parts, n)
-    d_two_sent, act_later, d_gate_later = lax.optimization_barrier((d_two_sent, activation, d_gate))
+    d_two_sent, activation = lax.optimization_barrier((d_two_sent, activation))
+    grad_down = outer(scal, [activation], cot, "grad_down")
+    grad_down = scattered(grad_down, 1)
     d_hidden_two = sum_second(d_two_sent, d_two_kept, n)
-    grad_down = mm(act_later, cot, TN).astype(BF16)
-    grad_gate = mm(d_gate_later, hidden_two, TN).astype(BF16)
-    d_hidden_two, grad_down, grad_gate = lax.optimization_barrier((d_hidden_two, grad_down, grad_gate))
-    grad_down, grad_gate = scattered(grad_down, 1), scattered(grad_gate, 1)
+    out_parts = project_sum(scal, [activation], w_down, n, "project_down")
+    d_hidden_two = tied(d_hidden_two, out_parts)
     gain_row = ((1, width), F32)
     d_mid, *d_mid_own, d_gain_two = own_rows(
         d_mid_kernel, scal, [own_f32, own_half, own_half, gain_row], (mid, gain_two, cotangent), d_hidden_two, "d_mid"
     )
-    d_mid_own, act_later, d_up_later = lax.optimization_barrier((d_mid_own, act_later, d_up))
     d_mid_halves = all_blocks(d_mid_own, n)
-    out_parts = project_sum(scal, [act_later], w_down, n, "project_down")
-    grad_up = mm(d_up_later, hidden_two, TN).astype(BF16)
-    d_mid_halves, out_parts, grad_up = lax.optimization_barrier((d_mid_halves, out_parts, grad_up))
-    grad_up = scattered(grad_up, 1)
+    d_gate, d_up = tied((d_gate, d_up), (d_mid_halves[0][2], d_mid_halves[1][1]))
+    grad_gate = outer(scal, [d_gate], hidden_two, "grad_gate")
+    grad_up = outer(scal, [d_up], hidden_two, "grad_up")
+    d_mid_halves = tied(d_mid_halves, (grad_gate, grad_up))
+    grad_gate = scattered(grad_gate, 1)
+    out_parts = tied(out_parts, d_mid_halves)
     out_sent, out_kept = sum_first(out_parts, n)
     d_mid_low, d_attended = project_back(scal, d_mid_halves, w_out, n)
 
-    def sent_back(d_two, d_one, after=()):
-        across = tied(swap(d_one, 1, "seq"), after)
+    def sent_back(d_two, d_one):
+        across = swap(d_one, 1, "seq")
         sent = (d_two.astype(F32) + jnp.where(odd, across.astype(F32), 0.0)).astype(BF16)
         return across, sent
 
@@ -786,46 +870,62 @@
 
     d_attended, out_sent = lax.optimization_barrier((d_attended, out_sent))
     out_terms = sum_second(out_sent, out_kept, n)
+    grad_out = scattered(outer(scal, attended, d_mid_low, "grad_out"), 1)
     dq, d_two, d_one, d_own = back(0, d_attended)
-    low_later = tied(d_mid_low, dq)
-    grad_out = jnp.concatenate([mm(a, low_later, TN).astype(BF16) for a in attended], axis=0)
-    across, sent = sent_back(d_two, d_one, grad_out)
-    grad_out = scattered(grad_out, 1)
+    across, sent = sent_back(d_two, d_one)
+    d_attended, sent, across = lax.optimization_barrier((d_attended, sent, across))
+    back_two = lax.ppermute(sent, "seq", left_two)
+    dq_1, d_two_1, d_one_1, d_own_1 = back(1, d_attended)
+    d_one_1, back_two, out_terms = lax.optimization_barrier((d_one_1, back_two, out_terms))
     out_own = own_rows(output_kernel, scal, [own_half, own_half], (mid,), out_terms, "output")
     out_halves = all_blocks(out_own, n)
-    d_attended, sent, across, out_own = lax.optimization_barrier((d_attended, sent, across, out_own))
-    back_two = lax.ppermute(sent, "seq", left_two)
-    dq_1, d_two_1, d_one_1, d_own_1 = back(1, d_attended)
-    across_1, sent_1 = sent_back(d_two_1, d_one_1, back_two)
-    sent_1, back_two = lax.optimization_barrier((sent_1, back_two))
+    across_1, sent_1 = sent_back(d_two_1, d_one_1)
+    sent_1, across_1, back_two = lax.optimization_barrier((sent_1, across_1, back_two))
     back_two_1 = lax.ppermute(sent_1, "seq", left_two)
+    back_two = tied(back_two, (out_halves[0][2], out_halves[1][1]))
     first = finish(scal, d_own, across, back_two, dq, cosine, sine, n)
     output = place(scal, out_halves, tuple(range(n)), BF16, n)
-    back_two_1 = tied(back_two_1, (first, output, grad_down))
+    back_two_1 = tied(back_two_1, output)
+    grad_up = scattered(tied(grad_up, back_two_1), 1)
     second = finish(scal, d_own_1, across_1, back_two_1, dq_1, cosine, sine, n)
-    d_gain_one, parts = project_one_back(scal, [first, second], (w_query, w_key, w_value), block_input, n)
+    weights = (w_query, w_key, w_value)
+    last_part = project_one_back(scal, [first, second], weights, n, n - 1, 1)
+    parts = project_one_back(scal, tied([first, second], last_part), weights, n, 0, n - 1)
+    parts = list(parts) + list(last_part)
     d_one_sent, d_one_kept = sum_first(parts, n)
-    d_one_sent, first, second = lax.optimization_barrier((d_one_sent, first, second))
+    grad_first = outer(scal, [hidden_one], tied(first, last_part), "grad_first")
+    d_one_sent, parts, grad_first = lax.optimization_barrier((d_one_sent, parts, grad_first))
     d_hidden_one = sum_second(d_one_sent, d_one_kept, n)
-    grad_first = mm(hidden_one, first, TN).astype(BF16)
-    grad_second = mm(hidden_one, second, TN).astype(BF16)
-    gains = seq_sums(jnp.concatenate([d_gain_one, d_gain_two], axis=0))
-    d_hidden_one, gains = tied((d_hidden_one, gains), (grad_first, grad_second, grad_gate))
-    grad_qkv = [scattered(grad_first, 0), scattered(grad_second, 0)]
+    d_gain_one = gain_back(scal, block_input, parts, n)
+    d_hidden_one = tied(d_hidden_one, d_gain_one)
     input_grad, *input_own_halves = own_rows(
         input_kernel, scal, [own_f32, own_half, own_half], (block_input, gain_one, d_mid), d_hidden_one, "input"
     )
     input_halves = all_blocks(input_own_halves, n)
+    near = (input_halves[0][2], input_halves[1][1])
+    second, gains = tied((second, jnp.concatenate([d_gain_one, d_gain_two], axis=0)), near)
+    grad_second = outer(scal, [hidden_one], second, "grad_second")
+    gains = seq_sums(gains)
     for bit in bits_of(n):
         gains = gains + swap(gains, bit)
     early, late = tuple(range(n - 1)), (n - 1,)
-    early_halves = [side[: n - 1] for side in input_halves]
-    grad_input = place(scal, tied(early_halves, grad_up), early, F32, n, own=input_grad)
-    grad_input = place(scal, input_halves, late, F32, n, whole=grad_input)
-
-    part = grad_qkv[0].shape[1] // 3
+    early_halves = tied([side[: n - 1] for side in input_halves], (grad_first, grad_second))
+    placed = place(scal, early_halves, early, F32, n, own=input_grad)
+    grad_input = place(scal, input_halves, late, F32, n, whole=placed)
+    grad_first, grad_second = scattered(grad_first, 0), scattered(grad_second, 0)
+
+    grads, after = [], input_own_halves
+    for grad in (grad_down, grad_gate, grad_out):
+        after = tied(grad, after)
+        grads.append(after)
+    after = (after, placed)
+    for grad in (grad_up, grad_first, grad_second):
+        after = tied(grad, after)
+        grads.append(after)
+    grad_down, grad_gate, grad_out, grad_up, grad_first, grad_second = grads
+    part = w_query.shape[1] // GROUPS
     grad_query, grad_key, grad_value = (
-        jnp.concatenate([g[:, k * part : (k + 1) * part] for g in grad_qkv], axis=1).astype(F32)
+        jnp.concatenate([g[:, k * part : (k + 1) * part] for g in (grad_first, grad_second)], axis=1).astype(F32)
         for k in range(3)
     )
     return (

time: 650 us -> 597 us (0.918)
  waiting for transfers between devices: 240 us -> 157 us
  Pallas kernels: 222 us -> 283 us
  matrix products: 41.3 us -> 0 us
  local copies, waits for them, and re-layouts: 21.2 us -> 34.8 us
    ppermute x55, waiting for transfers between devices: 174 us -> 91.3 us  [swap(): return lax.ppermute(array, axis, [(i, i ^ bit) for i in range(size)])]
    pallas_call x18 -> x30, Pallas kernels: 211 us -> 273 us  [call(): pl.pallas_call(body, grid_spec=pltpu.PrefetchScalarGridSpec(num_scalar_pr...]
    dot_general x7 -> x0, matrix products: 41.3 us -> none  [mm(): return lax.dot_general(a, b, dims, preferred_element_type=F32)]
    ppermute x1, waiting for transfers between devices: 48.3 us -> 17.5 us  [on_device(): back_two = lax.ppermute(sent, 'seq', left_two)]
    ppermute x2, waiting for transfers between devices: 1.82 us -> 23.8 us  [on_device(): twos = [lax.ppermute(own, 'seq', right_two) for own in packed]]
    unnamed x120 -> x176, local copies, waits for them, and re-layouts: 17.3 us -> 30.6 us
    reduce_scatter x6, waiting for transfers between devices: 8.2 us -> 21.4 us  [scattered(): return lax.psum_scatter(grad, 'seq', scatter_dimension=dim, tiled=True)]
  transfers between devices with their start and end apart: 69 -> 68, of which waited for: 33 -> 21; matrix products, arithmetic and copies ran while one was open for 9% -> 4% of each run, Pallas kernels for 23% -> 42%
where the time goes in v3:
time: 597 us; the launch traced here: 589 us
  Pallas kernels  283 us (47%)
  waiting for transfers between devices  157 us (26%)
  starting transfers between devices  75.5 us (13%)
  local copies, waits for them, and re-layouts  34.8 us (6%)
  other arithmetic  23.8 us (4%)
  between operations  15.6 us (3%)
    pallas_call x30, Pallas kernels, call(): pl.pallas_call(body, grid_spec=pltpu.PrefetchScalarGridSpec(num_scalar_pr...  273 us
    ppermute x55, waiting for transfers between devices, swap(): return lax.ppermute(array, axis, [(i, i ^ bit) for i in range(size)])  91.3 us
    ppermute x55, starting transfers between devices, swap(): return lax.ppermute(array, axis, [(i, i ^ bit) for i in range(size)])  58.6 us
    unnamed x176, local copies, waits for them, and re-layouts  30.6 us
    ppermute x2, waiting for transfers between devices, on_device(): twos = [lax.ppermute(own, 'seq', right_two) for own in packed]  23.8 us
    reduce_scatter x6, waiting for transfers between devices, scattered(): return lax.psum_scatter(grad, 'seq', scatter_dimension=dim, tiled=True)  21.4 us
    ppermute x1, waiting for transfers between devices, on_device(): back_two = lax.ppermute(sent, 'seq', left_two)  17.5 us
  transfers between devices with their start and end apart: 68, of which 21 were waited for; matrix products, arithmetic and copies ran while one was open for 4% of the time, Pallas kernels for 42%

profile of v3, /device:TPU:0, one launch (start us, length us, event | category | flops | bytes accessed | tf_op | source)
XLA Modules:
  0.0 589.4 jit_solution(2363699345620233484)
XLA Ops:
  10.9 10.2 %project_keys.1 = (bf16[1024,2048]{1,0:T(8,128)(2,1)}, bf16[4,1024,256]{2,1,0:T(8,128)(2,1)S(1)}, bf16[2,1024,256]{2,1,0:T(8,128)(2,1)S(1)}, bf16[2,1024,256]{2,1,0:T(8,128)(2,1)S(1)}) custom-call(s32[2]{0:T(128)S(1)} %pad_add_fusion.2.me_ref.refs_0_._.s_ref_, bf16[1024,2048]{1,0:T(8,128)(2,1)} %refs_0_.3, f32[1,2048]{1,0:T(1,128)S(1)} %bitcast.22, ...), custom_call_target="tpu_custom_call" | custom-call | tf_op jit(solution)/shard_map/project_keys/pallas_call | solution.py:37
  21.1 5.0 collective-permute-start
  27.8 5.6 project_query.1.refs_1_
  33.4 15.1 %collective-permute-done.refs_2_ = bf16[2,1024,256]{2,1,0:T(8,128)(2,1)S(1)} collective-permute-done((bf16[2,1024,256]{2,1,0:T(8,128)(2,1)S(1)}, bf16[2,1024,256]{2,1,0:T(8,128)(2,1)S(1)}, u32[]{:S(2)}, u32[]{:S(2)}) %collective-permute-start) | collective-permute-done | bytes 1048608 | tf_op jit(solution)/shard_map/ppermute | solution.py:811
  49.8 4.5 collective-permute-start.3
  55.5 13.2 %attend.3 = (bf16[1024,256]{1,0:T(8,128)(2,1)S(1)}, f32[2,1,1024]{2,1,0:T(1,128)S(1)}) custom-call(s32[2]{0:T(128)S(1)} %pad_add_fusion.2.me_ref.refs_0_._.s_ref_, bf16[1024,512]{1,0:T(8,128)(2,1)S(1)} %project_query.1.refs_1_, bf16[2,1024,256]{2,1,0:T(8,128)(2,1)S(1)} %collective-permute-done.refs_2_, bf16[4,1024,256]{2,1,0:T(8,128)(2,1)} %copy-done.78, ...), custom_call_target="tpu_custom_call" | custom-call | tf_op jit(solution)/shard_map/attend/pallas_call | solution.py:37
  68.7 8.7 %collective-permute-done.3.refs_2_ = bf16[2,1024,256]{2,1,0:T(8,128)(2,1)S(1)} collective-permute-done((bf16[2,1024,256]{2,1,0:T(8,128)(2,1)S(1)}, bf16[2,1024,256]{2,1,0:T(8,128)(2,1)S(1)}, u32[]{:S(2)}, u32[]{:S(2)}) %collective-permute-start.3) | collective-permute-done | bytes 1048608 | tf_op jit(solution)/shard_map/ppermute | solution.py:811
  79.2 3.0 collective-permute-done.4.refs_4_
  82.3 4.7 attend.4
  91.3 10.5 %attend.5 = (bf16[1024,256]{1,0:T(8,128)(2,1)S(1)}, f32[2,1,1024]{2,1,0:T(1,128)S(1)}) custom-call(s32[2]{0:T(128)S(1)} %pad_add_fusion.2.me_ref.refs_0_._.s_ref_, bf16[1024,512]{1,0:T(8,128)(2,1)S(1)} %project_query.1.refs_1_, bf16[2,1024,256]{2,1,0:T(8,128)(2,1)S(1)} %collective-permute-done.3.refs_2_, ...), custom_call_target="tpu_custom_call", output_to_operand_aliasing={{0}: (7, {}), {1}: (8, {})} | custom-call | tf_op jit(solution)/shard_map/attend/pallas_call | solution.py:37
  101.8 4.6 project_out.3
  111.1 12.0 %project_cotangent.1 = (bf16[1024,2048]{1,0:T(8,128)(2,1)S(1)}, f32[1024,1376]{1,0:T(8,128)}) custom-call(s32[2]{0:T(128)S(1)} %pad_add_fusion.2.me_ref.refs_0_._.s_ref_, bf16[1024,2048]{1,0:T(8,128)(2,1)} %refs_2_.5, bf16[1376,2048]{1,0:T(8,128)(2,1)} %refs_2_.4), custom_call_target="tpu_custom_call" | custom-call | tf_op jit(solution)/shard_map/project_cotangent/pallas_call | solution.py:37
  125.2 6.2 %collective-permute-done.8.refs_4_ = bf16[256,1024]{1,0:T(8,128)(2,1)S(1)} collective-permute-done((bf16[256,1024]{1,0:T(8,128)(2,1)S(1)}, bf16[256,1024]{1,0:T(8,128)(2,1)S(1)}, u32[]{:S(2)}, u32[]{:S(2)}) %collective-permute-start.8) | collective-permute-done | bytes 524320 | tf_op jit(solution)/shard_map/ppermute | solution.py:67
  131.4 4.8 mid.1
  138.4 10.2 %collective-permute-done.12.refs_2_ = bf16[256,1024]{1,0:T(8,128)(2,1)S(1)} collective-permute-done((bf16[256,1024]{1,0:T(8,128)(2,1)S(1)}, bf16[256,1024]{1,0:T(8,128)(2,1)S(1)}, u32[]{:S(2)}, u32[]{:S(2)}) %collective-permute-start.12) | collective-permute-done | bytes 524320 | tf_op jit(solution)/shard_map/ppermute | solution.py:67
  153.0 13.4 %mlp.3 = (bf16[1024,2048]{1,0:T(8,128)(2,1)}, bf16[1024,1376]{1,0:T(8,128)(2,1)}, bf16[1024,1376]{1,0:T(8,128)(2,1)}, bf16[1024,1376]{1,0:T(8,128)(2,1)}, bf16[2...) custom-call(s32[2]{0:T(128)} %copy-done.68, bf16[256,1024]{1,0:T(8,128)(2,1)} %copy-done.67, bf16[256,1024]{1,0:T(8,128)(2,1)} %copy-done.66, ...), custom_call_target="tpu_custom_call" | custom-call | tf_op jit(solution)/shard_map/mlp/pallas_call | solution.py:37
  167.4 13.6 %mlp.4 = (bf16[1024,2048]{1,0:T(8,128)(2,1)}, bf16[1024,1376]{1,0:T(8,128)(2,1)}, bf16[1024,1376]{1,0:T(8,128)(2,1)}, bf16[1024,1376]{1,0:T(8,128)(2,1)}, bf16[2...) custom-call(s32[2]{0:T(128)} %copy-done.68, ...), custom_call_target="tpu_custom_call", output_to_operand_aliasing={{0}: (6, {}), {1}: (7, {}), {2}: (8, {}), {3}: (9, {})} | custom-call | tf_op jit(solution)/shard_map/mlp/pallas_call | solution.py:37
  185.1 22.7 %mlp.5 = (bf16[1024,2048]{1,0:T(8,128)(2,1)}, bf16[1024,1376]{1,0:T(8,128)(2,1)}, bf16[1024,1376]{1,0:T(8,128)(2,1)}, bf16[1024,1376]{1,0:T(8,128)(2,1)}, bf16[2...) custom-call(s32[2]{0:T(128)} %copy-done.68, ...), custom_call_target="tpu_custom_call", output_to_operand_aliasing={{0}: (8, {}), {1}: (9, {}), {2}: (10, {}), {3}: (11, {})} | custom-call | tf_op jit(solution)/shard_map/mlp/pallas_call | solution.py:37
  210.6 9.7 %grad_down.1 = bf16[1376,2048]{1,0:T(8,128)(2,1)} custom-call(s32[2]{0:T(128)S(1)} %copy-done.69, bf16[1024,1376]{1,0:T(8,128)(2,1)S(1)} %copy-done, bf16[1024,2048]{1,0:T(8,128)(2,1)} %copy-done.17), custom_call_target="tpu_custom_call" | custom-call | tf_op jit(solution)/shard_map/grad_down/pallas_call | solution.py:37
  225.3 11.8 %project_down.1 = (bf16[256,1024]{1,0:T(8,128)(2,1)S(1)}, bf16[256,1024]{1,0:T(8,128)(2,1)S(1)}, bf16[256,1024]{1,0:T(8,128)(2,1)S(1)}, bf16[256,1024]{1,0:T(8,1...) custom-call(s32[2]{0:T(128)S(1)} %copy-done.69, ...), custom_call_target="tpu_custom_call" | custom-call | tf_op jit(solution)/shard_map/project_down/pallas_call | solution.py:37
  243.6 5.7 d_mid.1
  250.8 7.6 %collective-permute-done.24.refs_3_ = bf16[256,1024]{1,0:T(8,128)(2,1)S(1)} collective-permute-done((bf16[256,1024]{1,0:T(8,128)(2,1)S(1)}, bf16[256,1024]{1,0:T(8,128)(2,1)S(1)}, u32[]{:S(2)}, u32[]{:S(2)}) %collective-permute-start.24) | collective-permute-done | bytes 524320 | tf_op jit(solution)/shard_map/ppermute | solution.py:67
  259.5 9.7 %grad_gate.1 = bf16[1376,2048]{1,0:T(8,128)(2,1)} custom-call(s32[2]{0:T(128)S(1)} %copy-done.69, bf16[1024,1376]{1,0:T(8,128)(2,1)S(1)} %copy-done.1, bf16[1024,2048]{1,0:T(8,128)(2,1)} %get-tuple-element.268.refs_1_), custom_call_target="tpu_custom_call" | custom-call | tf_op jit(solution)/shard_map/grad_gate/pallas_call | solution.py:37
  273.4 9.7 %grad_up.1 = bf16[1376,2048]{1,0:T(8,128)(2,1)} custom-call(s32[2]{0:T(128)S(1)} %copy-done.69, bf16[1024,1376]{1,0:T(8,128)(2,1)S(1)} %copy-done.2, bf16[1024,2048]{1,0:T(8,128)(2,1)} %get-tuple-element.268.refs_1_), custom_call_target="tpu_custom_call" | custom-call | tf_op jit(solution)/shard_map/grad_up/pallas_call | solution.py:37
  283.2 9.5 %collective-permute-done.25.refs_4_ = bf16[256,1024]{1,0:T(8,128)(2,1)} collective-permute-done((bf16[256,1024]{1,0:T(8,128)(2,1)}, bf16[256,1024]{1,0:T(8,128)(2,1)}, u32[]{:S(2)}, u32[]{:S(2)}) %collective-permute-start.25) | collective-permute-done | bytes 524320 | tf_op jit(solution)/shard_map/ppermute | solution.py:67
  299.7 6.4 %project_back.1 = (bf16[1024,2048]{1,0:T(8,128)(2,1)}, bf16[1024,512]{1,0:T(8,128)(2,1)S(1)}) custom-call(s32[2]{0:T(128)S(1)} %copy-done.69, bf16[256,1024]{1,0:T(8,128)(2,1)S(1)} %copy-done.47, bf16[256,1024]{1,0:T(8,128)(2,1)} %collective-permute-done.23.refs_2_, bf16[256,1024]{1,0:T(8,128)(2,1)S(1)} %copy-done.51, ...), custom_call_target="tpu_custom_call" | custom-call | tf_op jit(solution)/shard_map/project_back/pallas_call | solution.py:37
  308.2 19.5 %attend_back.2 = (bf16[1024,256]{1,0:T(8,128)(2,1)S(1)}, bf16[2,1024,256]{2,1,0:T(8,128)(2,1)S(1)}, bf16[2,1024,256]{2,1,0:T(8,128)(2,1)}, bf16[2,1024,256]{2,1,0:T(8,128)(2,1)S(1)}) custom-call(s32[2]{0:T(128)S(1)} %copy-done.69, bf16[1024,512]{1,0:T(8,128)(2,1)} %copy-done.8, bf16[2,1024,256]{2,1,0:T(8,128)(2,1)} %copy-done.34, ...), custom_call_target="tpu_custom_call" | custom-call | flops 69000003584 | tf_op jit(solution)/shard_map/attend_back/pallas_call | solution.py:37
  332.9 6.4 %grad_out.1 = bf16[512,2048]{1,0:T(8,128)(2,1)} custom-call(s32[2]{0:T(128)S(1)} %copy-done.69, bf16[1024,256]{1,0:T(8,128)(2,1)S(1)} %copy-done.14, bf16[1024,256]{1,0:T(8,128)(2,1)S(1)} %copy-done.12, bf16[1024,2048]{1,0:T(8,128)(2,1)} %get-tuple-element.360.refs_2_), custom_call_target="tpu_custom_call" | custom-call | tf_op jit(solution)/shard_map/grad_out/pallas_call | solution.py:37
  343.9 19.4 %attend_back.3 = (bf16[1024,256]{1,0:T(8,128)(2,1)S(1)}, bf16[2,1024,256]{2,1,0:T(8,128)(2,1)S(1)}, bf16[2,1024,256]{2,1,0:T(8,128)(2,1)S(1)}, bf16[2,1024,256]{2,1,0:T(8,128)(2,1)S(1)}) custom-call(s32[2]{0:T(128)S(1)} %copy-done.69, bf16[1024,512]{1,0:T(8,128)(2,1)} %copy-done.8, bf16[2,1024,256]{2,1,0:T(8,128)(2,1)} %copy-done.19, ...), custom_call_target="tpu_custom_call" | custom-call | flops 69000003584 | tf_op jit(solution)/shard_map/attend_back/pallas_call | solution.py:37
  365.1 17.5 %collective-permute-done.32.back_ref = bf16[2,1024,256]{2,1,0:T(8,128)(2,1)S(1)} collective-permute-done((bf16[2,1024,256]{2,1,0:T(8,128)(2,1)S(1)}, bf16[2,1024,256]{2,1,0:T(8,128)(2,1)S(1)}, u32[]{:S(2)}, u32[]{:S(2)}) %collective-permute-start.32) | collective-permute-done | bytes 1048608 | tf_op jit(solution)/shard_map/ppermute | solution.py:877
  382.6 3.4 output.1
  391.8 9.0 %collective-permute-done.38.refs_3_ = bf16[256,1024]{1,0:T(8,128)(2,1)S(1)} collective-permute-done((bf16[256,1024]{1,0:T(8,128)(2,1)S(1)}, bf16[256,1024]{1,0:T(8,128)(2,1)S(1)}, u32[]{:S(2)}, u32[]{:S(2)}) %collective-permute-start.38) | collective-permute-done | bytes 524320 | tf_op jit(solution)/shard_map/ppermute | solution.py:67
  402.8 10.3 %collective-permute-done.37.refs_2_ = bf16[256,1024]{1,0:T(8,128)(2,1)S(1)} collective-permute-done((bf16[256,1024]{1,0:T(8,128)(2,1)S(1)}, bf16[256,1024]{1,0:T(8,128)(2,1)S(1)}, u32[]{:S(2)}, u32[]{:S(2)}) %collective-permute-start.37) | collective-permute-done | bytes 524320 | tf_op jit(solution)/shard_map/ppermute | solution.py:67
  413.1 10.5 %collective-permute-done.39.refs_4_ = bf16[256,1024]{1,0:T(8,128)(2,1)S(1)} collective-permute-done((bf16[256,1024]{1,0:T(8,128)(2,1)S(1)}, bf16[256,1024]{1,0:T(8,128)(2,1)S(1)}, u32[]{:S(2)}, u32[]{:S(2)}) %collective-permute-start.39) | collective-permute-done | bytes 524320 | tf_op jit(solution)/shard_map/ppermute | solution.py:67
  423.7 3.0 place.3
  434.1 2.9 finish.3.refs_1_
  438.3 6.1 %project_one_back.2 = (bf16[256,1024]{1,0:T(8,128)(2,1)}, bf16[256,1024]{1,0:T(8,128)(2,1)}) custom-call(s32[2]{0:T(128)S(1)} %copy-done.69, bf16[1024,768]{1,0:T(8,128)(2,1)S(1)} %copy-done.5, bf16[1024,768]{1,0:T(8,128)(2,1)S(1)} %copy-done.3, bf16[2048,512]{1,0:T(8,128)(2,1)} %refs_2_.7, bf16[2048,512]{1,0:T(8,128)(2,1)} %refs_3_.7, bf16[2048,512]{1,0:T(8,128)(2,1)} %refs_4_.3), custom_call_target="tpu_custom_call" | custom-call | tf_op jit(solution)/shard_map/project_one_back/pallas_call | solution.py:37
  446.7 8.2 %grad_first.1 = bf16[2048,768]{1,0:T(8,128)(2,1)} custom-call(s32[2]{0:T(128)S(1)} %copy-done.69, bf16[1024,2048]{1,0:T(8,128)(2,1)} %get-tuple-element.191.h_ref.refs_0_, bf16[1024,768]{1,0:T(8,128)(2,1)S(1)} %copy-done.5), custom_call_target="tpu_custom_call" | custom-call | tf_op jit(solution)/shard_map/grad_first/pallas_call | solution.py:37
  454.9 9.4 %project_one_back.3 = (bf16[256,1024]{1,0:T(8,128)(2,1)S(1)}, bf16[256,1024]{1,0:T(8,128)(2,1)S(1)}, bf16[256,1024]{1,0:T(8,128)(2,1)S(1)}, bf16[256,1024]{1,0:T...) custom-call(s32[2]{0:T(128)S(1)} %copy-done.69, bf16[1024,768]{1,0:T(8,128)(2,1)S(1)} %copy-done.5, ...), custom_call_target="tpu_custom_call" | custom-call | tf_op jit(solution)/shard_map/project_one_back/pallas_call | solution.py:37
  474.1 11.7 %gain_back.1 = f32[1,2048]{1,0:T(1,128)S(1)} custom-call(s32[2]{0:T(128)S(1)} %copy-done.69, bf16[1024,2048]{1,0:T(8,128)(2,1)} %refs_0_.3, bf16[256,1024]{1,0:T(8,128)(2,1)S(1)} %get-tuple-element.340.refs_2_.refs_3_, bf16[256,1024]{1,0:T(8,128)(2,1)S(1)} %get-tuple-element.343.refs_3_.refs_6_, bf16[256,1024]{1,0:T(8,128)(2,1)S(1)} %copy-done.57, ...), custom_call_target="tpu_custom_call" | custom-call | tf_op jit(solution)/shard_map/gain_back/pallas_call | solution.py:37
  485.8 8.6 %collective-permute-done.48.refs_5_ = bf16[256,1024]{1,0:T(8,128)(2,1)S(1)} collective-permute-done((bf16[256,1024]{1,0:T(8,128)(2,1)}, bf16[256,1024]{1,0:T(8,128)(2,1)S(1)}, u32[]{:S(2)}, u32[]{:S(2)}) %collective-permute-start.48) | collective-permute-done | bytes 524320 | tf_op jit(solution)/shard_map/ppermute | solution.py:67
  494.4 5.3 input.1
  501.7 9.6 %collective-permute-done.51.refs_3_ = bf16[256,1024]{1,0:T(8,128)(2,1)S(1)} collective-permute-done((bf16[256,1024]{1,0:T(8,128)(2,1)S(1)}, bf16[256,1024]{1,0:T(8,128)(2,1)S(1)}, u32[]{:S(2)}, u32[]{:S(2)}) %collective-permute-start.51) | collective-permute-done | bytes 524320 | tf_op jit(solution)/shard_map/ppermute | solution.py:67
  512.1 8.1 %grad_second.1 = bf16[2048,768]{1,0:T(8,128)(2,1)} custom-call(s32[2]{0:T(128)S(1)} %copy-done.69, bf16[1024,2048]{1,0:T(8,128)(2,1)} %get-tuple-element.191.h_ref.refs_0_, bf16[1024,768]{1,0:T(8,128)(2,1)S(1)} %copy-done.4), custom_call_target="tpu_custom_call" | custom-call | tf_op jit(solution)/shard_map/grad_second/pallas_call | solution.py:37
  520.2 3.9 collective-permute-start.57
  532.6 3.7 collective-permute-done.60
  539.0 4.7 place.4.refs_3_
  553.8 21.4 %reduce-scatter.17.cloned.1.call-done = bf16[256,768]{1,0:T(8,128)(2,1)} async-done(((bf16[2048,768]{1,0:T(8,128)(2,1)}), bf16[256,768]{1,0:T(8,128)(2,1)}) %reduce-scatter.17.cloned.1.call-update) | async-done | bytes 393232 | tf_op jit(solution)/shard_map/reduce_scatter | solution.py:774
  (348 shorter events, 133.0 us)
Async XLA Ops:
  7.2 539.1 %reduce-scatter.15.cloned.1.call-start = ((), (), s32[]{:S(2)}) async-start(), calls=%async_computation.10 | async-start | bytes 6340608 | tf_op jit(solution)/shard_map/reduce_scatter | solution.py:774
  21.1 27.3 %collective-permute-start = (bf16[2,1024,256]{2,1,0:T(8,128)(2,1)S(1)}, bf16[2,1024,256]{2,1,0:T(8,128)(2,1)S(1)}, u32[]{:S(2)}, u32[]{:S(2)}) collective-permute-start(bf16[2,1024,256]{2,1,0:T(8,128)(2,1)S(1)} %get-tuple-element.192.refs_5_), channel_id=1, source_target_pairs={{0,8},{4,12},{8,16},{12,20},{16,24},{20,28},{1,9},{5,13},{9,17},{1... | collective-permute-start | bytes 3145736 | tf_op jit(solution)/shard_map/ppermute | solution.py:811
  26.1 28.1 %collective-permute-start.1 = (bf16[4,1024,256]{2,1,0:T(8,128)(2,1)S(1)}, bf16[4,1024,256]{2,1,0:T(8,128)(2,1)S(1)}, u32[]{:S(2)}, u32[]{:S(2)}) collective-permute-start(bf16[4,1024,256]{2,1,0:T(8,128)(2,1)S(1)} %get-tuple-element.194), channel_id=1, source_target_pairs={{0,4},{8,12},{16,20},{24,28},{1,5},{9,13},{17,21},{25,29},{2,6},{1... | collective-permute-start | bytes 6291464 | tf_op jit(solution)/shard_map/ppermute | solution.py:812
  49.8 27.7 %collective-permute-start.3 = (bf16[2,1024,256]{2,1,0:T(8,128)(2,1)S(1)}, bf16[2,1024,256]{2,1,0:T(8,128)(2,1)S(1)}, u32[]{:S(2)}, u32[]{:S(2)}) collective-permute-start(bf16[2,1024,256]{2,1,0:T(8,128)(2,1)S(1)} %get-tuple-element.196.refs_5_), channel_id=1, source_target_pairs={{0,8},{4,12},{8,16},{12,20},{16,24},{20,28},{1,9},{5,13},{9,17},{1... | collective-permute-start | bytes 3145736 | tf_op jit(solution)/shard_map/ppermute | solution.py:811
  88.2 19.4 %collective-permute-start.6 = (bf16[256,1024]{1,0:T(8,128)(2,1)S(1)}, bf16[256,1024]{1,0:T(8,128)(2,1)S(1)}, u32[]{:S(2)}, u32[]{:S(2)}) collective-permute-start(bf16[256,1024]{1,0:T(8,128)(2,1)S(1)} %get-tuple-element.201), channel_id=1, source_target_pairs={{0,2},{1,3},{2,0},{3,1},{4,6},{5,7},{6,4},{7,5},{8,10},{9,11},{10,... | collective-permute-start | bytes 1572872 | tf_op jit(solution)/shard_map/ppermute | solution.py:67
  89.8 18.0 %collective-permute-start.7 = (bf16[256,1024]{1,0:T(8,128)(2,1)S(1)}, bf16[256,1024]{1,0:T(8,128)(2,1)S(1)}, u32[]{:S(2)}, u32[]{:S(2)}) collective-permute-start(bf16[256,1024]{1,0:T(8,128)(2,1)S(1)} %get-tuple-element.200), channel_id=1, source_target_pairs={{0,1},{1,0},{2,3},{3,2},{4,5},{5,4},{6,7},{7,6},{8,9},{9,8},{10,11... | collective-permute-start | bytes 1572872 | tf_op jit(solution)/shard_map/ppermute | solution.py:67
  106.5 18.7 %collective-permute-start.5 = (bf16[256,1024]{1,0:T(8,128)(2,1)S(1)}, bf16[256,1024]{1,0:T(8,128)(2,1)S(1)}, u32[]{:S(2)}, u32[]{:S(2)}) collective-permute-start(bf16[256,1024]{1,0:T(8,128)(2,1)S(1)} %get-tuple-element.206), channel_id=1, source_target_pairs={{0,1},{1,0},{2,3},{3,2},{4,5},{5,4},{6,7},{7,6},{8,9},{9,8},{10,11... | collective-permute-start | bytes 1572872 | tf_op jit(solution)/shard_map/ppermute | solution.py:67
  107.1 18.1 %collective-permute-start.9 = (bf16[256,1024]{1,0:T(8,128)(2,1)S(1)}, bf16[256,1024]{1,0:T(8,128)(2,1)S(1)}, u32[]{:S(2)}, u32[]{:S(2)}) collective-permute-start(bf16[256,1024]{1,0:T(8,128)(2,1)S(1)} %get-tuple-element.211), channel_id=1, source_target_pairs={{0,2},{1,3},{2,0},{3,1},{4,6},{5,7},{6,4},{7,5},{8,10},{9,11},{10,... | collective-permute-start | bytes 1572872 | tf_op jit(solution)/shard_map/ppermute | solution.py:67
  108.0 23.4 %collective-permute-start.8 = (bf16[256,1024]{1,0:T(8,128)(2,1)S(1)}, bf16[256,1024]{1,0:T(8,128)(2,1)S(1)}, u32[]{:S(2)}, u32[]{:S(2)}) collective-permute-start(bf16[256,1024]{1,0:T(8,128)(2,1)S(1)} %add_convert_fusion.8), channel_id=1, source_target_pairs={{0,2},{1,3},{2,0},{3,1},{4,6},{5,7},{6,4},{7,5},{8,10},{9,11},{10,... | collective-permute-start | bytes 1572872 | tf_op jit(solution)/shard_map/ppermute | solution.py:67
  109.6 21.8 %collective-permute-start.10 = (bf16[256,1024]{1,0:T(8,128)(2,1)S(1)}, bf16[256,1024]{1,0:T(8,128)(2,1)S(1)}, u32[]{:S(2)}, u32[]{:S(2)}) collective-permute-start(bf16[256,1024]{1,0:T(8,128)(2,1)S(1)} %add_convert_fusion.9), channel_id=1, source_target_pairs={{0,1},{1,0},{2,3},{3,2},{4,5},{5,4},{6,7},{7,6},{8,9},{9,8},{10,11... | collective-permute-start | bytes 1572872 | tf_op jit(solution)/shard_map/ppermute | solution.py:67
  148.6 17.8 %collective-permute-start.15 = (bf16[256,1024]{1,0:T(8,128)(2,1)S(1)}, bf16[256,1024]{1,0:T(8,128)(2,1)S(1)}, u32[]{:S(2)}, u32[]{:S(2)}) collective-permute-start(bf16[256,1024]{1,0:T(8,128)(2,1)S(1)} %collective-permute-done.12.refs_2_), channel_id=1, source_target_pairs={{0,1},{1,0},{2,3},{3,2},{4,5},{5,4},{6,7},{7,6},{8,9},{9,8},{10,11... | collective-permute-start | bytes 1572872 | tf_op jit(solution)/shard_map/ppermute | solution.py:67
  150.1 16.4 %collective-permute-start.16 = (bf16[256,1024]{1,0:T(8,128)(2,1)S(1)}, bf16[256,1024]{1,0:T(8,128)(2,1)S(1)}, u32[]{:S(2)}, u32[]{:S(2)}) collective-permute-start(bf16[256,1024]{1,0:T(8,128)(2,1)S(1)} %collective-permute-done.13.refs_3_), channel_id=1, source_target_pairs={{0,2},{1,3},{2,0},{3,1},{4,6},{5,7},{6,4},{7,5},{8,10},{9,11},{10,... | collective-permute-start | bytes 1572872 | tf_op jit(solution)/shard_map/ppermute | solution.py:67
  151.4 32.1 %collective-permute-start.11 = (bf16[256,1024]{1,0:T(8,128)(2,1)S(1)}, bf16[256,1024]{1,0:T(8,128)(2,1)S(1)}, u32[]{:S(2)}, u32[]{:S(2)}) collective-permute-start(bf16[256,1024]{1,0:T(8,128)(2,1)S(1)} %get-tuple-element.223.refs_1_), channel_id=1, source_target_pairs={{0,1},{1,0},{2,3},{3,2},{4,5},{5,4},{6,7},{7,6},{8,9},{9,8},{10,11... | collective-permute-start | bytes 1572872 | tf_op jit(solution)/shard_map/ppermute | solution.py:67
  152.9 30.6 %collective-permute-start.14 = (bf16[256,1024]{1,0:T(8,128)(2,1)S(1)}, bf16[256,1024]{1,0:T(8,128)(2,1)S(1)}, u32[]{:S(2)}, u32[]{:S(2)}) collective-permute-start(bf16[256,1024]{1,0:T(8,128)(2,1)S(1)} %get-tuple-element.224.refs_2_), channel_id=1, source_target_pairs={{0,2},{1,3},{2,0},{3,1},{4,6},{5,7},{6,4},{7,5},{8,10},{9,11},{10,... | collective-permute-start | bytes 1572872 | tf_op jit(solution)/shard_map/ppermute | solution.py:67
  181.0 26.9 %collective-permute-start.18 = (bf16[256,1024]{1,0:T(8,128)(2,1)}, bf16[256,1024]{1,0:T(8,128)(2,1)S(1)}, u32[]{:S(2)}, u32[]{:S(2)}) collective-permute-start(bf16[256,1024]{1,0:T(8,128)(2,1)} %get-tuple-element.240), channel_id=1, source_target_pairs={{0,2},{1,3},{2,0},{3,1},{4,6},{5,7},{6,4},{7,5},{8,10},{9,11},{10,... | collective-permute-start | bytes 1572872 | tf_op jit(solution)/shard_map/ppermute | solution.py:67
  183.0 26.3 %collective-permute-start.19 = (bf16[256,1024]{1,0:T(8,128)(2,1)}, bf16[256,1024]{1,0:T(8,128)(2,1)S(1)}, u32[]{:S(2)}, u32[]{:S(2)}) collective-permute-start(bf16[256,1024]{1,0:T(8,128)(2,1)} %get-tuple-element.242), channel_id=1, source_target_pairs={{0,1},{1,0},{2,3},{3,2},{4,5},{5,4},{6,7},{7,6},{8,9},{9,8},{10,11... | collective-permute-start | bytes 1572872 | tf_op jit(solution)/shard_map/ppermute | solution.py:67
  220.3 328.3 %reduce-scatter.13.cloned.1.call-start = ((), (), s32[]{:S(2)}) async-start(), calls=%async_computation.9 | async-start | bytes 6340608 | tf_op jit(solution)/shard_map/reduce_scatter | solution.py:774
  221.3 22.3 %collective-permute-start.17 = (bf16[256,1024]{1,0:T(8,128)(2,1)S(1)}, bf16[256,1024]{1,0:T(8,128)(2,1)S(1)}, u32[]{:S(2)}, u32[]{:S(2)}) collective-permute-start(bf16[256,1024]{1,0:T(8,128)(2,1)S(1)} %copy-done.87), channel_id=1, source_target_pairs={{0,1},{1,0},{2,3},{3,2},{4,5},{5,4},{6,7},{7,6},{8,9},{9,8},{10,11... | collective-permute-start | bytes 1572872 | tf_op jit(solution)/shard_map/ppermute | solution.py:67
  222.8 20.7 %collective-permute-start.21 = (bf16[256,1024]{1,0:T(8,128)(2,1)S(1)}, bf16[256,1024]{1,0:T(8,128)(2,1)S(1)}, u32[]{:S(2)}, u32[]{:S(2)}) collective-permute-start(bf16[256,1024]{1,0:T(8,128)(2,1)S(1)} %copy-done.86), channel_id=1, source_target_pairs={{0,2},{1,3},{2,0},{3,1},{4,6},{5,7},{6,4},{7,5},{8,10},{9,11},{10,... | collective-permute-start | bytes 1572872 | tf_op jit(solution)/shard_map/ppermute | solution.py:67
  222.8 20.7 %collective-permute-start.20 = (bf16[256,1024]{1,0:T(8,128)(2,1)S(1)}, bf16[256,1024]{1,0:T(8,128)(2,1)S(1)}, u32[]{:S(2)}, u32[]{:S(2)}) collective-permute-start(bf16[256,1024]{1,0:T(8,128)(2,1)S(1)} %add_convert_fusion.6), channel_id=1, source_target_pairs={{0,2},{1,3},{2,0},{3,1},{4,6},{5,7},{6,4},{7,5},{8,10},{9,11},{10,... | collective-permute-start | bytes 1572872 | tf_op jit(solution)/shard_map/ppermute | solution.py:67
  224.8 18.7 %collective-permute-start.22 = (bf16[256,1024]{1,0:T(8,128)(2,1)S(1)}, bf16[256,1024]{1,0:T(8,128)(2,1)S(1)}, u32[]{:S(2)}, u32[]{:S(2)}) collective-permute-start(bf16[256,1024]{1,0:T(8,128)(2,1)S(1)} %add_convert_fusion.7), channel_id=1, source_target_pairs={{0,1},{1,0},{2,3},{3,2},{4,5},{5,4},{6,7},{7,6},{8,9},{9,8},{10,11... | collective-permute-start | bytes 1572872 | tf_op jit(solution)/shard_map/ppermute | solution.py:67
  269.3 279.3 %reduce-scatter.11.cloned.1.call-start = ((), (), s32[]{:S(2)}) async-start(), calls=%async_computation.8 | async-start | bytes 2359296 | tf_op jit(solution)/shard_map/reduce_scatter | solution.py:774
  269.3 13.8 %collective-permute-start.23 = (bf16[256,1024]{1,0:T(8,128)(2,1)}, bf16[256,1024]{1,0:T(8,128)(2,1)}, u32[]{:S(2)}, u32[]{:S(2)}) collective-permute-start(bf16[256,1024]{1,0:T(8,128)(2,1)} %copy-done.46), channel_id=1, source_target_pairs={{0,1},{1,0},{2,3},{3,2},{4,5},{5,4},{6,7},{7,6},{8,9},{9,8},{10,11... | collective-permute-start | bytes 1572872 | tf_op jit(solution)/shard_map/ppermute | solution.py:67
  272.6 20.1 %collective-permute-start.25 = (bf16[256,1024]{1,0:T(8,128)(2,1)}, bf16[256,1024]{1,0:T(8,128)(2,1)}, u32[]{:S(2)}, u32[]{:S(2)}) collective-permute-start(bf16[256,1024]{1,0:T(8,128)(2,1)} %copy-done.50), channel_id=1, source_target_pairs={{0,1},{1,0},{2,3},{3,2},{4,5},{5,4},{6,7},{7,6},{8,9},{9,8},{10,11... | collective-permute-start | bytes 1572872 | tf_op jit(solution)/shard_map/ppermute | solution.py:67
  273.2 20.7 %collective-permute-start.28 = (bf16[256,1024]{1,0:T(8,128)(2,1)}, bf16[256,1024]{1,0:T(8,128)(2,1)}, u32[]{:S(2)}, u32[]{:S(2)}) collective-permute-start(bf16[256,1024]{1,0:T(8,128)(2,1)} %copy-done.52), channel_id=1, source_target_pairs={{0,2},{1,3},{2,0},{3,1},{4,6},{5,7},{6,4},{7,5},{8,10},{9,11},{10,... | collective-permute-start | bytes 1572872 | tf_op jit(solution)/shard_map/ppermute | solution.py:67
  330.5 34.6 %collective-permute-start.33 = (bf16[256,1024]{1,0:T(8,128)(2,1)}, bf16[256,1024]{1,0:T(8,128)(2,1)}, u32[]{:S(2)}, u32[]{:S(2)}) collective-permute-start(bf16[256,1024]{1,0:T(8,128)(2,1)} %copy-done.75), channel_id=1, source_target_pairs={{0,1},{1,0},{2,3},{3,2},{4,5},{5,4},{6,7},{7,6},{8,9},{9,8},{10,11... | collective-permute-start | bytes 1572872 | tf_op jit(solution)/shard_map/ppermute | solution.py:67
  332.3 32.8 %collective-permute-start.35 = (bf16[256,1024]{1,0:T(8,128)(2,1)}, bf16[256,1024]{1,0:T(8,128)(2,1)}, u32[]{:S(2)}, u32[]{:S(2)}) collective-permute-start(bf16[256,1024]{1,0:T(8,128)(2,1)} %copy-done.74), channel_id=1, source_target_pairs={{0,2},{1,3},{2,0},{3,1},{4,6},{5,7},{6,4},{7,5},{8,10},{9,11},{10,... | collective-permute-start | bytes 1572872 | tf_op jit(solution)/shard_map/ppermute | solution.py:67
  339.3 213.4 %reduce-scatter.9.cloned.1.call-start = ((), (), s32[]{:S(2)}) async-start(), calls=%async_computation.7 | async-start | bytes 6340608 | tf_op jit(solution)/shard_map/reduce_scatter | solution.py:774
  339.4 25.7 %collective-permute-start.34 = (bf16[256,1024]{1,0:T(8,128)(2,1)}, bf16[256,1024]{1,0:T(8,128)(2,1)S(1)}, u32[]{:S(2)}, u32[]{:S(2)}) collective-permute-start(bf16[256,1024]{1,0:T(8,128)(2,1)} %add_convert_fusion.4), channel_id=1, source_target_pairs={{0,2},{1,3},{2,0},{3,1},{4,6},{5,7},{6,4},{7,5},{8,10},{9,11},{10,... | collective-permute-start | bytes 1572872 | tf_op jit(solution)/shard_map/ppermute | solution.py:67
  340.9 24.2 %collective-permute-start.36 = (bf16[256,1024]{1,0:T(8,128)(2,1)}, bf16[256,1024]{1,0:T(8,128)(2,1)S(1)}, u32[]{:S(2)}, u32[]{:S(2)}) collective-permute-start(bf16[256,1024]{1,0:T(8,128)(2,1)} %add_convert_fusion.5), channel_id=1, source_target_pairs={{0,1},{1,0},{2,3},{3,2},{4,5},{5,4},{6,7},{7,6},{8,9},{9,8},{10,11... | collective-permute-start | bytes 1572872 | tf_op jit(solution)/shard_map/ppermute | solution.py:67
  342.6 39.9 %collective-permute-start.32 = (bf16[2,1024,256]{2,1,0:T(8,128)(2,1)S(1)}, bf16[2,1024,256]{2,1,0:T(8,128)(2,1)S(1)}, u32[]{:S(2)}, u32[]{:S(2)}) collective-permute-start(bf16[2,1024,256]{2,1,0:T(8,128)(2,1)S(1)} %add_convert_fusion.1), channel_id=1, source_target_pairs={{8,0},{12,4},{16,8},{20,12},{24,16},{28,20},{9,1},{13,5},{17,9},{2... | collective-permute-start | bytes 3145736 | tf_op jit(solution)/shard_map/ppermute | solution.py:877
  385.9 14.8 %collective-permute-start.38 = (bf16[256,1024]{1,0:T(8,128)(2,1)S(1)}, bf16[256,1024]{1,0:T(8,128)(2,1)S(1)}, u32[]{:S(2)}, u32[]{:S(2)}) collective-permute-start(bf16[256,1024]{1,0:T(8,128)(2,1)S(1)} %get-tuple-element.303.refs_1_), channel_id=1, source_target_pairs={{0,2},{1,3},{2,0},{3,1},{4,6},{5,7},{6,4},{7,5},{8,10},{9,11},{10,... | collective-permute-start | bytes 1572872 | tf_op jit(solution)/shard_map/ppermute | solution.py:67
  387.1 15.0 %collective-permute-start.40 = (bf16[256,1024]{1,0:T(8,128)(2,1)S(1)}, bf16[256,1024]{1,0:T(8,128)(2,1)S(1)}, u32[]{:S(2)}, u32[]{:S(2)}) collective-permute-start(bf16[256,1024]{1,0:T(8,128)(2,1)S(1)} %get-tuple-element.304.refs_5_), channel_id=1, source_target_pairs={{0,1},{1,0},{2,3},{3,2},{4,5},{5,4},{6,7},{7,6},{8,9},{9,8},{10,11... | collective-permute-start | bytes 1572872 | tf_op jit(solution)/shard_map/ppermute | solution.py:67
  388.4 38.3 %collective-permute-start.44 = (bf16[2,1024,256]{2,1,0:T(8,128)(2,1)S(1)}, bf16[2,1024,256]{2,1,0:T(8,128)(2,1)S(1)}, u32[]{:S(2)}, u32[]{:S(2)}) collective-permute-start(bf16[2,1024,256]{2,1,0:T(8,128)(2,1)S(1)} %add_convert_fusion), channel_id=1, source_target_pairs={{8,0},{12,4},{16,8},{20,12},{24,16},{28,20},{9,1},{13,5},{17,9},{2... | collective-permute-start | bytes 3145736 | tf_op jit(solution)/shard_map/ppermute | solution.py:884
  389.7 23.5 %collective-permute-start.37 = (bf16[256,1024]{1,0:T(8,128)(2,1)S(1)}, bf16[256,1024]{1,0:T(8,128)(2,1)S(1)}, u32[]{:S(2)}, u32[]{:S(2)}) collective-permute-start(bf16[256,1024]{1,0:T(8,128)(2,1)S(1)} %get-tuple-element.303.refs_1_), channel_id=1, source_target_pairs={{0,1},{1,0},{2,3},{3,2},{4,5},{5,4},{6,7},{7,6},{8,9},{9,8},{10,11... | collective-permute-start | bytes 1572872 | tf_op jit(solution)/shard_map/ppermute | solution.py:67
  390.9 22.3 %collective-permute-start.41 = (bf16[256,1024]{1,0:T(8,128)(2,1)S(1)}, bf16[256,1024]{1,0:T(8,128)(2,1)S(1)}, u32[]{:S(2)}, u32[]{:S(2)}) collective-permute-start(bf16[256,1024]{1,0:T(8,128)(2,1)S(1)} %get-tuple-element.304.refs_5_), channel_id=1, source_target_pairs={{0,2},{1,3},{2,0},{3,1},{4,6},{5,7},{6,4},{7,5},{8,10},{9,11},{10,... | collective-permute-start | bytes 1572872 | tf_op jit(solution)/shard_map/ppermute | solution.py:67
  400.7 22.9 %collective-permute-start.39 = (bf16[256,1024]{1,0:T(8,128)(2,1)S(1)}, bf16[256,1024]{1,0:T(8,128)(2,1)S(1)}, u32[]{:S(2)}, u32[]{:S(2)}) collective-permute-start(bf16[256,1024]{1,0:T(8,128)(2,1)S(1)} %collective-permute-done.38.refs_3_), channel_id=1, source_target_pairs={{0,1},{1,0},{2,3},{3,2},{4,5},{5,4},{6,7},{7,6},{8,9},{9,8},{10,11... | collective-permute-start | bytes 1572872 | tf_op jit(solution)/shard_map/ppermute | solution.py:67
  402.1 21.5 %collective-permute-start.42 = (bf16[256,1024]{1,0:T(8,128)(2,1)S(1)}, bf16[256,1024]{1,0:T(8,128)(2,1)S(1)}, u32[]{:S(2)}, u32[]{:S(2)}) collective-permute-start(bf16[256,1024]{1,0:T(8,128)(2,1)S(1)} %collective-permute-done.40.refs_6_), channel_id=1, source_target_pairs={{0,2},{1,3},{2,0},{3,1},{4,6},{5,7},{6,4},{7,5},{8,10},{9,11},{10,... | collective-permute-start | bytes 1572872 | tf_op jit(solution)/shard_map/ppermute | solution.py:67
  427.7 125.0 %reduce-scatter.7.cloned.1.call-start = ((), (), s32[]{:S(2)}) async-start(), calls=%async_computation.6 | async-start | bytes 3538944 | tf_op jit(solution)/shard_map/reduce_scatter | solution.py:774
  444.4 20.0 %collective-permute-start.46 = (bf16[256,1024]{1,0:T(8,128)(2,1)}, bf16[256,1024]{1,0:T(8,128)(2,1)}, u32[]{:S(2)}, u32[]{:S(2)}) collective-permute-start(bf16[256,1024]{1,0:T(8,128)(2,1)} %get-tuple-element.339.refs_9_), channel_id=1, source_target_pairs={{0,2},{1,3},{2,0},{3,1},{4,6},{5,7},{6,4},{7,5},{8,10},{9,11},{10,... | collective-permute-start | bytes 1572872 | tf_op jit(solution)/shard_map/ppermute | solution.py:67
  445.3 21.5 %collective-permute-start.47 = (bf16[256,1024]{1,0:T(8,128)(2,1)}, bf16[256,1024]{1,0:T(8,128)(2,1)}, u32[]{:S(2)}, u32[]{:S(2)}) collective-permute-start(bf16[256,1024]{1,0:T(8,128)(2,1)} %get-tuple-element.338.refs_8_), channel_id=1, source_target_pairs={{0,1},{1,0},{2,3},{3,2},{4,5},{5,4},{6,7},{7,6},{8,9},{9,8},{10,11... | collective-permute-start | bytes 1572872 | tf_op jit(solution)/shard_map/ppermute | solution.py:67
  468.9 106.3 %reduce-scatter.17.cloned.1.call-start = ((), (), s32[]{:S(2)}) async-start(), calls=%async_computation.11 | async-start | bytes 3538944 | tf_op jit(solution)/shard_map/reduce_scatter | solution.py:774
  470.0 15.8 %collective-permute-start.45 = (bf16[256,1024]{1,0:T(8,128)(2,1)S(1)}, bf16[256,1024]{1,0:T(8,128)(2,1)S(1)}, u32[]{:S(2)}, u32[]{:S(2)}) collective-permute-start(bf16[256,1024]{1,0:T(8,128)(2,1)S(1)} %copy-done.57), channel_id=1, source_target_pairs={{0,1},{1,0},{2,3},{3,2},{4,5},{5,4},{6,7},{7,6},{8,9},{9,8},{10,11... | collective-permute-start | bytes 1572872 | tf_op jit(solution)/shard_map/ppermute | solution.py:67
  470.7 15.1 %collective-permute-start.49 = (bf16[256,1024]{1,0:T(8,128)(2,1)S(1)}, bf16[256,1024]{1,0:T(8,128)(2,1)S(1)}, u32[]{:S(2)}, u32[]{:S(2)}) collective-permute-start(bf16[256,1024]{1,0:T(8,128)(2,1)S(1)} %copy-done.55), channel_id=1, source_target_pairs={{0,2},{1,3},{2,0},{3,1},{4,6},{5,7},{6,4},{7,5},{8,10},{9,11},{10,... | collective-permute-start | bytes 1572872 | tf_op jit(solution)/shard_map/ppermute | solution.py:67
  471.8 22.6 %collective-permute-start.48 = (bf16[256,1024]{1,0:T(8,128)(2,1)}, bf16[256,1024]{1,0:T(8,128)(2,1)S(1)}, u32[]{:S(2)}, u32[]{:S(2)}) collective-permute-start(bf16[256,1024]{1,0:T(8,128)(2,1)} %add_convert_fusion.2), channel_id=1, source_target_pairs={{0,2},{1,3},{2,0},{3,1},{4,6},{5,7},{6,4},{7,5},{8,10},{9,11},{10,... | collective-permute-start | bytes 1572872 | tf_op jit(solution)/shard_map/ppermute | solution.py:67
  472.7 21.7 %collective-permute-start.50 = (bf16[256,1024]{1,0:T(8,128)(2,1)}, bf16[256,1024]{1,0:T(8,128)(2,1)S(1)}, u32[]{:S(2)}, u32[]{:S(2)}) collective-permute-start(bf16[256,1024]{1,0:T(8,128)(2,1)} %add_convert_fusion.3), channel_id=1, source_target_pairs={{0,1},{1,0},{2,3},{3,2},{4,5},{5,4},{6,7},{7,6},{8,9},{9,8},{10,11... | collective-permute-start | bytes 1572872 | tf_op jit(solution)/shard_map/ppermute | solution.py:67
  543.7 36.4 %collective-permute-start.52 = (bf16[256,1024]{1,0:T(8,128)(2,1)S(1)}, bf16[256,1024]{1,0:T(8,128)(2,1)S(1)}, u32[]{:S(2)}, u32[]{:S(2)}) collective-permute-start(bf16[256,1024]{1,0:T(8,128)(2,1)S(1)} %collective-permute-done.51.refs_3_), channel_id=1, source_target_pairs={{0,1},{1,0},{2,3},{3,2},{4,5},{5,4},{6,7},{7,6},{8,9},{9,8},{10,11... | collective-permute-start | bytes 1572872 | tf_op jit(solution)/shard_map/ppermute | solution.py:67
  544.8 35.3 %collective-permute-start.54 = (bf16[256,1024]{1,0:T(8,128)(2,1)}, bf16[256,1024]{1,0:T(8,128)(2,1)S(1)}, u32[]{:S(2)}, u32[]{:S(2)}) collective-permute-start(bf16[256,1024]{1,0:T(8,128)(2,1)} %collective-permute-done.53.refs_5_), channel_id=1, source_target_pairs={{0,2},{1,3},{2,0},{3,1},{4,6},{5,7},{6,4},{7,5},{8,10},{9,11},{10,... | collective-permute-start | bytes 1572872 | tf_op jit(solution)/shard_map/ppermute | solution.py:67
  (108 other events, 1131.8 us)
Sparse Core Ops, SparseCore 0:
  220.4 64.8 reduce-scatter.14
  287.7 61.9 reduce-scatter.12
  352.0 42.5 reduce-scatter.10
  427.8 64.4 reduce-scatter.8
  494.6 38.9 reduce-scatter.6
  535.8 39.3 reduce-scatter.16

commit v4 on v3

--- a/solution.py
+++ b/solution.py
@@ -49,6 +49,9 @@
         cost_estimate=pl.CostEstimate(flops=weight, bytes_accessed=0, transcendentals=0),
         name=name,
     )(*args, *into)
+
+
+RESIDENT = pl.BlockSpec(memory_space=pltpu.VMEM)
 
 
 def fixed(shape):
@@ -581,12 +584,12 @@
         lambda *refs: mlp_kernel(count, *refs),
         (count,),
         [fixed((rows, half))] * (2 * count)
-        + [pl.BlockSpec((rows, hid), mine), fixed((hid, width)), fixed((hid, width))],
+        + [pl.BlockSpec((rows, hid), mine), RESIDENT, RESIDENT],
         [pl.BlockSpec((rows, width), mine)] + [pl.BlockSpec((rows, hid), mine)] * 3 + specs,
         [((tokens, width), BF16)] + [((tokens, hid), BF16)] * 3 + outs,
         (scal, *left, *right, d_act, w_gate, w_up),
         "mlp",
-        vmem=56,
+        vmem=34,
         into=into,
     )
     return results[:4], results[4:]
@@ -919,10 +922,11 @@
         after = tied(grad, after)
         grads.append(after)
     after = (after, placed)
-    for grad in (grad_up, grad_first, grad_second):
+    for grad in (grad_up, grad_first):
         after = tied(grad, after)
         grads.append(after)
-    grad_down, grad_gate, grad_out, grad_up, grad_first, grad_second = grads
+    grad_second = tied(grad_second, (after, grad_input))
+    grad_down, grad_gate, grad_out, grad_up, grad_first = grads
     part = w_query.shape[1] // GROUPS
     grad_query, grad_key, grad_value = (
         jnp.concatenate([g[:, k * part : (k + 1) * part] for g in (grad_first, grad_second)], axis=1).astype(F32)

time: 597 us -> 587 us (0.983)
  Pallas kernels: 283 us -> 274 us
    pallas_call x30, Pallas kernels: 273 us -> 264 us  [call(): pl.pallas_call(body, grid_spec=pltpu.PrefetchScalarGridSpec(num_scalar_pr...]
    unnamed x176 -> x162, local copies, waits for them, and re-layouts: 30.6 us -> 35.4 us
  transfers between devices with their start and end apart: 68 -> 68, of which waited for: 21 -> 27; matrix products, arithmetic and copies ran while one was open for 4% -> 3% of each run, Pallas kernels for 42% -> 42%
where the time goes in v4:
time: 587 us; the launch traced here: 579 us
  Pallas kernels  274 us (47%)
  waiting for transfers between devices  156 us (27%)
  starting transfers between devices  72.6 us (12%)
  local copies, waits for them, and re-layouts  38.5 us (7%)
  other arithmetic  22.4 us (4%)
  between operations  15.5 us (3%)
    pallas_call x30, Pallas kernels, call(): pl.pallas_call(body, grid_spec=pltpu.PrefetchScalarGridSpec(num_scalar_pr...  264 us
    ppermute x55, waiting for transfers between devices, swap(): return lax.ppermute(array, axis, [(i, i ^ bit) for i in range(size)])  96.6 us
    ppermute x55, starting transfers between devices, swap(): return lax.ppermute(array, axis, [(i, i ^ bit) for i in range(size)])  55.7 us
    unnamed x162, local copies, waits for them, and re-layouts  35.4 us
    ppermute x2, waiting for transfers between devices, on_device(): twos = [lax.ppermute(own, 'seq', right_two) for own in packed]  23.7 us
    ppermute x1, waiting for transfers between devices, on_device(): back_two = lax.ppermute(sent, 'seq', left_two)  16.7 us
    reduce_scatter x6, waiting for transfers between devices, scattered(): return lax.psum_scatter(grad, 'seq', scatter_dimension=dim, tiled=True)  15.8 us
  transfers between devices with their start and end apart: 68, of which 27 were waited for; matrix products, arithmetic and copies ran while one was open for 3% of the time, Pallas kernels for 42%

profile of v4, /device:TPU:0, one launch (start us, length us, event | category | flops | bytes accessed | tf_op | source)
XLA Modules:
  0.0 578.8 jit_solution(2898616858616511728)
XLA Ops:
  10.9 10.2 %project_keys.1 = (bf16[1024,2048]{1,0:T(8,128)(2,1)}, bf16[4,1024,256]{2,1,0:T(8,128)(2,1)S(1)}, bf16[2,1024,256]{2,1,0:T(8,128)(2,1)S(1)}, bf16[2,1024,256]{2,1,0:T(8,128)(2,1)S(1)}) custom-call(s32[2]{0:T(128)S(1)} %pad_add_fusion.2.me_ref.refs_0_._.s_ref_, bf16[1024,2048]{1,0:T(8,128)(2,1)} %refs_0_.3, f32[1,2048]{1,0:T(1,128)S(1)} %bitcast.27, ...), custom_call_target="tpu_custom_call" | custom-call | tf_op jit(solution)/shard_map/project_keys/pallas_call | solution.py:37
  21.1 5.0 collective-permute-start
  27.7 5.6 project_query.1.refs_1_
  33.4 15.1 %collective-permute-done.refs_2_ = bf16[2,1024,256]{2,1,0:T(8,128)(2,1)S(1)} collective-permute-done((bf16[2,1024,256]{2,1,0:T(8,128)(2,1)S(1)}, bf16[2,1024,256]{2,1,0:T(8,128)(2,1)S(1)}, u32[]{:S(2)}, u32[]{:S(2)}) %collective-permute-start) | collective-permute-done | bytes 1048608 | tf_op jit(solution)/shard_map/ppermute | solution.py:814
  49.8 4.5 collective-permute-start.3
  55.6 13.2 %attend.3 = (bf16[1024,256]{1,0:T(8,128)(2,1)S(1)}, f32[2,1,1024]{2,1,0:T(1,128)S(1)}) custom-call(s32[2]{0:T(128)S(1)} %pad_add_fusion.2.me_ref.refs_0_._.s_ref_, bf16[1024,512]{1,0:T(8,128)(2,1)S(1)} %project_query.1.refs_1_, bf16[2,1024,256]{2,1,0:T(8,128)(2,1)S(1)} %collective-permute-done.refs_2_, bf16[4,1024,256]{2,1,0:T(8,128)(2,1)} %copy-done.76, ...), custom_call_target="tpu_custom_call" | custom-call | tf_op jit(solution)/shard_map/attend/pallas_call | solution.py:37
  68.8 8.7 %collective-permute-done.3.refs_2_ = bf16[2,1024,256]{2,1,0:T(8,128)(2,1)S(1)} collective-permute-done((bf16[2,1024,256]{2,1,0:T(8,128)(2,1)S(1)}, bf16[2,1024,256]{2,1,0:T(8,128)(2,1)S(1)}, u32[]{:S(2)}, u32[]{:S(2)}) %collective-permute-start.3) | collective-permute-done | bytes 1048608 | tf_op jit(solution)/shard_map/ppermute | solution.py:814
  79.2 3.0 collective-permute-done.4.refs_4_
  82.3 4.7 attend.4
  91.3 10.5 %attend.5 = (bf16[1024,256]{1,0:T(8,128)(2,1)S(1)}, f32[2,1,1024]{2,1,0:T(1,128)S(1)}) custom-call(s32[2]{0:T(128)S(1)} %pad_add_fusion.2.me_ref.refs_0_._.s_ref_, bf16[1024,512]{1,0:T(8,128)(2,1)S(1)} %project_query.1.refs_1_, bf16[2,1024,256]{2,1,0:T(8,128)(2,1)S(1)} %collective-permute-done.3.refs_2_, ...), custom_call_target="tpu_custom_call", output_to_operand_aliasing={{0}: (7, {}), {1}: (8, {})} | custom-call | tf_op jit(solution)/shard_map/attend/pallas_call | solution.py:37
  101.8 4.6 project_out.3
  111.1 12.1 %project_cotangent.1 = (bf16[1024,2048]{1,0:T(8,128)(2,1)S(1)}, f32[1024,1376]{1,0:T(8,128)}) custom-call(s32[2]{0:T(128)S(1)} %pad_add_fusion.2.me_ref.refs_0_._.s_ref_, bf16[1024,2048]{1,0:T(8,128)(2,1)} %refs_2_.5, bf16[1376,2048]{1,0:T(8,128)(2,1)} %refs_2_.4), custom_call_target="tpu_custom_call" | custom-call | tf_op jit(solution)/shard_map/project_cotangent/pallas_call | solution.py:37
  125.1 6.3 %collective-permute-done.8.refs_4_ = bf16[256,1024]{1,0:T(8,128)(2,1)S(1)} collective-permute-done((bf16[256,1024]{1,0:T(8,128)(2,1)S(1)}, bf16[256,1024]{1,0:T(8,128)(2,1)S(1)}, u32[]{:S(2)}, u32[]{:S(2)}) %collective-permute-start.8) | collective-permute-done | bytes 524320 | tf_op jit(solution)/shard_map/ppermute | solution.py:70
  131.4 4.9 mid.1
  138.3 10.2 %collective-permute-done.12.refs_2_ = bf16[256,1024]{1,0:T(8,128)(2,1)S(1)} collective-permute-done((bf16[256,1024]{1,0:T(8,128)(2,1)S(1)}, bf16[256,1024]{1,0:T(8,128)(2,1)S(1)}, u32[]{:S(2)}, u32[]{:S(2)}) %collective-permute-start.12) | collective-permute-done | bytes 524320 | tf_op jit(solution)/shard_map/ppermute | solution.py:70
  152.9 10.6 %mlp.3 = (bf16[1024,2048]{1,0:T(8,128)(2,1)S(1)}, bf16[1024,1376]{1,0:T(8,128)(2,1)S(1)}, bf16[1024,1376]{1,0:T(8,128)(2,1)S(1)}, bf16[1024,1376]{1,0:T(8,128)(2...) custom-call(s32[2]{0:T(128)S(1)} %pad_add_fusion.2.me_ref.refs_0_._.s_ref_, ...), custom_call_target="tpu_custom_call" | custom-call | tf_op jit(solution)/shard_map/mlp/pallas_call | solution.py:37
  164.9 10.8 %mlp.4 = (bf16[1024,2048]{1,0:T(8,128)(2,1)S(1)}, bf16[1024,1376]{1,0:T(8,128)(2,1)S(1)}, bf16[1024,1376]{1,0:T(8,128)(2,1)S(1)}, bf16[1024,1376]{1,0:T(8,128)(2...) custom-call(s32[2]{0:T(128)S(1)} %pad_add_fusion.2.me_ref.refs_0_._., ...), custom_call_target="tpu_custom_call", output_to_operand_aliasing={{0}: (6, {}), {1}: (7, {}), {2}: (8, {}), {3}: (9, {})} | custom-call | tf_op jit(solution)/shard_map/mlp/pallas_call | solution.py:37
  178.6 19.6 %mlp.5 = (bf16[1024,2048]{1,0:T(8,128)(2,1)S(1)}, bf16[1024,1376]{1,0:T(8,128)(2,1)S(1)}, bf16[1024,1376]{1,0:T(8,128)(2,1)S(1)}, bf16[1024,1376]{1,0:T(8,128)(2...) custom-call(s32[2]{0:T(128)S(1)} %pad_add_fusion.2.me_ref.refs_0_._., ...), custom_call_target="tpu_custom_call", output_to_operand_aliasing={{0}: (8, {}), {1}: (9, {}), {2}: (10, {}), {3}: (11, {})} | custom-call | tf_op jit(solution)/shard_map/mlp/pallas_call | solution.py:37
  207.0 9.7 %grad_down.1 = bf16[1376,2048]{1,0:T(8,128)(2,1)} custom-call(s32[2]{0:T(128)S(1)} %pad_add_fusion.2.me_ref.refs_0_._.s_ref_, bf16[1024,1376]{1,0:T(8,128)(2,1)S(1)} %copy-done.2, bf16[1024,2048]{1,0:T(8,128)(2,1)} %copy-done.21), custom_call_target="tpu_custom_call" | custom-call | tf_op jit(solution)/shard_map/grad_down/pallas_call | solution.py:37
  220.9 11.8 %project_down.1 = (bf16[256,1024]{1,0:T(8,128)(2,1)S(1)}, bf16[256,1024]{1,0:T(8,128)(2,1)S(1)}, bf16[256,1024]{1,0:T(8,128)(2,1)S(1)}, bf16[256,1024]{1,0:T(8,1...) custom-call(s32[2]{0:T(128)S(1)} %pad_add_fusion.2.me_ref.refs_0_._., ...), custom_call_target="tpu_custom_call" | custom-call | tf_op jit(solution)/shard_map/project_down/pallas_call | solution.py:37
  239.1 5.7 d_mid.1
  245.4 8.5 %collective-permute-done.24.refs_3_ = bf16[256,1024]{1,0:T(8,128)(2,1)S(1)} collective-permute-done((bf16[256,1024]{1,0:T(8,128)(2,1)S(1)}, bf16[256,1024]{1,0:T(8,128)(2,1)S(1)}, u32[]{:S(2)}, u32[]{:S(2)}) %collective-permute-start.24) | collective-permute-done | bytes 524320 | tf_op jit(solution)/shard_map/ppermute | solution.py:70
  255.6 9.7 %grad_gate.1 = bf16[1376,2048]{1,0:T(8,128)(2,1)} custom-call(s32[2]{0:T(128)S(1)} %pad_add_fusion.2.me_ref.refs_0_._.s_ref_, bf16[1024,1376]{1,0:T(8,128)(2,1)S(1)} %copy-done.4, bf16[1024,2048]{1,0:T(8,128)(2,1)} %copy-done), custom_call_target="tpu_custom_call" | custom-call | tf_op jit(solution)/shard_map/grad_gate/pallas_call | solution.py:37
  269.5 9.7 %grad_up.1 = bf16[1376,2048]{1,0:T(8,128)(2,1)} custom-call(s32[2]{0:T(128)S(1)} %pad_add_fusion.2.me_ref.refs_0_._.s_ref_, bf16[1024,1376]{1,0:T(8,128)(2,1)S(1)} %copy-done.6, bf16[1024,2048]{1,0:T(8,128)(2,1)} %copy-done), custom_call_target="tpu_custom_call" | custom-call | tf_op jit(solution)/shard_map/grad_up/pallas_call | solution.py:37
  279.2 8.2 %collective-permute-done.25.refs_4_ = bf16[256,1024]{1,0:T(8,128)(2,1)} collective-permute-done((bf16[256,1024]{1,0:T(8,128)(2,1)}, bf16[256,1024]{1,0:T(8,128)(2,1)}, u32[]{:S(2)}, u32[]{:S(2)}) %collective-permute-start.25) | collective-permute-done | bytes 524320 | tf_op jit(solution)/shard_map/ppermute | solution.py:70
  294.7 6.5 %project_back.1 = (bf16[1024,2048]{1,0:T(8,128)(2,1)}, bf16[1024,512]{1,0:T(8,128)(2,1)S(1)}) custom-call(s32[2]{0:T(128)S(1)} %pad_add_fusion.2.me_ref.refs_0_._.s_ref_, bf16[256,1024]{1,0:T(8,128)(2,1)S(1)} %copy-done.49, bf16[256,1024]{1,0:T(8,128)(2,1)} %collective-permute-done.23.refs_2_, bf16[256,1024]{1,0:T(8,128)(2,1)S(1)} %copy-done.53, ...), custom_call_target="tpu_custom_call" | custom-call | tf_op jit(solution)/shard_map/project_back/pallas_call | solution.py:37
  303.2 19.5 %attend_back.2 = (bf16[1024,256]{1,0:T(8,128)(2,1)S(1)}, bf16[2,1024,256]{2,1,0:T(8,128)(2,1)S(1)}, bf16[2,1024,256]{2,1,0:T(8,128)(2,1)}, bf16[2,1024,256]{2,1,0:T(8,128)(2,1)S(1)}) custom-call(s32[2]{0:T(128)S(1)} %pad_add_fusion.2.me_ref.refs_0_._.s_ref_, bf16[1024,512]{1,0:T(8,128)(2,1)} %copy-done.12, bf16[2,1024,256]{2,1,0:T(8,128)(2,1)} %copy-done.38, ...), custom_call_target="tpu_custom_call" | custom-call | flops 69000003584 | tf_op jit(solution)/shard_map/attend_back/pallas_call | solution.py:37
  327.2 6.4 %grad_out.1 = bf16[512,2048]{1,0:T(8,128)(2,1)} custom-call(s32[2]{0:T(128)S(1)} %pad_add_fusion.2.me_ref.refs_0_._.s_ref_, bf16[1024,256]{1,0:T(8,128)(2,1)S(1)} %copy-done.18, bf16[1024,256]{1,0:T(8,128)(2,1)S(1)} %copy-done.16, bf16[1024,2048]{1,0:T(8,128)(2,1)} %get-tuple-element.360.refs_2_), custom_call_target="tpu_custom_call" | custom-call | tf_op jit(solution)/shard_map/grad_out/pallas_call | solution.py:37
  338.9 19.3 %attend_back.3 = (bf16[1024,256]{1,0:T(8,128)(2,1)S(1)}, bf16[2,1024,256]{2,1,0:T(8,128)(2,1)S(1)}, bf16[2,1024,256]{2,1,0:T(8,128)(2,1)S(1)}, bf16[2,1024,256]{2,1,0:T(8,128)(2,1)S(1)}) custom-call(s32[2]{0:T(128)S(1)} %pad_add_fusion.2.me_ref.refs_0_._.s_ref_, bf16[1024,512]{1,0:T(8,128)(2,1)} %copy-done.12, bf16[2,1024,256]{2,1,0:T(8,128)(2,1)} %copy-done.23, ...), custom_call_target="tpu_custom_call" | custom-call | flops 69000003584 | tf_op jit(solution)/shard_map/attend_back/pallas_call | solution.py:37
  360.1 16.7 %collective-permute-done.32.back_ref = bf16[2,1024,256]{2,1,0:T(8,128)(2,1)S(1)} collective-permute-done((bf16[2,1024,256]{2,1,0:T(8,128)(2,1)S(1)}, bf16[2,1024,256]{2,1,0:T(8,128)(2,1)S(1)}, u32[]{:S(2)}, u32[]{:S(2)}) %collective-permute-start.32) | collective-permute-done | bytes 1048608 | tf_op jit(solution)/shard_map/ppermute | solution.py:880
  376.8 3.4 output.1
  386.0 9.0 %collective-permute-done.38.refs_3_ = bf16[256,1024]{1,0:T(8,128)(2,1)S(1)} collective-permute-done((bf16[256,1024]{1,0:T(8,128)(2,1)S(1)}, bf16[256,1024]{1,0:T(8,128)(2,1)S(1)}, u32[]{:S(2)}, u32[]{:S(2)}) %collective-permute-start.38) | collective-permute-done | bytes 524320 | tf_op jit(solution)/shard_map/ppermute | solution.py:70
  397.0 10.1 %collective-permute-done.37.refs_2_ = bf16[256,1024]{1,0:T(8,128)(2,1)S(1)} collective-permute-done((bf16[256,1024]{1,0:T(8,128)(2,1)S(1)}, bf16[256,1024]{1,0:T(8,128)(2,1)S(1)}, u32[]{:S(2)}, u32[]{:S(2)}) %collective-permute-start.37) | collective-permute-done | bytes 524320 | tf_op jit(solution)/shard_map/ppermute | solution.py:70
  407.1 10.5 %collective-permute-done.39.refs_4_ = bf16[256,1024]{1,0:T(8,128)(2,1)S(1)} collective-permute-done((bf16[256,1024]{1,0:T(8,128)(2,1)S(1)}, bf16[256,1024]{1,0:T(8,128)(2,1)S(1)}, u32[]{:S(2)}, u32[]{:S(2)}) %collective-permute-start.39) | collective-permute-done | bytes 524320 | tf_op jit(solution)/shard_map/ppermute | solution.py:70
  417.6 3.0 place.3
  425.1 2.9 finish.2.refs_0_.refs_1_
  432.3 6.1 %project_one_back.2 = (bf16[256,1024]{1,0:T(8,128)(2,1)}, bf16[256,1024]{1,0:T(8,128)(2,1)}) custom-call(s32[2]{0:T(128)S(1)} %pad_add_fusion.2.me_ref.refs_0_._.s_ref_, bf16[1024,768]{1,0:T(8,128)(2,1)S(1)} %copy-done.9, bf16[1024,768]{1,0:T(8,128)(2,1)S(1)} %copy-done.7, bf16[2048,512]{1,0:T(8,128)(2,1)} %refs_2_.7, bf16[2048,512]{1,0:T(8,128)(2,1)} %refs_3_.7, ...), custom_call_target="tpu_custom_call" | custom-call | tf_op jit(solution)/shard_map/project_one_back/pallas_call | solution.py:37
  440.2 8.1 %grad_first.1 = bf16[2048,768]{1,0:T(8,128)(2,1)} custom-call(s32[2]{0:T(128)S(1)} %pad_add_fusion.2.me_ref.refs_0_._.s_ref_, bf16[1024,2048]{1,0:T(8,128)(2,1)} %get-tuple-element.191.h_ref.refs_0_, bf16[1024,768]{1,0:T(8,128)(2,1)S(1)} %copy-done.9), custom_call_target="tpu_custom_call" | custom-call | tf_op jit(solution)/shard_map/grad_first/pallas_call | solution.py:37
  448.3 9.5 %project_one_back.3 = (bf16[256,1024]{1,0:T(8,128)(2,1)S(1)}, bf16[256,1024]{1,0:T(8,128)(2,1)S(1)}, bf16[256,1024]{1,0:T(8,128)(2,1)S(1)}, bf16[256,1024]{1,0:T...) custom-call(s32[2]{0:T(128)S(1)} %pad_add_fusion.2.me_ref.refs_0_._.s_ref_, ...), custom_call_target="tpu_custom_call" | custom-call | tf_op jit(solution)/shard_map/project_one_back/pallas_call | solution.py:37
  467.6 11.7 %gain_back.1 = f32[1,2048]{1,0:T(1,128)S(1)} custom-call(s32[2]{0:T(128)S(1)} %pad_add_fusion.2.me_ref.refs_0_._.s_ref_, bf16[1024,2048]{1,0:T(8,128)(2,1)} %refs_0_.3, bf16[256,1024]{1,0:T(8,128)(2,1)S(1)} %get-tuple-element.340.refs_2_.refs_3_, bf16[256,1024]{1,0:T(8,128)(2,1)S(1)} %get-tuple-element.343.refs_3_.refs_6_, bf16[256,1024]{1,0:T(8,128)(2,1)S(1)} %copy-done.59, ...), custom_call_target="tpu_custom_call" | custom-call | tf_op jit(solution)/shard_map/gain_back/pallas_call | solution.py:37
  479.8 8.7 %collective-permute-done.48.refs_5_ = bf16[256,1024]{1,0:T(8,128)(2,1)S(1)} collective-permute-done((bf16[256,1024]{1,0:T(8,128)(2,1)}, bf16[256,1024]{1,0:T(8,128)(2,1)S(1)}, u32[]{:S(2)}, u32[]{:S(2)}) %collective-permute-start.48) | collective-permute-done | bytes 524320 | tf_op jit(solution)/shard_map/ppermute | solution.py:70
  488.5 5.2 input.1
  495.6 9.5 %collective-permute-done.51.refs_3_ = bf16[256,1024]{1,0:T(8,128)(2,1)S(1)} collective-permute-done((bf16[256,1024]{1,0:T(8,128)(2,1)S(1)}, bf16[256,1024]{1,0:T(8,128)(2,1)S(1)}, u32[]{:S(2)}, u32[]{:S(2)}) %collective-permute-start.51) | collective-permute-done | bytes 524320 | tf_op jit(solution)/shard_map/ppermute | solution.py:70
  505.8 8.3 %grad_second.1 = bf16[2048,768]{1,0:T(8,128)(2,1)} custom-call(s32[2]{0:T(128)S(1)} %pad_add_fusion.2.me_ref.refs_0_._.s_ref_, bf16[1024,2048]{1,0:T(8,128)(2,1)} %get-tuple-element.191.h_ref.refs_0_, bf16[1024,768]{1,0:T(8,128)(2,1)S(1)} %copy-done.8), custom_call_target="tpu_custom_call" | custom-call | tf_op jit(solution)/shard_map/grad_second/pallas_call | solution.py:37
  514.2 3.2 collective-permute-start.57
  525.3 5.2 collective-permute-done.60
  532.6 4.7 place.4.refs_3_
  552.1 15.8 %reduce-scatter.17.cloned.1.call-done = bf16[256,768]{1,0:T(8,128)(2,1)} async-done(((bf16[2048,768]{1,0:T(8,128)(2,1)}), bf16[256,768]{1,0:T(8,128)(2,1)}) %reduce-scatter.17.cloned.1.call-update) | async-done | bytes 393232 | tf_op jit(solution)/shard_map/reduce_scatter | solution.py:777
  (335 shorter events, 137.5 us)
Async XLA Ops:
  7.2 532.6 %reduce-scatter.15.cloned.1.call-start = ((), (), s32[]{:S(2)}) async-start(), calls=%async_computation.10 | async-start | bytes 6340608 | tf_op jit(solution)/shard_map/reduce_scatter | solution.py:777
  21.1 27.3 %collective-permute-start = (bf16[2,1024,256]{2,1,0:T(8,128)(2,1)S(1)}, bf16[2,1024,256]{2,1,0:T(8,128)(2,1)S(1)}, u32[]{:S(2)}, u32[]{:S(2)}) collective-permute-start(bf16[2,1024,256]{2,1,0:T(8,128)(2,1)S(1)} %get-tuple-element.192.refs_5_), channel_id=1, source_target_pairs={{0,8},{4,12},{8,16},{12,20},{16,24},{20,28},{1,9},{5,13},{9,17},{1... | collective-permute-start | bytes 3145736 | tf_op jit(solution)/shard_map/ppermute | solution.py:814
  26.1 28.1 %collective-permute-start.1 = (bf16[4,1024,256]{2,1,0:T(8,128)(2,1)S(1)}, bf16[4,1024,256]{2,1,0:T(8,128)(2,1)S(1)}, u32[]{:S(2)}, u32[]{:S(2)}) collective-permute-start(bf16[4,1024,256]{2,1,0:T(8,128)(2,1)S(1)} %get-tuple-element.194), channel_id=1, source_target_pairs={{0,4},{8,12},{16,20},{24,28},{1,5},{9,13},{17,21},{25,29},{2,6},{1... | collective-permute-start | bytes 6291464 | tf_op jit(solution)/shard_map/ppermute | solution.py:815
  49.8 27.7 %collective-permute-start.3 = (bf16[2,1024,256]{2,1,0:T(8,128)(2,1)S(1)}, bf16[2,1024,256]{2,1,0:T(8,128)(2,1)S(1)}, u32[]{:S(2)}, u32[]{:S(2)}) collective-permute-start(bf16[2,1024,256]{2,1,0:T(8,128)(2,1)S(1)} %get-tuple-element.196.refs_5_), channel_id=1, source_target_pairs={{0,8},{4,12},{8,16},{12,20},{16,24},{20,28},{1,9},{5,13},{9,17},{1... | collective-permute-start | bytes 3145736 | tf_op jit(solution)/shard_map/ppermute | solution.py:814
  88.2 19.4 %collective-permute-start.6 = (bf16[256,1024]{1,0:T(8,128)(2,1)S(1)}, bf16[256,1024]{1,0:T(8,128)(2,1)S(1)}, u32[]{:S(2)}, u32[]{:S(2)}) collective-permute-start(bf16[256,1024]{1,0:T(8,128)(2,1)S(1)} %get-tuple-element.201), channel_id=1, source_target_pairs={{0,2},{1,3},{2,0},{3,1},{4,6},{5,7},{6,4},{7,5},{8,10},{9,11},{10,... | collective-permute-start | bytes 1572872 | tf_op jit(solution)/shard_map/ppermute | solution.py:70
  89.8 18.0 %collective-permute-start.7 = (bf16[256,1024]{1,0:T(8,128)(2,1)S(1)}, bf16[256,1024]{1,0:T(8,128)(2,1)S(1)}, u32[]{:S(2)}, u32[]{:S(2)}) collective-permute-start(bf16[256,1024]{1,0:T(8,128)(2,1)S(1)} %get-tuple-element.200), channel_id=1, source_target_pairs={{0,1},{1,0},{2,3},{3,2},{4,5},{5,4},{6,7},{7,6},{8,9},{9,8},{10,11... | collective-permute-start | bytes 1572872 | tf_op jit(solution)/shard_map/ppermute | solution.py:70
  106.5 18.7 %collective-permute-start.5 = (bf16[256,1024]{1,0:T(8,128)(2,1)S(1)}, bf16[256,1024]{1,0:T(8,128)(2,1)S(1)}, u32[]{:S(2)}, u32[]{:S(2)}) collective-permute-start(bf16[256,1024]{1,0:T(8,128)(2,1)S(1)} %get-tuple-element.206), channel_id=1, source_target_pairs={{0,1},{1,0},{2,3},{3,2},{4,5},{5,4},{6,7},{7,6},{8,9},{9,8},{10,11... | collective-permute-start | bytes 1572872 | tf_op jit(solution)/shard_map/ppermute | solution.py:70
  107.1 18.1 %collective-permute-start.9 = (bf16[256,1024]{1,0:T(8,128)(2,1)S(1)}, bf16[256,1024]{1,0:T(8,128)(2,1)S(1)}, u32[]{:S(2)}, u32[]{:S(2)}) collective-permute-start(bf16[256,1024]{1,0:T(8,128)(2,1)S(1)} %get-tuple-element.211), channel_id=1, source_target_pairs={{0,2},{1,3},{2,0},{3,1},{4,6},{5,7},{6,4},{7,5},{8,10},{9,11},{10,... | collective-permute-start | bytes 1572872 | tf_op jit(solution)/shard_map/ppermute | solution.py:70
  108.0 23.4 %collective-permute-start.8 = (bf16[256,1024]{1,0:T(8,128)(2,1)S(1)}, bf16[256,1024]{1,0:T(8,128)(2,1)S(1)}, u32[]{:S(2)}, u32[]{:S(2)}) collective-permute-start(bf16[256,1024]{1,0:T(8,128)(2,1)S(1)} %add_convert_fusion.8), channel_id=1, source_target_pairs={{0,2},{1,3},{2,0},{3,1},{4,6},{5,7},{6,4},{7,5},{8,10},{9,11},{10,... | collective-permute-start | bytes 1572872 | tf_op jit(solution)/shard_map/ppermute | solution.py:70
  109.6 21.8 %collective-permute-start.10 = (bf16[256,1024]{1,0:T(8,128)(2,1)S(1)}, bf16[256,1024]{1,0:T(8,128)(2,1)S(1)}, u32[]{:S(2)}, u32[]{:S(2)}) collective-permute-start(bf16[256,1024]{1,0:T(8,128)(2,1)S(1)} %add_convert_fusion.9), channel_id=1, source_target_pairs={{0,1},{1,0},{2,3},{3,2},{4,5},{5,4},{6,7},{7,6},{8,9},{9,8},{10,11... | collective-permute-start | bytes 1572872 | tf_op jit(solution)/shard_map/ppermute | solution.py:70
  136.9 13.2 %collective-permute-start.13 = (bf16[256,1024]{1,0:T(8,128)(2,1)S(1)}, bf16[256,1024]{1,0:T(8,128)(2,1)S(1)}, u32[]{:S(2)}, u32[]{:S(2)}) collective-permute-start(bf16[256,1024]{1,0:T(8,128)(2,1)S(1)} %get-tuple-element.224.refs_2_), channel_id=1, source_target_pairs={{0,1},{1,0},{2,3},{3,2},{4,5},{5,4},{6,7},{7,6},{8,9},{9,8},{10,11... | collective-permute-start | bytes 1572872 | tf_op jit(solution)/shard_map/ppermute | solution.py:70
  148.6 15.0 %collective-permute-start.15 = (bf16[256,1024]{1,0:T(8,128)(2,1)S(1)}, bf16[256,1024]{1,0:T(8,128)(2,1)S(1)}, u32[]{:S(2)}, u32[]{:S(2)}) collective-permute-start(bf16[256,1024]{1,0:T(8,128)(2,1)S(1)} %collective-permute-done.12.refs_2_), channel_id=1, source_target_pairs={{0,1},{1,0},{2,3},{3,2},{4,5},{5,4},{6,7},{7,6},{8,9},{9,8},{10,11... | collective-permute-start | bytes 1572872 | tf_op jit(solution)/shard_map/ppermute | solution.py:70
  150.0 14.9 %collective-permute-start.16 = (bf16[256,1024]{1,0:T(8,128)(2,1)S(1)}, bf16[256,1024]{1,0:T(8,128)(2,1)S(1)}, u32[]{:S(2)}, u32[]{:S(2)}) collective-permute-start(bf16[256,1024]{1,0:T(8,128)(2,1)S(1)} %collective-permute-done.13.refs_3_), channel_id=1, source_target_pairs={{0,2},{1,3},{2,0},{3,1},{4,6},{5,7},{6,4},{7,5},{8,10},{9,11},{10,... | collective-permute-start | bytes 1572872 | tf_op jit(solution)/shard_map/ppermute | solution.py:70
  151.4 27.2 %collective-permute-start.11 = (bf16[256,1024]{1,0:T(8,128)(2,1)S(1)}, bf16[256,1024]{1,0:T(8,128)(2,1)S(1)}, u32[]{:S(2)}, u32[]{:S(2)}) collective-permute-start(bf16[256,1024]{1,0:T(8,128)(2,1)S(1)} %get-tuple-element.223.refs_1_), channel_id=1, source_target_pairs={{0,1},{1,0},{2,3},{3,2},{4,5},{5,4},{6,7},{7,6},{8,9},{9,8},{10,11... | collective-permute-start | bytes 1572872 | tf_op jit(solution)/shard_map/ppermute | solution.py:70
  152.9 25.7 %collective-permute-start.14 = (bf16[256,1024]{1,0:T(8,128)(2,1)S(1)}, bf16[256,1024]{1,0:T(8,128)(2,1)S(1)}, u32[]{:S(2)}, u32[]{:S(2)}) collective-permute-start(bf16[256,1024]{1,0:T(8,128)(2,1)S(1)} %get-tuple-element.224.refs_2_), channel_id=1, source_target_pairs={{0,2},{1,3},{2,0},{3,1},{4,6},{5,7},{6,4},{7,5},{8,10},{9,11},{10,... | collective-permute-start | bytes 1572872 | tf_op jit(solution)/shard_map/ppermute | solution.py:70
  175.7 29.3 %collective-permute-start.18 = (bf16[256,1024]{1,0:T(8,128)(2,1)S(1)}, bf16[256,1024]{1,0:T(8,128)(2,1)S(1)}, u32[]{:S(2)}, u32[]{:S(2)}) collective-permute-start(bf16[256,1024]{1,0:T(8,128)(2,1)S(1)} %get-tuple-element.240), channel_id=1, source_target_pairs={{0,2},{1,3},{2,0},{3,1},{4,6},{5,7},{6,4},{7,5},{8,10},{9,11},{10,... | collective-permute-start | bytes 1572872 | tf_op jit(solution)/shard_map/ppermute | solution.py:70
  177.2 28.1 %collective-permute-start.19 = (bf16[256,1024]{1,0:T(8,128)(2,1)S(1)}, bf16[256,1024]{1,0:T(8,128)(2,1)S(1)}, u32[]{:S(2)}, u32[]{:S(2)}) collective-permute-start(bf16[256,1024]{1,0:T(8,128)(2,1)S(1)} %get-tuple-element.242), channel_id=1, source_target_pairs={{0,1},{1,0},{2,3},{3,2},{4,5},{5,4},{6,7},{7,6},{8,9},{9,8},{10,11... | collective-permute-start | bytes 1572872 | tf_op jit(solution)/shard_map/ppermute | solution.py:70
  216.7 325.4 %reduce-scatter.13.cloned.1.call-start = ((), (), s32[]{:S(2)}) async-start(), calls=%async_computation.9 | async-start | bytes 6340608 | tf_op jit(solution)/shard_map/reduce_scatter | solution.py:777
  216.7 22.3 %collective-permute-start.17 = (bf16[256,1024]{1,0:T(8,128)(2,1)S(1)}, bf16[256,1024]{1,0:T(8,128)(2,1)S(1)}, u32[]{:S(2)}, u32[]{:S(2)}) collective-permute-start(bf16[256,1024]{1,0:T(8,128)(2,1)S(1)} %get-tuple-element.238), channel_id=1, source_target_pairs={{0,1},{1,0},{2,3},{3,2},{4,5},{5,4},{6,7},{7,6},{8,9},{9,8},{10,11... | collective-permute-start | bytes 1572872 | tf_op jit(solution)/shard_map/ppermute | solution.py:70
  217.4 21.7 %collective-permute-start.21 = (bf16[256,1024]{1,0:T(8,128)(2,1)S(1)}, bf16[256,1024]{1,0:T(8,128)(2,1)S(1)}, u32[]{:S(2)}, u32[]{:S(2)}) collective-permute-start(bf16[256,1024]{1,0:T(8,128)(2,1)S(1)} %get-tuple-element.246), channel_id=1, source_target_pairs={{0,2},{1,3},{2,0},{3,1},{4,6},{5,7},{6,4},{7,5},{8,10},{9,11},{10,... | collective-permute-start | bytes 1572872 | tf_op jit(solution)/shard_map/ppermute | solution.py:70
  218.0 21.1 %collective-permute-start.20 = (bf16[256,1024]{1,0:T(8,128)(2,1)}, bf16[256,1024]{1,0:T(8,128)(2,1)S(1)}, u32[]{:S(2)}, u32[]{:S(2)}) collective-permute-start(bf16[256,1024]{1,0:T(8,128)(2,1)} %add_convert_fusion.6), channel_id=1, source_target_pairs={{0,2},{1,3},{2,0},{3,1},{4,6},{5,7},{6,4},{7,5},{8,10},{9,11},{10,... | collective-permute-start | bytes 1572872 | tf_op jit(solution)/shard_map/ppermute | solution.py:70
  219.4 19.7 %collective-permute-start.22 = (bf16[256,1024]{1,0:T(8,128)(2,1)S(1)}, bf16[256,1024]{1,0:T(8,128)(2,1)S(1)}, u32[]{:S(2)}, u32[]{:S(2)}) collective-permute-start(bf16[256,1024]{1,0:T(8,128)(2,1)S(1)} %add_convert_fusion.7), channel_id=1, source_target_pairs={{0,1},{1,0},{2,3},{3,2},{4,5},{5,4},{6,7},{7,6},{8,9},{9,8},{10,11... | collective-permute-start | bytes 1572872 | tf_op jit(solution)/shard_map/ppermute | solution.py:70
  265.3 276.8 %reduce-scatter.11.cloned.1.call-start = ((), (), s32[]{:S(2)}) async-start(), calls=%async_computation.8 | async-start | bytes 2359296 | tf_op jit(solution)/shard_map/reduce_scatter | solution.py:777
  265.4 13.8 %collective-permute-start.23 = (bf16[256,1024]{1,0:T(8,128)(2,1)}, bf16[256,1024]{1,0:T(8,128)(2,1)}, u32[]{:S(2)}, u32[]{:S(2)}) collective-permute-start(bf16[256,1024]{1,0:T(8,128)(2,1)} %copy-done.48), channel_id=1, source_target_pairs={{0,1},{1,0},{2,3},{3,2},{4,5},{5,4},{6,7},{7,6},{8,9},{9,8},{10,11... | collective-permute-start | bytes 1572872 | tf_op jit(solution)/shard_map/ppermute | solution.py:70
  265.5 13.7 %collective-permute-start.27 = (bf16[256,1024]{1,0:T(8,128)(2,1)}, bf16[256,1024]{1,0:T(8,128)(2,1)}, u32[]{:S(2)}, u32[]{:S(2)}) collective-permute-start(bf16[256,1024]{1,0:T(8,128)(2,1)} %copy-done.50), channel_id=1, source_target_pairs={{0,2},{1,3},{2,0},{3,1},{4,6},{5,7},{6,4},{7,5},{8,10},{9,11},{10,... | collective-permute-start | bytes 1572872 | tf_op jit(solution)/shard_map/ppermute | solution.py:70
  266.7 20.6 %collective-permute-start.25 = (bf16[256,1024]{1,0:T(8,128)(2,1)}, bf16[256,1024]{1,0:T(8,128)(2,1)}, u32[]{:S(2)}, u32[]{:S(2)}) collective-permute-start(bf16[256,1024]{1,0:T(8,128)(2,1)} %copy-done.52), channel_id=1, source_target_pairs={{0,1},{1,0},{2,3},{3,2},{4,5},{5,4},{6,7},{7,6},{8,9},{9,8},{10,11... | collective-permute-start | bytes 1572872 | tf_op jit(solution)/shard_map/ppermute | solution.py:70
  268.7 19.5 %collective-permute-start.28 = (bf16[256,1024]{1,0:T(8,128)(2,1)}, bf16[256,1024]{1,0:T(8,128)(2,1)}, u32[]{:S(2)}, u32[]{:S(2)}) collective-permute-start(bf16[256,1024]{1,0:T(8,128)(2,1)} %copy-done.54), channel_id=1, source_target_pairs={{0,2},{1,3},{2,0},{3,1},{4,6},{5,7},{6,4},{7,5},{8,10},{9,11},{10,... | collective-permute-start | bytes 1572872 | tf_op jit(solution)/shard_map/ppermute | solution.py:70
  325.5 34.6 %collective-permute-start.33 = (bf16[256,1024]{1,0:T(8,128)(2,1)}, bf16[256,1024]{1,0:T(8,128)(2,1)}, u32[]{:S(2)}, u32[]{:S(2)}) collective-permute-start(bf16[256,1024]{1,0:T(8,128)(2,1)} %copy-done.73), channel_id=1, source_target_pairs={{0,1},{1,0},{2,3},{3,2},{4,5},{5,4},{6,7},{7,6},{8,9},{9,8},{10,11... | collective-permute-start | bytes 1572872 | tf_op jit(solution)/shard_map/ppermute | solution.py:70
  326.2 33.9 %collective-permute-start.35 = (bf16[256,1024]{1,0:T(8,128)(2,1)}, bf16[256,1024]{1,0:T(8,128)(2,1)}, u32[]{:S(2)}, u32[]{:S(2)}) collective-permute-start(bf16[256,1024]{1,0:T(8,128)(2,1)} %copy-done.72), channel_id=1, source_target_pairs={{0,2},{1,3},{2,0},{3,1},{4,6},{5,7},{6,4},{7,5},{8,10},{9,11},{10,... | collective-permute-start | bytes 1572872 | tf_op jit(solution)/shard_map/ppermute | solution.py:70
  333.6 212.6 %reduce-scatter.9.cloned.1.call-start = ((), (), s32[]{:S(2)}) async-start(), calls=%async_computation.7 | async-start | bytes 6340608 | tf_op jit(solution)/shard_map/reduce_scatter | solution.py:777
  333.7 26.4 %collective-permute-start.34 = (bf16[256,1024]{1,0:T(8,128)(2,1)}, bf16[256,1024]{1,0:T(8,128)(2,1)S(1)}, u32[]{:S(2)}, u32[]{:S(2)}) collective-permute-start(bf16[256,1024]{1,0:T(8,128)(2,1)} %add_convert_fusion.4), channel_id=1, source_target_pairs={{0,2},{1,3},{2,0},{3,1},{4,6},{5,7},{6,4},{7,5},{8,10},{9,11},{10,... | collective-permute-start | bytes 1572872 | tf_op jit(solution)/shard_map/ppermute | solution.py:70
  334.7 25.3 %collective-permute-start.36 = (bf16[256,1024]{1,0:T(8,128)(2,1)}, bf16[256,1024]{1,0:T(8,128)(2,1)S(1)}, u32[]{:S(2)}, u32[]{:S(2)}) collective-permute-start(bf16[256,1024]{1,0:T(8,128)(2,1)} %add_convert_fusion.5), channel_id=1, source_target_pairs={{0,1},{1,0},{2,3},{3,2},{4,5},{5,4},{6,7},{7,6},{8,9},{9,8},{10,11... | collective-permute-start | bytes 1572872 | tf_op jit(solution)/shard_map/ppermute | solution.py:70
  337.6 39.2 %collective-permute-start.32 = (bf16[2,1024,256]{2,1,0:T(8,128)(2,1)S(1)}, bf16[2,1024,256]{2,1,0:T(8,128)(2,1)S(1)}, u32[]{:S(2)}, u32[]{:S(2)}) collective-permute-start(bf16[2,1024,256]{2,1,0:T(8,128)(2,1)S(1)} %add_convert_fusion.1), channel_id=1, source_target_pairs={{8,0},{12,4},{16,8},{20,12},{24,16},{28,20},{9,1},{13,5},{17,9},{2... | collective-permute-start | bytes 3145736 | tf_op jit(solution)/shard_map/ppermute | solution.py:880
  380.2 14.8 %collective-permute-start.38 = (bf16[256,1024]{1,0:T(8,128)(2,1)S(1)}, bf16[256,1024]{1,0:T(8,128)(2,1)S(1)}, u32[]{:S(2)}, u32[]{:S(2)}) collective-permute-start(bf16[256,1024]{1,0:T(8,128)(2,1)S(1)} %get-tuple-element.303.refs_1_), channel_id=1, source_target_pairs={{0,2},{1,3},{2,0},{3,1},{4,6},{5,7},{6,4},{7,5},{8,10},{9,11},{10,... | collective-permute-start | bytes 1572872 | tf_op jit(solution)/shard_map/ppermute | solution.py:70
  381.1 14.8 %collective-permute-start.40 = (bf16[256,1024]{1,0:T(8,128)(2,1)S(1)}, bf16[256,1024]{1,0:T(8,128)(2,1)S(1)}, u32[]{:S(2)}, u32[]{:S(2)}) collective-permute-start(bf16[256,1024]{1,0:T(8,128)(2,1)S(1)} %get-tuple-element.304.refs_5_), channel_id=1, source_target_pairs={{0,1},{1,0},{2,3},{3,2},{4,5},{5,4},{6,7},{7,6},{8,9},{9,8},{10,11... | collective-permute-start | bytes 1572872 | tf_op jit(solution)/shard_map/ppermute | solution.py:70
  382.5 38.2 %collective-permute-start.44 = (bf16[2,1024,256]{2,1,0:T(8,128)(2,1)S(1)}, bf16[2,1024,256]{2,1,0:T(8,128)(2,1)S(1)}, u32[]{:S(2)}, u32[]{:S(2)}) collective-permute-start(bf16[2,1024,256]{2,1,0:T(8,128)(2,1)S(1)} %add_convert_fusion), channel_id=1, source_target_pairs={{8,0},{12,4},{16,8},{20,12},{24,16},{28,20},{9,1},{13,5},{17,9},{2... | collective-permute-start | bytes 3145736 | tf_op jit(solution)/shard_map/ppermute | solution.py:887
  383.8 23.3 %collective-permute-start.37 = (bf16[256,1024]{1,0:T(8,128)(2,1)S(1)}, bf16[256,1024]{1,0:T(8,128)(2,1)S(1)}, u32[]{:S(2)}, u32[]{:S(2)}) collective-permute-start(bf16[256,1024]{1,0:T(8,128)(2,1)S(1)} %get-tuple-element.303.refs_1_), channel_id=1, source_target_pairs={{0,1},{1,0},{2,3},{3,2},{4,5},{5,4},{6,7},{7,6},{8,9},{9,8},{10,11... | collective-permute-start | bytes 1572872 | tf_op jit(solution)/shard_map/ppermute | solution.py:70
  384.8 22.3 %collective-permute-start.41 = (bf16[256,1024]{1,0:T(8,128)(2,1)S(1)}, bf16[256,1024]{1,0:T(8,128)(2,1)S(1)}, u32[]{:S(2)}, u32[]{:S(2)}) collective-permute-start(bf16[256,1024]{1,0:T(8,128)(2,1)S(1)} %get-tuple-element.304.refs_5_), channel_id=1, source_target_pairs={{0,2},{1,3},{2,0},{3,1},{4,6},{5,7},{6,4},{7,5},{8,10},{9,11},{10,... | collective-permute-start | bytes 1572872 | tf_op jit(solution)/shard_map/ppermute | solution.py:70
  394.9 22.7 %collective-permute-start.39 = (bf16[256,1024]{1,0:T(8,128)(2,1)S(1)}, bf16[256,1024]{1,0:T(8,128)(2,1)S(1)}, u32[]{:S(2)}, u32[]{:S(2)}) collective-permute-start(bf16[256,1024]{1,0:T(8,128)(2,1)S(1)} %collective-permute-done.38.refs_3_), channel_id=1, source_target_pairs={{0,1},{1,0},{2,3},{3,2},{4,5},{5,4},{6,7},{7,6},{8,9},{9,8},{10,11... | collective-permute-start | bytes 1572872 | tf_op jit(solution)/shard_map/ppermute | solution.py:70
  395.9 21.8 %collective-permute-start.42 = (bf16[256,1024]{1,0:T(8,128)(2,1)S(1)}, bf16[256,1024]{1,0:T(8,128)(2,1)S(1)}, u32[]{:S(2)}, u32[]{:S(2)}) collective-permute-start(bf16[256,1024]{1,0:T(8,128)(2,1)S(1)} %collective-permute-done.40.refs_6_), channel_id=1, source_target_pairs={{0,2},{1,3},{2,0},{3,1},{4,6},{5,7},{6,4},{7,5},{8,10},{9,11},{10,... | collective-permute-start | bytes 1572872 | tf_op jit(solution)/shard_map/ppermute | solution.py:70
  421.7 124.5 %reduce-scatter.7.cloned.1.call-start = ((), (), s32[]{:S(2)}) async-start(), calls=%async_computation.6 | async-start | bytes 3538944 | tf_op jit(solution)/shard_map/reduce_scatter | solution.py:777
  438.4 19.4 %collective-permute-start.46 = (bf16[256,1024]{1,0:T(8,128)(2,1)}, bf16[256,1024]{1,0:T(8,128)(2,1)}, u32[]{:S(2)}, u32[]{:S(2)}) collective-permute-start(bf16[256,1024]{1,0:T(8,128)(2,1)} %get-tuple-element.339.refs_9_), channel_id=1, source_target_pairs={{0,2},{1,3},{2,0},{3,1},{4,6},{5,7},{6,4},{7,5},{8,10},{9,11},{10,... | collective-permute-start | bytes 1572872 | tf_op jit(solution)/shard_map/ppermute | solution.py:70
  439.6 20.7 %collective-permute-start.47 = (bf16[256,1024]{1,0:T(8,128)(2,1)}, bf16[256,1024]{1,0:T(8,128)(2,1)}, u32[]{:S(2)}, u32[]{:S(2)}) collective-permute-start(bf16[256,1024]{1,0:T(8,128)(2,1)} %get-tuple-element.338.refs_8_), channel_id=1, source_target_pairs={{0,1},{1,0},{2,3},{3,2},{4,5},{5,4},{6,7},{7,6},{8,9},{9,8},{10,11... | collective-permute-start | bytes 1572872 | tf_op jit(solution)/shard_map/ppermute | solution.py:70
  462.4 105.4 %reduce-scatter.17.cloned.1.call-start = ((), (), s32[]{:S(2)}) async-start(), calls=%async_computation.11 | async-start | bytes 3538944 | tf_op jit(solution)/shard_map/reduce_scatter | solution.py:777
  463.5 15.7 %collective-permute-start.45 = (bf16[256,1024]{1,0:T(8,128)(2,1)S(1)}, bf16[256,1024]{1,0:T(8,128)(2,1)S(1)}, u32[]{:S(2)}, u32[]{:S(2)}) collective-permute-start(bf16[256,1024]{1,0:T(8,128)(2,1)S(1)} %copy-done.59), channel_id=1, source_target_pairs={{0,1},{1,0},{2,3},{3,2},{4,5},{5,4},{6,7},{7,6},{8,9},{9,8},{10,11... | collective-permute-start | bytes 1572872 | tf_op jit(solution)/shard_map/ppermute | solution.py:70
  464.9 14.9 %collective-permute-start.49 = (bf16[256,1024]{1,0:T(8,128)(2,1)S(1)}, bf16[256,1024]{1,0:T(8,128)(2,1)S(1)}, u32[]{:S(2)}, u32[]{:S(2)}) collective-permute-start(bf16[256,1024]{1,0:T(8,128)(2,1)S(1)} %copy-done.57), channel_id=1, source_target_pairs={{0,2},{1,3},{2,0},{3,1},{4,6},{5,7},{6,4},{7,5},{8,10},{9,11},{10,... | collective-permute-start | bytes 1572872 | tf_op jit(solution)/shard_map/ppermute | solution.py:70
  465.8 22.7 %collective-permute-start.48 = (bf16[256,1024]{1,0:T(8,128)(2,1)}, bf16[256,1024]{1,0:T(8,128)(2,1)S(1)}, u32[]{:S(2)}, u32[]{:S(2)}) collective-permute-start(bf16[256,1024]{1,0:T(8,128)(2,1)} %add_convert_fusion.2), channel_id=1, source_target_pairs={{0,2},{1,3},{2,0},{3,1},{4,6},{5,7},{6,4},{7,5},{8,10},{9,11},{10,... | collective-permute-start | bytes 1572872 | tf_op jit(solution)/shard_map/ppermute | solution.py:70
  466.9 21.5 %collective-permute-start.50 = (bf16[256,1024]{1,0:T(8,128)(2,1)}, bf16[256,1024]{1,0:T(8,128)(2,1)S(1)}, u32[]{:S(2)}, u32[]{:S(2)}) collective-permute-start(bf16[256,1024]{1,0:T(8,128)(2,1)} %add_convert_fusion.3), channel_id=1, source_target_pairs={{0,1},{1,0},{2,3},{3,2},{4,5},{5,4},{6,7},{7,6},{8,9},{9,8},{10,11... | collective-permute-start | bytes 1572872 | tf_op jit(solution)/shard_map/ppermute | solution.py:70
  (101 other events, 965.3 us)
Sparse Core Ops, SparseCore 0:
  216.8 63.9 reduce-scatter.14
  283.2 61.9 reduce-scatter.12
  347.5 41.8 reduce-scatter.10
  421.8 63.1 reduce-scatter.8
  487.2 38.9 reduce-scatter.6
  528.5 39.3 reduce-scatter.16

commit v5 on v4

--- a/solution.py
+++ b/solution.py
@@ -13,7 +13,7 @@
 F32 = jnp.float32
 BF16 = jnp.bfloat16
 MIB = 1024 * 1024
-STEPS = 4
+STEPS = 2
 GROUPS = 2
 
 NN = (((1,), (0,)), ((), ()))
@@ -589,7 +589,7 @@
         [((tokens, width), BF16)] + [((tokens, hid), BF16)] * 3 + outs,
         (scal, *left, *right, d_act, w_gate, w_up),
         "mlp",
-        vmem=34,
+        vmem=50,
         into=into,
     )
     return results[:4], results[4:]

time: 587 us -> 584 us (level)
  local copies, waits for them, and re-layouts: 38.5 us -> 31.6 us
    unnamed x162 -> x154, local copies, waits for them, and re-layouts: 35.4 us -> 28.5 us
  transfers between devices with their start and end apart: 68 -> 68, of which waited for: 27 -> 26; matrix products, arithmetic and copies ran while one was open for 3% -> 3% of each run, Pallas kernels for 42% -> 42%
where the time goes in v5:
time: 584 us; the launch traced here: 576 us
  Pallas kernels  273 us (47%)
  waiting for transfers between devices  159 us (27%)
  starting transfers between devices  74.1 us (13%)
  local copies, waits for them, and re-layouts  31.6 us (5%)
  other arithmetic  23.2 us (4%)
  between operations  15.2 us (3%)
    pallas_call x30, Pallas kernels, call(): pl.pallas_call(body, grid_spec=pltpu.PrefetchScalarGridSpec(num_scalar_pr...  263 us
    ppermute x55, waiting for transfers between devices, swap(): return lax.ppermute(array, axis, [(i, i ^ bit) for i in range(size)])  98.6 us
    ppermute x55, starting transfers between devices, swap(): return lax.ppermute(array, axis, [(i, i ^ bit) for i in range(size)])  57.1 us
    unnamed x154, local copies, waits for them, and re-layouts  28.5 us
    ppermute x2, waiting for transfers between devices, on_device(): twos = [lax.ppermute(own, 'seq', right_two) for own in packed]  23.7 us
    ppermute x1, waiting for transfers between devices, on_device(): back_two = lax.ppermute(sent, 'seq', left_two)  16.9 us
    reduce_scatter x6, waiting for transfers between devices, scattered(): return lax.psum_scatter(grad, 'seq', scatter_dimension=dim, tiled=True)  16.7 us
  transfers between devices with their start and end apart: 68, of which 26 were waited for; matrix products, arithmetic and copies ran while one was open for 3% of the time, Pallas kernels for 42%

profile of v5, /device:TPU:0, one launch (start us, length us, event | category | flops | bytes accessed | tf_op | source)
XLA Modules:
  0.0 576.1 jit_solution(8903179473574555808)
XLA Ops:
  10.9 10.2 %project_keys.1 = (bf16[1024,2048]{1,0:T(8,128)(2,1)}, bf16[4,1024,256]{2,1,0:T(8,128)(2,1)S(1)}, bf16[2,1024,256]{2,1,0:T(8,128)(2,1)S(1)}, bf16[2,1024,256]{2,1,0:T(8,128)(2,1)S(1)}) custom-call(s32[2]{0:T(128)S(1)} %pad_add_fusion.2.me_ref.refs_0_._.s_ref_, bf16[1024,2048]{1,0:T(8,128)(2,1)} %refs_0_.3, f32[1,2048]{1,0:T(1,128)S(1)} %bitcast.22, ...), custom_call_target="tpu_custom_call" | custom-call | tf_op jit(solution)/shard_map/project_keys/pallas_call | solution.py:37
  21.1 5.0 collective-permute-start
  27.7 5.6 project_query.1.refs_1_
  33.4 15.1 %collective-permute-done.refs_2_ = bf16[2,1024,256]{2,1,0:T(8,128)(2,1)S(1)} collective-permute-done((bf16[2,1024,256]{2,1,0:T(8,128)(2,1)S(1)}, bf16[2,1024,256]{2,1,0:T(8,128)(2,1)S(1)}, u32[]{:S(2)}, u32[]{:S(2)}) %collective-permute-start) | collective-permute-done | bytes 1048608 | tf_op jit(solution)/shard_map/ppermute | solution.py:814
  49.8 4.5 collective-permute-start.3
  55.6 13.2 %attend.3 = (bf16[1024,256]{1,0:T(8,128)(2,1)S(1)}, f32[2,1,1024]{2,1,0:T(1,128)S(1)}) custom-call(s32[2]{0:T(128)S(1)} %pad_add_fusion.2.me_ref.refs_0_._.s_ref_, bf16[1024,512]{1,0:T(8,128)(2,1)S(1)} %project_query.1.refs_1_, bf16[2,1024,256]{2,1,0:T(8,128)(2,1)S(1)} %collective-permute-done.refs_2_, bf16[4,1024,256]{2,1,0:T(8,128)(2,1)} %copy-done.72, ...), custom_call_target="tpu_custom_call" | custom-call | tf_op jit(solution)/shard_map/attend/pallas_call | solution.py:37
  68.8 8.7 %collective-permute-done.3.refs_2_ = bf16[2,1024,256]{2,1,0:T(8,128)(2,1)S(1)} collective-permute-done((bf16[2,1024,256]{2,1,0:T(8,128)(2,1)S(1)}, bf16[2,1024,256]{2,1,0:T(8,128)(2,1)S(1)}, u32[]{:S(2)}, u32[]{:S(2)}) %collective-permute-start.3) | collective-permute-done | bytes 1048608 | tf_op jit(solution)/shard_map/ppermute | solution.py:814
  79.3 3.0 collective-permute-done.4.refs_4_
  82.3 4.7 attend.4
  91.3 10.5 %attend.5 = (bf16[1024,256]{1,0:T(8,128)(2,1)S(1)}, f32[2,1,1024]{2,1,0:T(1,128)S(1)}) custom-call(s32[2]{0:T(128)S(1)} %pad_add_fusion.2.me_ref.refs_0_._.s_ref_, bf16[1024,512]{1,0:T(8,128)(2,1)S(1)} %project_query.1.refs_1_, bf16[2,1024,256]{2,1,0:T(8,128)(2,1)S(1)} %collective-permute-done.3.refs_2_, ...), custom_call_target="tpu_custom_call", output_to_operand_aliasing={{0}: (7, {}), {1}: (8, {})} | custom-call | tf_op jit(solution)/shard_map/attend/pallas_call | solution.py:37
  101.8 4.6 project_out.3
  111.1 12.0 %project_cotangent.1 = (bf16[1024,2048]{1,0:T(8,128)(2,1)S(1)}, f32[1024,1376]{1,0:T(8,128)}) custom-call(s32[2]{0:T(128)S(1)} %pad_add_fusion.2.me_ref.refs_0_._.s_ref_, bf16[1024,2048]{1,0:T(8,128)(2,1)} %refs_2_.5, bf16[1376,2048]{1,0:T(8,128)(2,1)} %refs_2_.4), custom_call_target="tpu_custom_call" | custom-call | tf_op jit(solution)/shard_map/project_cotangent/pallas_call | solution.py:37
  125.1 6.4 %collective-permute-done.8.refs_4_ = bf16[256,1024]{1,0:T(8,128)(2,1)S(1)} collective-permute-done((bf16[256,1024]{1,0:T(8,128)(2,1)S(1)}, bf16[256,1024]{1,0:T(8,128)(2,1)S(1)}, u32[]{:S(2)}, u32[]{:S(2)}) %collective-permute-start.8) | collective-permute-done | bytes 524320 | tf_op jit(solution)/shard_map/ppermute | solution.py:70
  131.4 4.0 mid.1
  137.5 10.2 %collective-permute-done.12.refs_2_ = bf16[256,1024]{1,0:T(8,128)(2,1)S(1)} collective-permute-done((bf16[256,1024]{1,0:T(8,128)(2,1)S(1)}, bf16[256,1024]{1,0:T(8,128)(2,1)S(1)}, u32[]{:S(2)}, u32[]{:S(2)}) %collective-permute-start.12) | collective-permute-done | bytes 524320 | tf_op jit(solution)/shard_map/ppermute | solution.py:70
  152.1 12.2 %mlp.3 = (bf16[1024,2048]{1,0:T(8,128)(2,1)}, bf16[1024,1376]{1,0:T(8,128)(2,1)}, bf16[1024,1376]{1,0:T(8,128)(2,1)}, bf16[1024,1376]{1,0:T(8,128)(2,1)}, bf16[2...) custom-call(s32[2]{0:T(128)S(1)} %pad_add_fusion.2.me_ref.refs_0_._.s_ref_, ...), custom_call_target="tpu_custom_call" | custom-call | tf_op jit(solution)/shard_map/mlp/pallas_call | solution.py:37
  164.3 12.4 %mlp.4 = (bf16[1024,2048]{1,0:T(8,128)(2,1)}, bf16[1024,1376]{1,0:T(8,128)(2,1)}, bf16[1024,1376]{1,0:T(8,128)(2,1)}, bf16[1024,1376]{1,0:T(8,128)(2,1)}, bf16[2...) custom-call(s32[2]{0:T(128)S(1)} %pad_add_fusion.2.me_ref.refs_0_._., ...), custom_call_target="tpu_custom_call", output_to_operand_aliasing={{0}: (6, {}), {1}: (7, {}), {2}: (8, {}), {3}: (9, {})} | custom-call | tf_op jit(solution)/shard_map/mlp/pallas_call | solution.py:37
  180.2 21.4 %mlp.5 = (bf16[1024,2048]{1,0:T(8,128)(2,1)}, bf16[1024,1376]{1,0:T(8,128)(2,1)}, bf16[1024,1376]{1,0:T(8,128)(2,1)}, bf16[1024,1376]{1,0:T(8,128)(2,1)}, bf16[2...) custom-call(s32[2]{0:T(128)S(1)} %pad_add_fusion.2.me_ref.refs_0_._., ...), custom_call_target="tpu_custom_call", output_to_operand_aliasing={{0}: (8, {}), {1}: (9, {}), {2}: (10, {}), {3}: (11, {})} | custom-call | tf_op jit(solution)/shard_map/mlp/pallas_call | solution.py:37
  203.6 9.6 %grad_down.1 = bf16[1376,2048]{1,0:T(8,128)(2,1)} custom-call(s32[2]{0:T(128)S(1)} %pad_add_fusion.2.me_ref.refs_0_._.s_ref_, bf16[1024,1376]{1,0:T(8,128)(2,1)S(1)} %copy-done, bf16[1024,2048]{1,0:T(8,128)(2,1)} %copy-done.17), custom_call_target="tpu_custom_call" | custom-call | tf_op jit(solution)/shard_map/grad_down/pallas_call | solution.py:37
  217.5 11.7 %project_down.1 = (bf16[256,1024]{1,0:T(8,128)(2,1)S(1)}, bf16[256,1024]{1,0:T(8,128)(2,1)S(1)}, bf16[256,1024]{1,0:T(8,128)(2,1)S(1)}, bf16[256,1024]{1,0:T(8,1...) custom-call(s32[2]{0:T(128)S(1)} %pad_add_fusion.2.me_ref.refs_0_._., ...), custom_call_target="tpu_custom_call" | custom-call | tf_op jit(solution)/shard_map/project_down/pallas_call | solution.py:37
  235.6 5.4 d_mid.1
  242.2 8.1 %collective-permute-done.24.refs_3_ = bf16[256,1024]{1,0:T(8,128)(2,1)S(1)} collective-permute-done((bf16[256,1024]{1,0:T(8,128)(2,1)S(1)}, bf16[256,1024]{1,0:T(8,128)(2,1)S(1)}, u32[]{:S(2)}, u32[]{:S(2)}) %collective-permute-start.24) | collective-permute-done | bytes 524320 | tf_op jit(solution)/shard_map/ppermute | solution.py:70
  251.8 9.7 %grad_gate.1 = bf16[1376,2048]{1,0:T(8,128)(2,1)} custom-call(s32[2]{0:T(128)S(1)} %pad_add_fusion.2.me_ref.refs_0_._.s_ref_, bf16[1024,1376]{1,0:T(8,128)(2,1)S(1)} %copy-done.1, bf16[1024,2048]{1,0:T(8,128)(2,1)} %get-tuple-element.268.refs_1_), custom_call_target="tpu_custom_call" | custom-call | tf_op jit(solution)/shard_map/grad_gate/pallas_call | solution.py:37
  265.7 9.7 %grad_up.1 = bf16[1376,2048]{1,0:T(8,128)(2,1)} custom-call(s32[2]{0:T(128)S(1)} %pad_add_fusion.2.me_ref.refs_0_._.s_ref_, bf16[1024,1376]{1,0:T(8,128)(2,1)S(1)} %copy-done.2, bf16[1024,2048]{1,0:T(8,128)(2,1)} %get-tuple-element.268.refs_1_), custom_call_target="tpu_custom_call" | custom-call | tf_op jit(solution)/shard_map/grad_up/pallas_call | solution.py:37
  275.4 8.8 %collective-permute-done.25.refs_4_ = bf16[256,1024]{1,0:T(8,128)(2,1)} collective-permute-done((bf16[256,1024]{1,0:T(8,128)(2,1)}, bf16[256,1024]{1,0:T(8,128)(2,1)}, u32[]{:S(2)}, u32[]{:S(2)}) %collective-permute-start.25) | collective-permute-done | bytes 524320 | tf_op jit(solution)/shard_map/ppermute | solution.py:70
  292.4 6.5 %project_back.1 = (bf16[1024,2048]{1,0:T(8,128)(2,1)}, bf16[1024,512]{1,0:T(8,128)(2,1)S(1)}) custom-call(s32[2]{0:T(128)S(1)} %pad_add_fusion.2.me_ref.refs_0_._.s_ref_, bf16[256,1024]{1,0:T(8,128)(2,1)S(1)} %copy-done.45, bf16[256,1024]{1,0:T(8,128)(2,1)} %collective-permute-done.23.refs_2_, bf16[256,1024]{1,0:T(8,128)(2,1)S(1)} %copy-done.49, ...), custom_call_target="tpu_custom_call" | custom-call | tf_op jit(solution)/shard_map/project_back/pallas_call | solution.py:37
  300.9 19.5 %attend_back.2 = (bf16[1024,256]{1,0:T(8,128)(2,1)S(1)}, bf16[2,1024,256]{2,1,0:T(8,128)(2,1)S(1)}, bf16[2,1024,256]{2,1,0:T(8,128)(2,1)}, bf16[2,1024,256]{2,1,0:T(8,128)(2,1)S(1)}) custom-call(s32[2]{0:T(128)S(1)} %pad_add_fusion.2.me_ref.refs_0_._.s_ref_, bf16[1024,512]{1,0:T(8,128)(2,1)} %copy-done.8, bf16[2,1024,256]{2,1,0:T(8,128)(2,1)} %copy-done.34, ...), custom_call_target="tpu_custom_call" | custom-call | flops 69000003584 | tf_op jit(solution)/shard_map/attend_back/pallas_call | solution.py:37
  325.1 6.4 %grad_out.1 = bf16[512,2048]{1,0:T(8,128)(2,1)} custom-call(s32[2]{0:T(128)S(1)} %pad_add_fusion.2.me_ref.refs_0_._.s_ref_, bf16[1024,256]{1,0:T(8,128)(2,1)S(1)} %copy-done.14, bf16[1024,256]{1,0:T(8,128)(2,1)S(1)} %copy-done.12, bf16[1024,2048]{1,0:T(8,128)(2,1)} %get-tuple-element.360.refs_2_), custom_call_target="tpu_custom_call" | custom-call | tf_op jit(solution)/shard_map/grad_out/pallas_call | solution.py:37
  336.6 19.5 %attend_back.3 = (bf16[1024,256]{1,0:T(8,128)(2,1)S(1)}, bf16[2,1024,256]{2,1,0:T(8,128)(2,1)S(1)}, bf16[2,1024,256]{2,1,0:T(8,128)(2,1)S(1)}, bf16[2,1024,256]{2,1,0:T(8,128)(2,1)S(1)}) custom-call(s32[2]{0:T(128)S(1)} %pad_add_fusion.2.me_ref.refs_0_._.s_ref_, bf16[1024,512]{1,0:T(8,128)(2,1)} %copy-done.8, bf16[2,1024,256]{2,1,0:T(8,128)(2,1)} %copy-done.19, ...), custom_call_target="tpu_custom_call" | custom-call | flops 69000003584 | tf_op jit(solution)/shard_map/attend_back/pallas_call | solution.py:37
  357.9 16.9 %collective-permute-done.32.back_ref = bf16[2,1024,256]{2,1,0:T(8,128)(2,1)S(1)} collective-permute-done((bf16[2,1024,256]{2,1,0:T(8,128)(2,1)S(1)}, bf16[2,1024,256]{2,1,0:T(8,128)(2,1)S(1)}, u32[]{:S(2)}, u32[]{:S(2)}) %collective-permute-start.32) | collective-permute-done | bytes 1048608 | tf_op jit(solution)/shard_map/ppermute | solution.py:880
  383.3 9.0 %collective-permute-done.38.refs_3_ = bf16[256,1024]{1,0:T(8,128)(2,1)S(1)} collective-permute-done((bf16[256,1024]{1,0:T(8,128)(2,1)S(1)}, bf16[256,1024]{1,0:T(8,128)(2,1)S(1)}, u32[]{:S(2)}, u32[]{:S(2)}) %collective-permute-start.38) | collective-permute-done | bytes 524320 | tf_op jit(solution)/shard_map/ppermute | solution.py:70
  394.3 10.0 %collective-permute-done.37.refs_2_ = bf16[256,1024]{1,0:T(8,128)(2,1)S(1)} collective-permute-done((bf16[256,1024]{1,0:T(8,128)(2,1)S(1)}, bf16[256,1024]{1,0:T(8,128)(2,1)S(1)}, u32[]{:S(2)}, u32[]{:S(2)}) %collective-permute-start.37) | collective-permute-done | bytes 524320 | tf_op jit(solution)/shard_map/ppermute | solution.py:70
  404.3 10.5 %collective-permute-done.39.refs_4_ = bf16[256,1024]{1,0:T(8,128)(2,1)S(1)} collective-permute-done((bf16[256,1024]{1,0:T(8,128)(2,1)S(1)}, bf16[256,1024]{1,0:T(8,128)(2,1)S(1)}, u32[]{:S(2)}, u32[]{:S(2)}) %collective-permute-start.39) | collective-permute-done | bytes 524320 | tf_op jit(solution)/shard_map/ppermute | solution.py:70
  414.8 3.0 place.3
  422.4 2.9 finish.2.refs_0_.refs_1_
  425.3 2.9 finish.3.refs_1_
  429.6 6.1 %project_one_back.2 = (bf16[256,1024]{1,0:T(8,128)(2,1)}, bf16[256,1024]{1,0:T(8,128)(2,1)}) custom-call(s32[2]{0:T(128)S(1)} %pad_add_fusion.2.me_ref.refs_0_._.s_ref_, bf16[1024,768]{1,0:T(8,128)(2,1)S(1)} %copy-done.5, bf16[1024,768]{1,0:T(8,128)(2,1)S(1)} %copy-done.3, bf16[2048,512]{1,0:T(8,128)(2,1)} %refs_2_.7, bf16[2048,512]{1,0:T(8,128)(2,1)} %refs_3_.7, ...), custom_call_target="tpu_custom_call" | custom-call | tf_op jit(solution)/shard_map/project_one_back/pallas_call | solution.py:37
  437.9 8.2 %grad_first.1 = bf16[2048,768]{1,0:T(8,128)(2,1)} custom-call(s32[2]{0:T(128)S(1)} %pad_add_fusion.2.me_ref.refs_0_._.s_ref_, bf16[1024,2048]{1,0:T(8,128)(2,1)} %get-tuple-element.191.h_ref.refs_0_, bf16[1024,768]{1,0:T(8,128)(2,1)S(1)} %copy-done.5), custom_call_target="tpu_custom_call" | custom-call | tf_op jit(solution)/shard_map/grad_first/pallas_call | solution.py:37
  446.1 9.5 %project_one_back.3 = (bf16[256,1024]{1,0:T(8,128)(2,1)S(1)}, bf16[256,1024]{1,0:T(8,128)(2,1)S(1)}, bf16[256,1024]{1,0:T(8,128)(2,1)S(1)}, bf16[256,1024]{1,0:T...) custom-call(s32[2]{0:T(128)S(1)} %pad_add_fusion.2.me_ref.refs_0_._.s_ref_, ...), custom_call_target="tpu_custom_call" | custom-call | tf_op jit(solution)/shard_map/project_one_back/pallas_call | solution.py:37
  465.3 8.5 %gain_back.1 = f32[1,2048]{1,0:T(1,128)S(1)} custom-call(s32[2]{0:T(128)S(1)} %pad_add_fusion.2.me_ref.refs_0_._.s_ref_, bf16[1024,2048]{1,0:T(8,128)(2,1)} %refs_0_.3, bf16[256,1024]{1,0:T(8,128)(2,1)S(1)} %get-tuple-element.340.refs_2_.refs_3_, bf16[256,1024]{1,0:T(8,128)(2,1)S(1)} %get-tuple-element.343.refs_3_.refs_6_, bf16[256,1024]{1,0:T(8,128)(2,1)S(1)} %copy-done.55, ...), custom_call_target="tpu_custom_call" | custom-call | tf_op jit(solution)/shard_map/gain_back/pallas_call | solution.py:37
  477.2 8.7 %collective-permute-done.48.refs_5_ = bf16[256,1024]{1,0:T(8,128)(2,1)S(1)} collective-permute-done((bf16[256,1024]{1,0:T(8,128)(2,1)}, bf16[256,1024]{1,0:T(8,128)(2,1)S(1)}, u32[]{:S(2)}, u32[]{:S(2)}) %collective-permute-start.48) | collective-permute-done | bytes 524320 | tf_op jit(solution)/shard_map/ppermute | solution.py:70
  485.9 4.5 input.1
  492.3 9.6 %collective-permute-done.51.refs_3_ = bf16[256,1024]{1,0:T(8,128)(2,1)S(1)} collective-permute-done((bf16[256,1024]{1,0:T(8,128)(2,1)S(1)}, bf16[256,1024]{1,0:T(8,128)(2,1)S(1)}, u32[]{:S(2)}, u32[]{:S(2)}) %collective-permute-start.51) | collective-permute-done | bytes 524320 | tf_op jit(solution)/shard_map/ppermute | solution.py:70
  502.7 8.2 %grad_second.1 = bf16[2048,768]{1,0:T(8,128)(2,1)} custom-call(s32[2]{0:T(128)S(1)} %pad_add_fusion.2.me_ref.refs_0_._.s_ref_, bf16[1024,2048]{1,0:T(8,128)(2,1)} %get-tuple-element.191.h_ref.refs_0_, bf16[1024,768]{1,0:T(8,128)(2,1)S(1)} %copy-done.4), custom_call_target="tpu_custom_call" | custom-call | tf_op jit(solution)/shard_map/grad_second/pallas_call | solution.py:37
  510.9 3.4 collective-permute-start.57
  522.2 4.7 collective-permute-done.60
  529.3 4.7 place.4.refs_3_
  548.8 16.7 %reduce-scatter.17.cloned.1.call-done = bf16[256,768]{1,0:T(8,128)(2,1)} async-done(((bf16[2048,768]{1,0:T(8,128)(2,1)}), bf16[256,768]{1,0:T(8,128)(2,1)}) %reduce-scatter.17.cloned.1.call-update) | async-done | bytes 393232 | tf_op jit(solution)/shard_map/reduce_scatter | solution.py:777
  (326 shorter events, 134.7 us)
Async XLA Ops:
  7.2 529.4 %reduce-scatter.15.cloned.1.call-start = ((), (), s32[]{:S(2)}) async-start(), calls=%async_computation.10 | async-start | bytes 6340608 | tf_op jit(solution)/shard_map/reduce_scatter | solution.py:777
  21.1 27.3 %collective-permute-start = (bf16[2,1024,256]{2,1,0:T(8,128)(2,1)S(1)}, bf16[2,1024,256]{2,1,0:T(8,128)(2,1)S(1)}, u32[]{:S(2)}, u32[]{:S(2)}) collective-permute-start(bf16[2,1024,256]{2,1,0:T(8,128)(2,1)S(1)} %get-tuple-element.192.refs_5_), channel_id=1, source_target_pairs={{0,8},{4,12},{8,16},{12,20},{16,24},{20,28},{1,9},{5,13},{9,17},{1... | collective-permute-start | bytes 3145736 | tf_op jit(solution)/shard_map/ppermute | solution.py:814
  26.1 28.1 %collective-permute-start.1 = (bf16[4,1024,256]{2,1,0:T(8,128)(2,1)S(1)}, bf16[4,1024,256]{2,1,0:T(8,128)(2,1)S(1)}, u32[]{:S(2)}, u32[]{:S(2)}) collective-permute-start(bf16[4,1024,256]{2,1,0:T(8,128)(2,1)S(1)} %get-tuple-element.194), channel_id=1, source_target_pairs={{0,4},{8,12},{16,20},{24,28},{1,5},{9,13},{17,21},{25,29},{2,6},{1... | collective-permute-start | bytes 6291464 | tf_op jit(solution)/shard_map/ppermute | solution.py:815
  49.8 27.7 %collective-permute-start.3 = (bf16[2,1024,256]{2,1,0:T(8,128)(2,1)S(1)}, bf16[2,1024,256]{2,1,0:T(8,128)(2,1)S(1)}, u32[]{:S(2)}, u32[]{:S(2)}) collective-permute-start(bf16[2,1024,256]{2,1,0:T(8,128)(2,1)S(1)} %get-tuple-element.196.refs_5_), channel_id=1, source_target_pairs={{0,8},{4,12},{8,16},{12,20},{16,24},{20,28},{1,9},{5,13},{9,17},{1... | collective-permute-start | bytes 3145736 | tf_op jit(solution)/shard_map/ppermute | solution.py:814
  88.2 19.4 %collective-permute-start.6 = (bf16[256,1024]{1,0:T(8,128)(2,1)S(1)}, bf16[256,1024]{1,0:T(8,128)(2,1)S(1)}, u32[]{:S(2)}, u32[]{:S(2)}) collective-permute-start(bf16[256,1024]{1,0:T(8,128)(2,1)S(1)} %get-tuple-element.201), channel_id=1, source_target_pairs={{0,2},{1,3},{2,0},{3,1},{4,6},{5,7},{6,4},{7,5},{8,10},{9,11},{10,... | collective-permute-start | bytes 1572872 | tf_op jit(solution)/shard_map/ppermute | solution.py:70
  89.8 18.0 %collective-permute-start.7 = (bf16[256,1024]{1,0:T(8,128)(2,1)S(1)}, bf16[256,1024]{1,0:T(8,128)(2,1)S(1)}, u32[]{:S(2)}, u32[]{:S(2)}) collective-permute-start(bf16[256,1024]{1,0:T(8,128)(2,1)S(1)} %get-tuple-element.200), channel_id=1, source_target_pairs={{0,1},{1,0},{2,3},{3,2},{4,5},{5,4},{6,7},{7,6},{8,9},{9,8},{10,11... | collective-permute-start | bytes 1572872 | tf_op jit(solution)/shard_map/ppermute | solution.py:70
  106.5 18.6 %collective-permute-start.5 = (bf16[256,1024]{1,0:T(8,128)(2,1)S(1)}, bf16[256,1024]{1,0:T(8,128)(2,1)S(1)}, u32[]{:S(2)}, u32[]{:S(2)}) collective-permute-start(bf16[256,1024]{1,0:T(8,128)(2,1)S(1)} %get-tuple-element.206), channel_id=1, source_target_pairs={{0,1},{1,0},{2,3},{3,2},{4,5},{5,4},{6,7},{7,6},{8,9},{9,8},{10,11... | collective-permute-start | bytes 1572872 | tf_op jit(solution)/shard_map/ppermute | solution.py:70
  107.1 18.0 %collective-permute-start.9 = (bf16[256,1024]{1,0:T(8,128)(2,1)S(1)}, bf16[256,1024]{1,0:T(8,128)(2,1)S(1)}, u32[]{:S(2)}, u32[]{:S(2)}) collective-permute-start(bf16[256,1024]{1,0:T(8,128)(2,1)S(1)} %get-tuple-element.211), channel_id=1, source_target_pairs={{0,2},{1,3},{2,0},{3,1},{4,6},{5,7},{6,4},{7,5},{8,10},{9,11},{10,... | collective-permute-start | bytes 1572872 | tf_op jit(solution)/shard_map/ppermute | solution.py:70
  108.0 23.4 %collective-permute-start.8 = (bf16[256,1024]{1,0:T(8,128)(2,1)S(1)}, bf16[256,1024]{1,0:T(8,128)(2,1)S(1)}, u32[]{:S(2)}, u32[]{:S(2)}) collective-permute-start(bf16[256,1024]{1,0:T(8,128)(2,1)S(1)} %add_convert_fusion.8), channel_id=1, source_target_pairs={{0,2},{1,3},{2,0},{3,1},{4,6},{5,7},{6,4},{7,5},{8,10},{9,11},{10,... | collective-permute-start | bytes 1572872 | tf_op jit(solution)/shard_map/ppermute | solution.py:70
  109.6 21.8 %collective-permute-start.10 = (bf16[256,1024]{1,0:T(8,128)(2,1)S(1)}, bf16[256,1024]{1,0:T(8,128)(2,1)S(1)}, u32[]{:S(2)}, u32[]{:S(2)}) collective-permute-start(bf16[256,1024]{1,0:T(8,128)(2,1)S(1)} %add_convert_fusion.9), channel_id=1, source_target_pairs={{0,1},{1,0},{2,3},{3,2},{4,5},{5,4},{6,7},{7,6},{8,9},{9,8},{10,11... | collective-permute-start | bytes 1572872 | tf_op jit(solution)/shard_map/ppermute | solution.py:70
  136.0 13.2 %collective-permute-start.13 = (bf16[256,1024]{1,0:T(8,128)(2,1)S(1)}, bf16[256,1024]{1,0:T(8,128)(2,1)S(1)}, u32[]{:S(2)}, u32[]{:S(2)}) collective-permute-start(bf16[256,1024]{1,0:T(8,128)(2,1)S(1)} %get-tuple-element.224.refs_2_), channel_id=1, source_target_pairs={{0,1},{1,0},{2,3},{3,2},{4,5},{5,4},{6,7},{7,6},{8,9},{9,8},{10,11... | collective-permute-start | bytes 1572872 | tf_op jit(solution)/shard_map/ppermute | solution.py:70
  147.8 16.6 %collective-permute-start.15 = (bf16[256,1024]{1,0:T(8,128)(2,1)S(1)}, bf16[256,1024]{1,0:T(8,128)(2,1)S(1)}, u32[]{:S(2)}, u32[]{:S(2)}) collective-permute-start(bf16[256,1024]{1,0:T(8,128)(2,1)S(1)} %collective-permute-done.12.refs_2_), channel_id=1, source_target_pairs={{0,1},{1,0},{2,3},{3,2},{4,5},{5,4},{6,7},{7,6},{8,9},{9,8},{10,11... | collective-permute-start | bytes 1572872 | tf_op jit(solution)/shard_map/ppermute | solution.py:70
  149.2 15.1 %collective-permute-start.16 = (bf16[256,1024]{1,0:T(8,128)(2,1)S(1)}, bf16[256,1024]{1,0:T(8,128)(2,1)S(1)}, u32[]{:S(2)}, u32[]{:S(2)}) collective-permute-start(bf16[256,1024]{1,0:T(8,128)(2,1)S(1)} %collective-permute-done.13.refs_3_), channel_id=1, source_target_pairs={{0,2},{1,3},{2,0},{3,1},{4,6},{5,7},{6,4},{7,5},{8,10},{9,11},{10,... | collective-permute-start | bytes 1572872 | tf_op jit(solution)/shard_map/ppermute | solution.py:70
  150.6 28.8 %collective-permute-start.11 = (bf16[256,1024]{1,0:T(8,128)(2,1)S(1)}, bf16[256,1024]{1,0:T(8,128)(2,1)S(1)}, u32[]{:S(2)}, u32[]{:S(2)}) collective-permute-start(bf16[256,1024]{1,0:T(8,128)(2,1)S(1)} %get-tuple-element.223.refs_1_), channel_id=1, source_target_pairs={{0,1},{1,0},{2,3},{3,2},{4,5},{5,4},{6,7},{7,6},{8,9},{9,8},{10,11... | collective-permute-start | bytes 1572872 | tf_op jit(solution)/shard_map/ppermute | solution.py:70
  152.1 27.3 %collective-permute-start.14 = (bf16[256,1024]{1,0:T(8,128)(2,1)S(1)}, bf16[256,1024]{1,0:T(8,128)(2,1)S(1)}, u32[]{:S(2)}, u32[]{:S(2)}) collective-permute-start(bf16[256,1024]{1,0:T(8,128)(2,1)S(1)} %get-tuple-element.224.refs_2_), channel_id=1, source_target_pairs={{0,2},{1,3},{2,0},{3,1},{4,6},{5,7},{6,4},{7,5},{8,10},{9,11},{10,... | collective-permute-start | bytes 1572872 | tf_op jit(solution)/shard_map/ppermute | solution.py:70
  176.8 24.9 %collective-permute-start.18 = (bf16[256,1024]{1,0:T(8,128)(2,1)S(1)}, bf16[256,1024]{1,0:T(8,128)(2,1)S(1)}, u32[]{:S(2)}, u32[]{:S(2)}) collective-permute-start(bf16[256,1024]{1,0:T(8,128)(2,1)S(1)} %get-tuple-element.240), channel_id=1, source_target_pairs={{0,2},{1,3},{2,0},{3,1},{4,6},{5,7},{6,4},{7,5},{8,10},{9,11},{10,... | collective-permute-start | bytes 1572872 | tf_op jit(solution)/shard_map/ppermute | solution.py:70
  178.8 23.8 %collective-permute-start.19 = (bf16[256,1024]{1,0:T(8,128)(2,1)S(1)}, bf16[256,1024]{1,0:T(8,128)(2,1)S(1)}, u32[]{:S(2)}, u32[]{:S(2)}) collective-permute-start(bf16[256,1024]{1,0:T(8,128)(2,1)S(1)} %get-tuple-element.242), channel_id=1, source_target_pairs={{0,1},{1,0},{2,3},{3,2},{4,5},{5,4},{6,7},{7,6},{8,9},{9,8},{10,11... | collective-permute-start | bytes 1572872 | tf_op jit(solution)/shard_map/ppermute | solution.py:70
  213.3 325.6 %reduce-scatter.13.cloned.1.call-start = ((), (), s32[]{:S(2)}) async-start(), calls=%async_computation.9 | async-start | bytes 6340608 | tf_op jit(solution)/shard_map/reduce_scatter | solution.py:777
  213.4 22.2 %collective-permute-start.17 = (bf16[256,1024]{1,0:T(8,128)(2,1)S(1)}, bf16[256,1024]{1,0:T(8,128)(2,1)S(1)}, u32[]{:S(2)}, u32[]{:S(2)}) collective-permute-start(bf16[256,1024]{1,0:T(8,128)(2,1)S(1)} %get-tuple-element.238), channel_id=1, source_target_pairs={{0,1},{1,0},{2,3},{3,2},{4,5},{5,4},{6,7},{7,6},{8,9},{9,8},{10,11... | collective-permute-start | bytes 1572872 | tf_op jit(solution)/shard_map/ppermute | solution.py:70
  214.8 20.7 %collective-permute-start.21 = (bf16[256,1024]{1,0:T(8,128)(2,1)S(1)}, bf16[256,1024]{1,0:T(8,128)(2,1)S(1)}, u32[]{:S(2)}, u32[]{:S(2)}) collective-permute-start(bf16[256,1024]{1,0:T(8,128)(2,1)S(1)} %get-tuple-element.246), channel_id=1, source_target_pairs={{0,2},{1,3},{2,0},{3,1},{4,6},{5,7},{6,4},{7,5},{8,10},{9,11},{10,... | collective-permute-start | bytes 1572872 | tf_op jit(solution)/shard_map/ppermute | solution.py:70
  214.9 20.6 %collective-permute-start.20 = (bf16[256,1024]{1,0:T(8,128)(2,1)}, bf16[256,1024]{1,0:T(8,128)(2,1)S(1)}, u32[]{:S(2)}, u32[]{:S(2)}) collective-permute-start(bf16[256,1024]{1,0:T(8,128)(2,1)} %add_convert_fusion.6), channel_id=1, source_target_pairs={{0,2},{1,3},{2,0},{3,1},{4,6},{5,7},{6,4},{7,5},{8,10},{9,11},{10,... | collective-permute-start | bytes 1572872 | tf_op jit(solution)/shard_map/ppermute | solution.py:70
  216.9 18.7 %collective-permute-start.22 = (bf16[256,1024]{1,0:T(8,128)(2,1)S(1)}, bf16[256,1024]{1,0:T(8,128)(2,1)S(1)}, u32[]{:S(2)}, u32[]{:S(2)}) collective-permute-start(bf16[256,1024]{1,0:T(8,128)(2,1)S(1)} %copy-done.75), channel_id=1, source_target_pairs={{0,1},{1,0},{2,3},{3,2},{4,5},{5,4},{6,7},{7,6},{8,9},{9,8},{10,11... | collective-permute-start | bytes 1572872 | tf_op jit(solution)/shard_map/ppermute | solution.py:70
  261.5 277.4 %reduce-scatter.11.cloned.1.call-start = ((), (), s32[]{:S(2)}) async-start(), calls=%async_computation.8 | async-start | bytes 2359296 | tf_op jit(solution)/shard_map/reduce_scatter | solution.py:777
  261.6 13.8 %collective-permute-start.23 = (bf16[256,1024]{1,0:T(8,128)(2,1)}, bf16[256,1024]{1,0:T(8,128)(2,1)}, u32[]{:S(2)}, u32[]{:S(2)}) collective-permute-start(bf16[256,1024]{1,0:T(8,128)(2,1)} %copy-done.44), channel_id=1, source_target_pairs={{0,1},{1,0},{2,3},{3,2},{4,5},{5,4},{6,7},{7,6},{8,9},{9,8},{10,11... | collective-permute-start | bytes 1572872 | tf_op jit(solution)/shard_map/ppermute | solution.py:70
  263.9 20.2 %collective-permute-start.25 = (bf16[256,1024]{1,0:T(8,128)(2,1)}, bf16[256,1024]{1,0:T(8,128)(2,1)}, u32[]{:S(2)}, u32[]{:S(2)}) collective-permute-start(bf16[256,1024]{1,0:T(8,128)(2,1)} %copy-done.48), channel_id=1, source_target_pairs={{0,1},{1,0},{2,3},{3,2},{4,5},{5,4},{6,7},{7,6},{8,9},{9,8},{10,11... | collective-permute-start | bytes 1572872 | tf_op jit(solution)/shard_map/ppermute | solution.py:70
  264.9 21.1 %collective-permute-start.28 = (bf16[256,1024]{1,0:T(8,128)(2,1)}, bf16[256,1024]{1,0:T(8,128)(2,1)}, u32[]{:S(2)}, u32[]{:S(2)}) collective-permute-start(bf16[256,1024]{1,0:T(8,128)(2,1)} %copy-done.50), channel_id=1, source_target_pairs={{0,2},{1,3},{2,0},{3,1},{4,6},{5,7},{6,4},{7,5},{8,10},{9,11},{10,... | collective-permute-start | bytes 1572872 | tf_op jit(solution)/shard_map/ppermute | solution.py:70
  286.0 12.9 %collective-permute-start.29 = (bf16[256,1024]{1,0:T(8,128)(2,1)}, bf16[256,1024]{1,0:T(8,128)(2,1)S(1)}, u32[]{:S(2)}, u32[]{:S(2)}) collective-permute-start(bf16[256,1024]{1,0:T(8,128)(2,1)} %copy-done.71), channel_id=1, source_target_pairs={{0,2},{1,3},{2,0},{3,1},{4,6},{5,7},{6,4},{7,5},{8,10},{9,11},{10,... | collective-permute-start | bytes 1572872 | tf_op jit(solution)/shard_map/ppermute | solution.py:70
  323.2 34.7 %collective-permute-start.33 = (bf16[256,1024]{1,0:T(8,128)(2,1)}, bf16[256,1024]{1,0:T(8,128)(2,1)}, u32[]{:S(2)}, u32[]{:S(2)}) collective-permute-start(bf16[256,1024]{1,0:T(8,128)(2,1)} %copy-done.69), channel_id=1, source_target_pairs={{0,1},{1,0},{2,3},{3,2},{4,5},{5,4},{6,7},{7,6},{8,9},{9,8},{10,11... | collective-permute-start | bytes 1572872 | tf_op jit(solution)/shard_map/ppermute | solution.py:70
  324.3 33.6 %collective-permute-start.35 = (bf16[256,1024]{1,0:T(8,128)(2,1)}, bf16[256,1024]{1,0:T(8,128)(2,1)}, u32[]{:S(2)}, u32[]{:S(2)}) collective-permute-start(bf16[256,1024]{1,0:T(8,128)(2,1)} %copy-done.68), channel_id=1, source_target_pairs={{0,2},{1,3},{2,0},{3,1},{4,6},{5,7},{6,4},{7,5},{8,10},{9,11},{10,... | collective-permute-start | bytes 1572872 | tf_op jit(solution)/shard_map/ppermute | solution.py:70
  331.4 211.5 %reduce-scatter.9.cloned.1.call-start = ((), (), s32[]{:S(2)}) async-start(), calls=%async_computation.7 | async-start | bytes 6340608 | tf_op jit(solution)/shard_map/reduce_scatter | solution.py:777
  331.5 26.4 %collective-permute-start.34 = (bf16[256,1024]{1,0:T(8,128)(2,1)}, bf16[256,1024]{1,0:T(8,128)(2,1)S(1)}, u32[]{:S(2)}, u32[]{:S(2)}) collective-permute-start(bf16[256,1024]{1,0:T(8,128)(2,1)} %add_convert_fusion.4), channel_id=1, source_target_pairs={{0,2},{1,3},{2,0},{3,1},{4,6},{5,7},{6,4},{7,5},{8,10},{9,11},{10,... | collective-permute-start | bytes 1572872 | tf_op jit(solution)/shard_map/ppermute | solution.py:70
  332.8 25.1 %collective-permute-start.36 = (bf16[256,1024]{1,0:T(8,128)(2,1)}, bf16[256,1024]{1,0:T(8,128)(2,1)S(1)}, u32[]{:S(2)}, u32[]{:S(2)}) collective-permute-start(bf16[256,1024]{1,0:T(8,128)(2,1)} %add_convert_fusion.5), channel_id=1, source_target_pairs={{0,1},{1,0},{2,3},{3,2},{4,5},{5,4},{6,7},{7,6},{8,9},{9,8},{10,11... | collective-permute-start | bytes 1572872 | tf_op jit(solution)/shard_map/ppermute | solution.py:70
  335.3 39.5 %collective-permute-start.32 = (bf16[2,1024,256]{2,1,0:T(8,128)(2,1)S(1)}, bf16[2,1024,256]{2,1,0:T(8,128)(2,1)S(1)}, u32[]{:S(2)}, u32[]{:S(2)}) collective-permute-start(bf16[2,1024,256]{2,1,0:T(8,128)(2,1)S(1)} %add_convert_fusion.1), channel_id=1, source_target_pairs={{8,0},{12,4},{16,8},{20,12},{24,16},{28,20},{9,1},{13,5},{17,9},{2... | collective-permute-start | bytes 3145736 | tf_op jit(solution)/shard_map/ppermute | solution.py:880
  377.5 14.8 %collective-permute-start.38 = (bf16[256,1024]{1,0:T(8,128)(2,1)S(1)}, bf16[256,1024]{1,0:T(8,128)(2,1)S(1)}, u32[]{:S(2)}, u32[]{:S(2)}) collective-permute-start(bf16[256,1024]{1,0:T(8,128)(2,1)S(1)} %get-tuple-element.303.refs_1_), channel_id=1, source_target_pairs={{0,2},{1,3},{2,0},{3,1},{4,6},{5,7},{6,4},{7,5},{8,10},{9,11},{10,... | collective-permute-start | bytes 1572872 | tf_op jit(solution)/shard_map/ppermute | solution.py:70
  378.3 14.9 %collective-permute-start.40 = (bf16[256,1024]{1,0:T(8,128)(2,1)S(1)}, bf16[256,1024]{1,0:T(8,128)(2,1)S(1)}, u32[]{:S(2)}, u32[]{:S(2)}) collective-permute-start(bf16[256,1024]{1,0:T(8,128)(2,1)S(1)} %get-tuple-element.304.refs_5_), channel_id=1, source_target_pairs={{0,1},{1,0},{2,3},{3,2},{4,5},{5,4},{6,7},{7,6},{8,9},{9,8},{10,11... | collective-permute-start | bytes 1572872 | tf_op jit(solution)/shard_map/ppermute | solution.py:70
  379.7 38.2 %collective-permute-start.44 = (bf16[2,1024,256]{2,1,0:T(8,128)(2,1)S(1)}, bf16[2,1024,256]{2,1,0:T(8,128)(2,1)S(1)}, u32[]{:S(2)}, u32[]{:S(2)}) collective-permute-start(bf16[2,1024,256]{2,1,0:T(8,128)(2,1)S(1)} %add_convert_fusion), channel_id=1, source_target_pairs={{8,0},{12,4},{16,8},{20,12},{24,16},{28,20},{9,1},{13,5},{17,9},{2... | collective-permute-start | bytes 3145736 | tf_op jit(solution)/shard_map/ppermute | solution.py:887
  381.0 23.3 %collective-permute-start.37 = (bf16[256,1024]{1,0:T(8,128)(2,1)S(1)}, bf16[256,1024]{1,0:T(8,128)(2,1)S(1)}, u32[]{:S(2)}, u32[]{:S(2)}) collective-permute-start(bf16[256,1024]{1,0:T(8,128)(2,1)S(1)} %get-tuple-element.303.refs_1_), channel_id=1, source_target_pairs={{0,1},{1,0},{2,3},{3,2},{4,5},{5,4},{6,7},{7,6},{8,9},{9,8},{10,11... | collective-permute-start | bytes 1572872 | tf_op jit(solution)/shard_map/ppermute | solution.py:70
  382.0 22.3 %collective-permute-start.41 = (bf16[256,1024]{1,0:T(8,128)(2,1)S(1)}, bf16[256,1024]{1,0:T(8,128)(2,1)S(1)}, u32[]{:S(2)}, u32[]{:S(2)}) collective-permute-start(bf16[256,1024]{1,0:T(8,128)(2,1)S(1)} %get-tuple-element.304.refs_5_), channel_id=1, source_target_pairs={{0,2},{1,3},{2,0},{3,1},{4,6},{5,7},{6,4},{7,5},{8,10},{9,11},{10,... | collective-permute-start | bytes 1572872 | tf_op jit(solution)/shard_map/ppermute | solution.py:70
  392.3 22.6 %collective-permute-start.39 = (bf16[256,1024]{1,0:T(8,128)(2,1)S(1)}, bf16[256,1024]{1,0:T(8,128)(2,1)S(1)}, u32[]{:S(2)}, u32[]{:S(2)}) collective-permute-start(bf16[256,1024]{1,0:T(8,128)(2,1)S(1)} %collective-permute-done.38.refs_3_), channel_id=1, source_target_pairs={{0,1},{1,0},{2,3},{3,2},{4,5},{5,4},{6,7},{7,6},{8,9},{9,8},{10,11... | collective-permute-start | bytes 1572872 | tf_op jit(solution)/shard_map/ppermute | solution.py:70
  393.2 21.6 %collective-permute-start.42 = (bf16[256,1024]{1,0:T(8,128)(2,1)S(1)}, bf16[256,1024]{1,0:T(8,128)(2,1)S(1)}, u32[]{:S(2)}, u32[]{:S(2)}) collective-permute-start(bf16[256,1024]{1,0:T(8,128)(2,1)S(1)} %collective-permute-done.40.refs_6_), channel_id=1, source_target_pairs={{0,2},{1,3},{2,0},{3,1},{4,6},{5,7},{6,4},{7,5},{8,10},{9,11},{10,... | collective-permute-start | bytes 1572872 | tf_op jit(solution)/shard_map/ppermute | solution.py:70
  418.9 124.1 %reduce-scatter.7.cloned.1.call-start = ((), (), s32[]{:S(2)}) async-start(), calls=%async_computation.6 | async-start | bytes 3538944 | tf_op jit(solution)/shard_map/reduce_scatter | solution.py:777
  435.7 19.9 %collective-permute-start.46 = (bf16[256,1024]{1,0:T(8,128)(2,1)}, bf16[256,1024]{1,0:T(8,128)(2,1)}, u32[]{:S(2)}, u32[]{:S(2)}) collective-permute-start(bf16[256,1024]{1,0:T(8,128)(2,1)} %get-tuple-element.339.refs_9_), channel_id=1, source_target_pairs={{0,2},{1,3},{2,0},{3,1},{4,6},{5,7},{6,4},{7,5},{8,10},{9,11},{10,... | collective-permute-start | bytes 1572872 | tf_op jit(solution)/shard_map/ppermute | solution.py:70
  437.0 21.1 %collective-permute-start.47 = (bf16[256,1024]{1,0:T(8,128)(2,1)}, bf16[256,1024]{1,0:T(8,128)(2,1)}, u32[]{:S(2)}, u32[]{:S(2)}) collective-permute-start(bf16[256,1024]{1,0:T(8,128)(2,1)} %get-tuple-element.338.refs_8_), channel_id=1, source_target_pairs={{0,1},{1,0},{2,3},{3,2},{4,5},{5,4},{6,7},{7,6},{8,9},{9,8},{10,11... | collective-permute-start | bytes 1572872 | tf_op jit(solution)/shard_map/ppermute | solution.py:70
  460.2 105.3 %reduce-scatter.17.cloned.1.call-start = ((), (), s32[]{:S(2)}) async-start(), calls=%async_computation.11 | async-start | bytes 3538944 | tf_op jit(solution)/shard_map/reduce_scatter | solution.py:777
  461.3 14.9 %collective-permute-start.45 = (bf16[256,1024]{1,0:T(8,128)(2,1)S(1)}, bf16[256,1024]{1,0:T(8,128)(2,1)S(1)}, u32[]{:S(2)}, u32[]{:S(2)}) collective-permute-start(bf16[256,1024]{1,0:T(8,128)(2,1)S(1)} %copy-done.55), channel_id=1, source_target_pairs={{0,1},{1,0},{2,3},{3,2},{4,5},{5,4},{6,7},{7,6},{8,9},{9,8},{10,11... | collective-permute-start | bytes 1572872 | tf_op jit(solution)/shard_map/ppermute | solution.py:70
  462.4 14.9 %collective-permute-start.49 = (bf16[256,1024]{1,0:T(8,128)(2,1)S(1)}, bf16[256,1024]{1,0:T(8,128)(2,1)S(1)}, u32[]{:S(2)}, u32[]{:S(2)}) collective-permute-start(bf16[256,1024]{1,0:T(8,128)(2,1)S(1)} %copy-done.53), channel_id=1, source_target_pairs={{0,2},{1,3},{2,0},{3,1},{4,6},{5,7},{6,4},{7,5},{8,10},{9,11},{10,... | collective-permute-start | bytes 1572872 | tf_op jit(solution)/shard_map/ppermute | solution.py:70
  463.1 22.9 %collective-permute-start.48 = (bf16[256,1024]{1,0:T(8,128)(2,1)}, bf16[256,1024]{1,0:T(8,128)(2,1)S(1)}, u32[]{:S(2)}, u32[]{:S(2)}) collective-permute-start(bf16[256,1024]{1,0:T(8,128)(2,1)} %add_convert_fusion.2), channel_id=1, source_target_pairs={{0,2},{1,3},{2,0},{3,1},{4,6},{5,7},{6,4},{7,5},{8,10},{9,11},{10,... | collective-permute-start | bytes 1572872 | tf_op jit(solution)/shard_map/ppermute | solution.py:70
  464.4 21.5 %collective-permute-start.50 = (bf16[256,1024]{1,0:T(8,128)(2,1)}, bf16[256,1024]{1,0:T(8,128)(2,1)S(1)}, u32[]{:S(2)}, u32[]{:S(2)}) collective-permute-start(bf16[256,1024]{1,0:T(8,128)(2,1)} %add_convert_fusion.3), channel_id=1, source_target_pairs={{0,1},{1,0},{2,3},{3,2},{4,5},{5,4},{6,7},{7,6},{8,9},{9,8},{10,11... | collective-permute-start | bytes 1572872 | tf_op jit(solution)/shard_map/ppermute | solution.py:70
  (97 other events, 870.5 us)
Sparse Core Ops, SparseCore 0:
  213.4 64.7 reduce-scatter.14
  280.6 62.0 reduce-scatter.12
  345.1 42.0 reduce-scatter.10
  419.0 63.5 reduce-scatter.8
  484.9 38.9 reduce-scatter.6
  526.1 39.3 reduce-scatter.16
